TPU v7x, 512 devices: a whole 4x4x16 slice. The times are simulated.
512 devices in a mesh: seq: 32 (over y, x, core), head: 16 (over z).
Axes of the slice: x: 4, y: 4, z: 16, core: 2. Of those that a mesh axis runs over, the one named last changes fastest.
Arguments:
- queries: bfloat16 [2, 32, 8, 32, 128], P(None, 'head'), may hold values from -128 to 128
- tree_keys: bfloat16 [2, 32, 32, 128], P(None, 'head'), may hold values from -8 to 8
- tree_values: bfloat16 [2, 32, 32, 128], P(None, 'head'), may hold values from -6 to 6
- cache_keys: bfloat16 [32, 32768, 128], P('head', 'seq'), may hold values from -6 to 6
- cache_values: bfloat16 [32, 32768, 128], P('head', 'seq'), may hold values from -6 to 6
- block_ids: int32 [32, 32], P('head'), may hold values from 0 to 255, as said below
- ancestors: int32 [4, 32, 32], replicated, may hold values from 0 to 1, as said below
- out_weight: bfloat16 [8192, 8192], P('seq', 'head'), may hold values from -0.0625 to 0.0625
Outputs:
- draft_mixed: bfloat16 [32, 4, 8192], P('seq', None, 'head')
- verify_mixed: bfloat16 [32, 4, 8192], P('seq', None, 'head')
Inputs may be any that keep to these rules, and one draw needn't show every extreme that they name: `block_ids`: the 32 block numbers of one pair are distinct, and for every pair one run of 1024 positions (positions s * 1024 to (s + 1) * 1024 - 1 for some s) holds at least half of its 32 blocks, or all 8 blocks of the run where the run has fewer. ancestors[r, n, k] is 1 exactly when k is n or an ancestor of n in request r's tree; node 0 is the root and every other node's parent has a smaller number.
All inputs are finite; a program needn't handle non-finite values.
Results may differ from a plain program's by a relative error of at most 0.009.
Values may be sent and summed in bfloat16 or wider, within the bound.
No kernel may reach another device: no remote copies, remote signals or barrier semaphores. Data moves between devices by JAX's collectives and lax.ppermute only.
A program may use at most 64 MiB of HBM per device.

v0:
```python
import math

import jax
import jax.numpy as jnp
from jax import lax
from jax.sharding import PartitionSpec as P

KVH = 8
BLOCK = 128


def in_one_piece(arrays, axis, split_dim, concat_dim, along):
    widths = [math.prod(a.shape[along:]) for a in arrays]
    both = jnp.concatenate(
        [a.reshape(*a.shape[:along], w) for a, w in zip(arrays, widths)], axis=along
    )
    whole = lax.all_to_all(both, axis, split_axis=split_dim, concat_axis=concat_dim, tiled=True)
    pieces = jnp.split(whole, [sum(widths[:k]) for k in range(1, len(widths))], axis=along)
    return tuple(
        (b.reshape(*whole.shape[:along], *a.shape[along:]) for a, b in zip(arrays, pieces))
    )


def sent_together(arrays, axis, dim, along):
    both = jnp.concatenate(arrays, axis=along)
    whole, at, finished = (lax.all_gather(both, axis, axis=dim, tiled=True), 0, [])
    for a in arrays:
        finished.append(lax.slice_in_dim(whole, at, at + a.shape[along], axis=along))
        at += a.shape[along]
    return tuple(finished)


def cut_along(shard, dim, devices):
    dims = shard.shape
    pieces = shard.reshape(*dims[:dim], devices, dims[dim] // devices, *dims[dim + 1 :])
    return jnp.moveaxis(pieces, dim, 0)


def summed_on_arrival(shard, axis, dim):
    devices = lax.axis_size(axis)
    pieces = lax.all_to_all(cut_along(shard, dim, devices), axis, 0, 0, tiled=True)
    return jnp.sum(pieces, axis=0)


def cache_partial(query_rows, key_rows, value_rows, chosen_mask, score_scale):
    scores = (
        jnp.einsum("pgnh,plh->pgnl", query_rows, key_rows, preferred_element_type=jnp.float32)
        * score_scale
    )
    if chosen_mask is not None:
        scores = jnp.where(chosen_mask[:, None, None, :], scores, -1e30)
    peaks = jnp.max(scores, axis=-1)
    weights = jnp.exp(scores - peaks[..., None])
    if chosen_mask is not None:
        weights = jnp.where(chosen_mask[:, None, None, :], weights, 0.0)
    totals = jnp.sum(weights, axis=-1)
    summed = jnp.einsum(
        "pgnl,plh->pgnh",
        weights.astype(jnp.bfloat16),
        value_rows,
        preferred_element_type=jnp.float32,
    )
    return (peaks, totals, summed)


def tree_partial(query_rows, tree_key_rows, tree_value_rows, tree_mask, score_scale):
    scores = (
        jnp.einsum("pgnh,pkh->pgnk", query_rows, tree_key_rows, preferred_element_type=jnp.float32)
        * score_scale
    )
    allowed = tree_mask[:, None] > 0
    scores = jnp.where(allowed, scores, -1e30)
    peaks = jnp.max(scores, axis=-1)
    weights = jnp.where(allowed, jnp.exp(scores - peaks[..., None]), 0.0)
    totals = jnp.sum(weights, axis=-1)
    summed = jnp.einsum(
        "pgnk,pkh->pgnh",
        weights.astype(jnp.bfloat16),
        tree_value_rows,
        preferred_element_type=jnp.float32,
    )
    return (peaks, totals, summed)


def combine_two(first_part, second_part):
    peaks = jnp.maximum(first_part[0], second_part[0])
    first_factor = jnp.exp(first_part[0] - peaks)
    second_factor = jnp.exp(second_part[0] - peaks)
    totals = first_part[1] * first_factor + second_part[1] * second_factor
    summed = first_part[2] * first_factor[..., None] + second_part[2] * second_factor[..., None]
    return (peaks, totals, summed)


def combine_over(peaks, totals, summed):
    highest = jnp.max(peaks, axis=0)
    factor = jnp.exp(peaks - highest[None])
    return (highest, jnp.sum(totals * factor, axis=0), jnp.sum(summed * factor[..., None], axis=0))


def finish(cache_part, tree_part):
    peaks, totals, summed = combine_two(cache_part, tree_part)
    result = summed / totals[..., None]
    pair_count, groups, node_count, head_dim = result.shape
    return (
        jnp.transpose(result, (0, 2, 1, 3))
        .reshape(pair_count, node_count, groups * head_dim)
        .astype(jnp.bfloat16)
    )


def local(
    queries, tree_keys, tree_values, cache_keys, cache_values, block_ids, ancestors, out_weight
):
    pair_dev, ctx_dev, head_dim = cache_keys.shape
    groups = queries.shape[2]
    node_count = queries.shape[3]
    requests = ancestors.shape[0]
    score_scale = head_dim ** (-0.5)
    seq_count = lax.axis_size("seq")
    seq_index = lax.axis_index("seq")
    head_index = lax.axis_index("head")
    blocks_dev = ctx_dev // BLOCK
    node_dev = node_count // seq_count
    pair_ids = head_index * pair_dev + jnp.arange(pair_dev, dtype=jnp.int32)
    picker = (pair_ids[:, None] // KVH == jnp.arange(requests, dtype=jnp.int32)[None, :]).astype(
        jnp.int32
    )
    tree_masks = jnp.sum(picker[:, :, None, None] * ancestors[None], axis=1)
    verify_part = cache_partial(queries[1], cache_keys, cache_values, None, score_scale)
    owned_ids = seq_index * blocks_dev + jnp.arange(blocks_dev, dtype=jnp.int32)
    chosen = jnp.any(block_ids[:, :, None] == owned_ids[None, None, :], axis=1)
    chosen_mask = jnp.broadcast_to(chosen[:, :, None], (pair_dev, blocks_dev, BLOCK)).reshape(
        pair_dev, ctx_dev
    )
    draft_part = cache_partial(queries[0], cache_keys, cache_values, chosen_mask, score_scale)
    arrived = in_one_piece(
        (
            draft_part[0][None],
            draft_part[1][None],
            draft_part[2][None],
            verify_part[0][None],
            verify_part[1][None],
            verify_part[2][None],
        ),
        "seq",
        3,
        0,
        4,
    )
    draft_cache = combine_over(arrived[0], arrived[1], arrived[2])
    verify_cache = combine_over(arrived[3], arrived[4], arrived[5])
    row_start = seq_index * node_dev
    mask_rows = lax.dynamic_slice_in_dim(tree_masks, row_start, node_dev, 1)
    draft_tree = tree_partial(
        lax.dynamic_slice_in_dim(queries[0], row_start, node_dev, 2),
        tree_keys[0],
        tree_values[0],
        mask_rows,
        score_scale,
    )
    verify_tree = tree_partial(
        lax.dynamic_slice_in_dim(queries[1], row_start, node_dev, 2),
        tree_keys[1],
        tree_values[1],
        mask_rows,
        score_scale,
    )
    draft_all, verify_all = sent_together(
        (finish(draft_cache, draft_tree), finish(verify_cache, verify_tree)), "seq", 1, 0
    )
    gathered = sent_together((draft_all, verify_all), "head", 0, 1)
    stacked = jnp.stack(gathered)
    stacked = stacked.reshape(2, requests, KVH, node_count, groups * head_dim)
    stacked = jnp.transpose(stacked, (3, 0, 1, 2, 4)).reshape(
        node_count, 2 * requests, KVH * groups * head_dim
    )
    rows_dev = out_weight.shape[0]
    columns = lax.dynamic_slice_in_dim(stacked, seq_index * rows_dev, rows_dev, 2)
    own_rows = summed_on_arrival(
        jnp.einsum("nrk,kd->nrd", columns, out_weight, preferred_element_type=jnp.float32), "seq", 0
    )
    own_rows = own_rows.reshape(node_dev, 2, requests, own_rows.shape[-1]).astype(jnp.bfloat16)
    return (own_rows[:, 0], own_rows[:, 1])


def solution(mesh):
    in_specs = (
        P(None, "head", None, None, None),
        P(None, "head", None, None),
        P(None, "head", None, None),
        P("head", "seq", None),
        P("head", "seq", None),
        P("head", None),
        P(),
        P("seq", "head"),
    )
    out_specs = (P("seq", None, "head"), P("seq", None, "head"))
    return jax.shard_map(local, mesh=mesh, in_specs=in_specs, out_specs=out_specs, check_vma=False)
```

profile of v0, /device:TPU:1, one launch (start us, length us, event | category | flops | bytes accessed | tf_op | source)
XLA Modules:
  0.0 188.2 jit_solution(727317911325273039)
XLA Ops:
  7.2 0.9 compare_reduce_fusion
  8.2 1.4 multiply_reduce_fusion
  9.7 0.5 fusion
  10.2 0.6 fusion.4
  10.9 0.7 convolution_bitcast_fusion.2
  11.5 0.5 fusion.2
  12.0 0.6 convolution_bitcast_fusion.1
  13.3 0.7 concatenate.10
  14.1 1.3 copy.66
  15.4 10.4 %all-to-all-start = ((f32[1,2,8,32,260]{4,2,1,0,3:T(8,128)}), f32[1,2,8,32,260]{4,2,1,0,3:T(8,128)S(1)}, u32[]{:S(2)}, u32[]{:S(2)}) async-start(f32[1,2,8,32,260]{4,2,1,0,3:T(8,128)} %copy.66), calls=%async_computation | async-start | bytes 1572864 | tf_op jit(solution)/shard_map/all_to_all | solution.py:17
  26.8 13.4 %all-to-all-done = f32[1,2,8,32,260]{4,2,1,0,3:T(8,128)S(1)} async-done(((f32[1,2,8,32,260]{4,2,1,0,3:T(8,128)}), f32[1,2,8,32,260]{4,2,1,0,3:T(8,128)S(1)}, u32[]{:S(2)}, u32[]{:S(2)}) %all-to-all-start) | async-done | bytes 532512 | tf_op jit(solution)/shard_map/all_to_all | solution.py:17
  40.2 1.1 copy.67
  41.6 0.6 fusion.15
  42.9 23.1 %all_gather.6 = bf16[4,32,1024]{2,0,1:T(4,128)(2,1)S(1)} all-gather(bf16[4,1,1024]{2,0,1:T(4,128)(2,1)S(1)} %pad_maximum_fusion.1), channel_id=1, replica_groups=mesh['seq'=32,'head'=16] {'seq'}, dimensions={1}, use_global_device_ids=true | all-gather | bytes 270336 | tf_op jit(solution)/shard_map/all_gather | solution.py:26
  66.5 0.7 copy.70
  67.2 69.8 %all-gather.2.cloned.1.call-done = bf16[32,64,1024]{2,1,0:T(8,128)(2,1)} async-done(((bf16[2,64,1024]{2,1,0:T(8,128)(2,1)}), bf16[32,64,1024]{2,1,0:T(8,128)(2,1)}) %all-gather.2.cloned.1.call-update) | async-done | bytes 4194320 | tf_op jit(solution)/shard_map/all_gather | solution.py:26
  137.1 2.7 %fusion.80 = (bf16[32,32,1024]{2,1,0:T(8,128)(2,1)S(1)}, bf16[32,32,1024]{2,1,0:T(8,128)(2,1)S(1)}) fusion(bf16[32,64,1024]{2,1,0:T(8,128)(2,1)} %all-gather.2.cloned.1.call-done), kind=kLoop, calls=%fused_computation.120 | loop fusion | bytes 8388608 | tf_op jit(solution)/shard_map/slice | solution.py:28
  139.7 1.2 copy.71
  140.9 1.2 copy.72
  142.1 2.3 %maximum_bitcast_fusion = bf16[32,2,4,8,1024]{4,3,2,1,0:T(8,128)(2,1)} fusion(bf16[1,4,8,32,1024]{4,2,1,0,3:T(8,128)(2,1)S(1)} %copy.72, bf16[1,4,8,32,1024]{4,2,1,0,3:T(8,128)(2,1)S(1)} %copy.71), kind=kLoop, calls=%fused_computation | loop fusion | flops 2097152 | bytes 8388608 | tf_op jit(solution)/shard_map/transpose | solution.py:174
  144.3 7.4 %reshape.390 = bf16[32,8,8192]{2,1,0:T(8,128)(2,1)} reshape(bf16[32,2,4,8,1024]{4,3,2,1,0:T(8,128)(2,1)} %maximum_bitcast_fusion) | data formatting | bytes 8388608 | tf_op jit(solution)/shard_map/reshape | solution.py:174
  151.8 1.1 convolution_bitcast_fusion
  152.9 27.8 %all_to_all.23 = f32[32,1,8,512]{3,2,1,0:T(8,128)S(1)} all-to-all(f32[32,1,8,512]{3,2,1,0:T(8,128)S(1)} %convolution_bitcast_fusion), channel_id=1, replica_groups=mesh['seq'=32,'head'=16] {'seq'}, dimensions={0} | all-to-all | bytes 1048576 | tf_op jit(solution)/shard_map/all_to_all | solution.py:41
  180.7 0.6 slice_bitcast_fusion.2
  (51 shorter events, 3.2 us)
Async XLA Ops:
  7.2 1.1 copy-start
  7.2 2.5 %copy-start.1 = (bf16[2,2,8,32,128]{4,3,2,1,0:T(8,128)(2,1)S(1)}, bf16[2,2,8,32,128]{4,3,2,1,0:T(8,128)(2,1)}, u32[]{:S(2)}) copy-start(bf16[2,2,8,32,128]{4,3,2,1,0:T(8,128)(2,1)} %param.8) | copy-start | bytes 786436
  9.7 1.2 copy-start.3
  14.1 11.9 %copy-start.2 = (bf16[2,2,8,32,128]{4,3,2,1,0:T(8,128)(2,1)S(1)}, bf16[2,2,8,32,128]{4,3,2,1,0:T(8,128)(2,1)}, u32[]{:S(2)}) copy-start(bf16[2,2,8,32,128]{4,3,2,1,0:T(8,128)(2,1)} %param.8) | copy-start | bytes 786436
  14.1 12.0 %copy-start.5 = (s32[4,32,32]{2,1,0:T(8,128)S(1)}, s32[4,32,32]{2,1,0:T(8,128)}, u32[]{:S(2)}) copy-start(s32[4,32,32]{2,1,0:T(8,128)} %param.14) | copy-start | bytes 49156
  14.1 12.2 %copy-start.6 = (bf16[2,2,32,128]{3,2,1,0:T(8,128)(2,1)S(1)}, bf16[2,2,32,128]{3,2,1,0:T(8,128)(2,1)}, u32[]{:S(2)}) copy-start(bf16[2,2,32,128]{3,2,1,0:T(8,128)(2,1)} %param.9) | copy-start | bytes 98308
  15.4 24.8 %all-to-all-start = ((f32[1,2,8,32,260]{4,2,1,0,3:T(8,128)}), f32[1,2,8,32,260]{4,2,1,0,3:T(8,128)S(1)}, u32[]{:S(2)}, u32[]{:S(2)}) async-start(f32[1,2,8,32,260]{4,2,1,0,3:T(8,128)} %copy.66), calls=%async_computation | async-start | bytes 1572864 | tf_op jit(solution)/shard_map/all_to_all | solution.py:17
  25.9 111.2 %all-gather.2.cloned.1.call-start = ((), (), s32[]{:S(2)}) async-start(), calls=%async_computation.2 | async-start | bytes 4456448 | tf_op jit(solution)/shard_map/all_gather | solution.py:26
  26.8 15.5 %copy-start.7 = (bf16[2,2,32,128]{3,2,1,0:T(8,128)(2,1)S(1)}, bf16[2,2,32,128]{3,2,1,0:T(8,128)(2,1)}, u32[]{:S(2)}) copy-start(bf16[2,2,32,128]{3,2,1,0:T(8,128)(2,1)} %param.10) | copy-start | bytes 98308
  144.3 7.4 %copy-start.4 = (bf16[256,512]{1,0:T(8,128)(2,1)S(1)}, bf16[256,512]{1,0:T(8,128)(2,1)}, u32[]{:S(2)}) copy-start(bf16[256,512]{1,0:T(8,128)(2,1)} %param.15) | copy-start | bytes 786436
Sparse Core Ops, SparseCore 0:
  67.4 69.6 all-gather.1
where the time goes:
time: 189 us; the launch traced here: 188 us
  waiting for transfers between devices  83.2 us (44%)
  blocking collectives  50.8 us (27%)
  local copies, waits for them, and re-layouts  18.1 us (10%)
  between operations  14.3 us (8%)
  starting transfers between devices  10.5 us (6%)
  other arithmetic  6.12 us (3%)
  matrix products  5.11 us (3%)
    all_gather x1, waiting for transfers between devices, sent_together(): lax.all_gather(both, axis, axis=dim, tiled=True)  69.8 us
    all_to_all x1, blocking collectives, summed_on_arrival(): lax.all_to_all(cut_along(shard, dim, devices), axis, 0, 0, tiled=True)  27.8 us
    all_gather x1, blocking collectives, sent_together(): lax.all_gather(both, axis, axis=dim, tiled=True)  23.1 us
    all_to_all x1, waiting for transfers between devices, in_one_piece(): lax.all_to_all(both, axis, split_axis=split_dim, concat_axis=concat_dim,...  13.4 us
    all_to_all x1, starting transfers between devices, in_one_piece(): lax.all_to_all(both, axis, split_axis=split_dim, concat_axis=concat_dim,...  10.4 us
    reshape x1, local copies, waits for them, and re-layouts, local(): jnp.transpose(stacked, (3, 0, 1, 2, 4))  7.44 us
  transfers between devices with their start and end apart: 2, of which 2 were waited for; matrix products, arithmetic and copies ran while one was open for 0% of the time, Pallas kernels for 0%

commit v1 on v0

v1 whole, which is shorter than its diff:
```python
import jax
import jax.numpy as jnp
from jax import lax
from jax.experimental import pallas as pl
from jax.experimental.pallas import tpu as pltpu
from jax.sharding import PartitionSpec as P

KVH = 8
BLOCK = 128
SCALE = 128 ** (-0.5) * 1.4426950408889634
NEG = -(2.0**100)
F32 = jnp.float32
BF16 = jnp.bfloat16
Y_GROUPS = [[y * 8 + k for y in range(4)] for k in range(8)]
XC_GROUPS = [[y * 8 + k for k in range(8)] for y in range(4)]
NT = (((1,), (1,)), ((), ()))
VMEM = pl.BlockSpec(memory_space=pltpu.VMEM)
PARAMS = pltpu.CompilerParams(vmem_limit_bytes=32 * 1024 * 1024)


def four_lanes(lane, tiles):
    low = jnp.where(lane < 32, tiles[0], tiles[1])
    high = jnp.where(lane < 96, tiles[2], tiles[3])
    return jnp.where(lane < 64, low, high)


def attend_kernel(
    q_ref, k_ref, v_ref, ids_ref, tk_ref, tv_ref, anc_ref, send_ref, tree_ref, acc_ref, stat_ref
):
    seq = lax.axis_index("seq")
    head = lax.axis_index("head")
    lane = lax.broadcasted_iota(jnp.int32, (8, 128), 1)
    first_half = (lane % 32) < 16
    for p in range(2):
        keys = k_ref[p]
        values = jnp.concatenate([v_ref[p], jnp.ones((1024, 128), BF16)], axis=1)
        ids = ids_ref[p : p + 1, :]
        bias = []
        for b in range(8):
            hit = jnp.max(jnp.where(ids == seq * 8 + b, 1.0, 0.0), axis=1, keepdims=True)
            bias.append(jnp.broadcast_to(jnp.where(hit > 0.5, 0.0, NEG), (1, BLOCK)))
        bias = jnp.concatenate(bias, axis=1)
        peaks, sums = [], []
        for a in range(2):
            q = q_ref[a, p].reshape(256, 128)
            t = lax.dot_general(q, keys, NT, preferred_element_type=F32) * SCALE
            if a == 0:
                t = t + bias
            peak = jnp.max(t, axis=1, keepdims=True).astype(BF16).astype(F32)
            w = jnp.exp2(t - peak).astype(BF16)
            peaks.append(peak)
            sums.append(jnp.dot(w, values, preferred_element_type=F32))
        for y in range(4):
            for gp in range(4):
                dest = y * 8 + p * 4 + gp
                rows = [(gp * 2 + g2) * 32 + y * 8 for g2 in range(2)]
                for a in range(2):
                    both = jnp.concatenate([sums[a][r : r + 8, :128] for r in rows], axis=0)
                    send_ref[dest, a * 16 : (a + 1) * 16, :] = both.astype(BF16)
                m = four_lanes(lane, [peaks[a][r : r + 8] for a in range(2) for r in rows])
                tot = four_lanes(lane, [sums[a][r : r + 8, 128:] for a in range(2) for r in rows])
                high = tot.astype(BF16).astype(F32)
                tot = jnp.where(first_half, high, tot - high)
                send_ref[dest, 32:48, :] = jnp.concatenate([m, tot], axis=0).astype(BF16)
    y, x, core = seq // 8, (seq % 8) // 2, seq % 2
    own, gp = x // 2, (x % 2) * 2 + core
    allowed = anc_ref[head // 4] > 0
    allowed = jnp.concatenate([allowed, allowed], axis=0)
    for a in range(2):
        q = q_ref[a, own, pl.ds(gp * 2, 2)].reshape(64, 128)
        t = lax.dot_general(q, tk_ref[a, own], NT, preferred_element_type=F32) * SCALE
        t = jnp.where(allowed, t, NEG)
        peak = jnp.max(t, axis=1, keepdims=True)
        w = jnp.where(allowed, jnp.exp2(t - peak), 0.0)
        total = jnp.sum(w, axis=1, keepdims=True)
        summed = jnp.dot(w.astype(BF16), tv_ref[a, own], preferred_element_type=F32)
        acc_ref[a] = summed.reshape(2, 32, 128)
        stat_ref[0, a] = jnp.broadcast_to(peak, (64, 128)).reshape(2, 32, 128)
        stat_ref[1, a] = jnp.broadcast_to(total, (64, 128)).reshape(2, 32, 128)
    start = pl.multiple_of(y * 8, 8)
    for a in range(2):
        for g2 in range(2):
            tree_ref[a * 2 + g2] = acc_ref[a, g2, pl.ds(start, 8), :]
    for k in range(2):
        tile = four_lanes(
            lane, [stat_ref[k, a, g2, pl.ds(start, 8), :] for a in range(2) for g2 in range(2)]
        )
        tree_ref[4 + k] = tile if k == 0 else jnp.where(first_half, tile, 0.0)


def combine_kernel(got_ref, tree_ref, out_ref):
    def spread(tile, at):
        return jnp.broadcast_to(tile[:, at : at + 1], (8, 128))

    peak = tree_ref[4]
    for s in range(32):
        peak = jnp.maximum(peak, got_ref[s, 32:48, :].astype(F32)[:8])
    factor = jnp.exp2(tree_ref[4] - peak)
    total = factor * tree_ref[5]
    summed = [spread(factor, k * 32) * tree_ref[k] for k in range(4)]
    for s in range(32):
        stat = got_ref[s, 32:48, :].astype(F32)
        factor = jnp.exp2(stat[:8] - peak)
        total = total + factor * stat[8:]
        for a in range(2):
            part = got_ref[s, a * 16 : (a + 1) * 16, :].astype(F32)
            for g2 in range(2):
                k = a * 2 + g2
                summed[k] = summed[k] + spread(factor, k * 32) * part[g2 * 8 : (g2 + 1) * 8]
    done = [
        summed[k] / (spread(total, k * 32) + spread(total, k * 32 + 16)) for k in range(4)
    ]
    rows = jnp.concatenate([done[0], done[2], done[1], done[3]], axis=0).astype(BF16)
    for h in range(16):
        out_ref[h] = rows


def project_kernel(x_ref, w_ref, out_ref, turn_ref):
    total = jnp.zeros((64, 512), F32)
    for j in range(4):
        left = jnp.concatenate(
            [
                jnp.concatenate([x_ref[r * 4 + j, g2 * 16 : (g2 + 1) * 16, :] for r in range(4)], axis=0)
                for g2 in range(2)
            ],
            axis=1,
        )
        total = total + jnp.dot(left, w_ref[j], preferred_element_type=F32)
    for r in range(4):
        for a in range(2):
            at = (r * 2 + a) * 8
            turn_ref[:, a * 4 + r, :] = total[at : at + 8]
    out_ref[...] = turn_ref[...].astype(BF16)


def add_kernel(got_ref, draft_ref, verify_ref):
    total = got_ref[0].astype(F32)
    for s in range(1, 8):
        total = total + got_ref[s].astype(F32)
    draft_ref[0] = total[:4].astype(BF16)
    verify_ref[0] = total[4:].astype(BF16)


def swap(array, axis, groups=None):
    return lax.all_to_all(array, axis, 0, 0, tiled=True, axis_index_groups=groups)


def local(
    queries, tree_keys, tree_values, cache_keys, cache_values, block_ids, ancestors, out_weight
):
    weights = swap(jnp.broadcast_to(out_weight[None], (4, 256, 512)), "seq", Y_GROUPS)
    send, tree = pl.pallas_call(
        attend_kernel,
        out_shape=(
            jax.ShapeDtypeStruct((32, 48, 128), BF16),
            jax.ShapeDtypeStruct((6, 8, 128), F32),
        ),
        in_specs=[VMEM] * 7,
        out_specs=(VMEM, VMEM),
        scratch_shapes=[pltpu.VMEM((2, 2, 32, 128), F32), pltpu.VMEM((2, 2, 2, 32, 128), F32)],
        compiler_params=PARAMS,
    )(queries, cache_keys, cache_values, block_ids, tree_keys, tree_values, ancestors)
    got = swap(send, "seq")
    rows = pl.pallas_call(
        combine_kernel,
        out_shape=jax.ShapeDtypeStruct((16, 32, 128), BF16),
        in_specs=[VMEM] * 2,
        out_specs=VMEM,
        compiler_params=PARAMS,
    )(got, tree)
    gathered = swap(rows, "head")
    parts = pl.pallas_call(
        project_kernel,
        out_shape=jax.ShapeDtypeStruct((8, 8, 512), BF16),
        in_specs=[VMEM] * 2,
        out_specs=VMEM,
        scratch_shapes=[pltpu.VMEM((8, 8, 512), F32)],
        compiler_params=PARAMS,
    )(gathered, weights)
    parts = swap(parts, "seq", XC_GROUPS)
    return pl.pallas_call(
        add_kernel,
        out_shape=(jax.ShapeDtypeStruct((1, 4, 512), BF16), jax.ShapeDtypeStruct((1, 4, 512), BF16)),
        in_specs=[VMEM],
        out_specs=(VMEM, VMEM),
        compiler_params=PARAMS,
    )(parts)


def solution(mesh):
    in_specs = (
        P(None, "head", None, None, None),
        P(None, "head", None, None),
        P(None, "head", None, None),
        P("head", "seq", None),
        P("head", "seq", None),
        P("head", None),
        P(),
        P("seq", "head"),
    )
    out_specs = (P("seq", None, "head"), P("seq", None, "head"))
    return jax.shard_map(local, mesh=mesh, in_specs=in_specs, out_specs=out_specs, check_vma=False)
```

time: 189 us -> 86.6 us (0.46)
  waiting for transfers between devices: 83.2 us -> 14.4 us
  between operations: 14.3 us -> 0.68 us
  local copies, waits for them, and re-layouts: 18.1 us -> 7.12 us
  starting transfers between devices: 10.5 us -> 3.51 us
  blocking collectives: 50.8 us -> 57 us
  other arithmetic: 6.12 us -> 0 us
  matrix products: 5.11 us -> 0 us
  Pallas kernels: 0 us -> 3.24 us
    all_gather x1 -> x0, waiting for transfers between devices: 69.8 us -> none  [sent_together(): lax.all_gather(both, axis, axis=dim, tiled=True)]
    all_to_all x1 -> x3, blocking collectives: 27.8 us -> 57 us  [swap(): lax.all_to_all(array, axis, 0, 0, tiled=True, axis_index_groups=groups)]
    all_gather x1 -> x0, blocking collectives: 23.1 us -> none  [sent_together(): lax.all_gather(both, axis, axis=dim, tiled=True)]
    reshape x1 -> x0, local copies, waits for them, and re-layouts: 7.44 us -> none  [local(): jnp.transpose(stacked, (3, 0, 1, 2, 4))]
    all_to_all x1, starting transfers between devices: 10.4 us -> 3.51 us  [swap(): lax.all_to_all(array, axis, 0, 0, tiled=True, axis_index_groups=groups)]
    unnamed x19 -> x16, local copies, waits for them, and re-layouts: 0.14 us -> 6.06 us
    dot_general x9 -> x0, matrix products: 5.11 us -> none  [the longest x2 1.93 us: cache_partial(): jnp.einsum('pgnh,plh->pgnl', query_rows, key_rows, preferred_element_type...]
    pallas_call x0 -> x4, Pallas kernels: none -> 3.24 us  [the longest x1 1.96 us: local(): pl.pallas_call(attend_kernel, out_shape=(jax.ShapeDtypeStruct((32, 48, 12...]
  transfers between devices with their start and end apart: 2 -> 1, of which waited for: 2 -> 1; matrix products, arithmetic and copies ran while one was open for 0% -> 0% of each run, Pallas kernels for 0% -> 0%
where the time goes in v1:
time: 86.6 us; the launch traced here: 86 us
  blocking collectives  57 us (66%)
  waiting for transfers between devices  14.4 us (17%)
  local copies, waits for them, and re-layouts  7.12 us (8%)
  starting transfers between devices  3.51 us (4%)
  Pallas kernels  3.24 us (4%)
    all_to_all x3, blocking collectives, swap(): lax.all_to_all(array, axis, 0, 0, tiled=True, axis_index_groups=groups)  57 us
    all_to_all x1, waiting for transfers between devices, swap(): lax.all_to_all(array, axis, 0, 0, tiled=True, axis_index_groups=groups)  14.4 us
    unnamed x16, local copies, waits for them, and re-layouts  6.06 us
    all_to_all x1, starting transfers between devices, swap(): lax.all_to_all(array, axis, 0, 0, tiled=True, axis_index_groups=groups)  3.51 us
    pallas_call x1, Pallas kernels, local(): pl.pallas_call(attend_kernel, out_shape=(jax.ShapeDtypeStruct((32, 48, 12...  1.96 us
  transfers between devices with their start and end apart: 1, of which 1 were waited for; matrix products, arithmetic and copies ran while one was open for 0% of the time, Pallas kernels for 0%

profile of v1, /device:TPU:1, one launch (start us, length us, event | category | flops | bytes accessed | tf_op | source)
XLA Modules:
  0.0 86.0 jit_solution(17957946484517596268)
XLA Ops:
  0.6 0.0 copy-start
  0.6 1.0 %copy-done = bf16[2,1024,128]{2,1,0:T(8,128)(2,1)S(1)} copy-done((bf16[2,1024,128]{2,1,0:T(8,128)(2,1)S(1)}, bf16[2,1024,128]{2,1,0:T(8,128)(2,1)}, u32[]{:S(2)}) %copy-start) | copy-done | bytes 524312
  1.7 1.0 %copy-done.1 = bf16[2,1024,128]{2,1,0:T(8,128)(2,1)S(1)} copy-done((bf16[2,1024,128]{2,1,0:T(8,128)(2,1)S(1)}, bf16[2,1024,128]{2,1,0:T(8,128)(2,1)}, u32[]{:S(2)}) %copy-start.1) | copy-done | bytes 524312
  2.7 0.0 copy-start.2
  2.7 0.9 %copy-done.2 = bf16[2,2,8,32,128]{4,3,2,1,0:T(8,128)(2,1)S(1)} copy-done((bf16[2,2,8,32,128]{4,3,2,1,0:T(8,128)(2,1)S(1)}, bf16[2,2,8,32,128]{4,3,2,1,0:T(8,128)(2,1)}, u32[]{:S(2)}) %copy-start.2) | copy-done | bytes 262168
  3.7 0.0 copy-start.3
  3.7 0.8 copy-done.3
  4.5 0.0 copy-start.4
  4.5 0.8 copy-done.4
  5.3 0.0 copy-start.5
  5.3 0.8 copy-done.5
  6.0 0.0 copy-start.6
  6.0 0.7 copy-done.6
  6.7 2.0 %shard_map.95 = (bf16[32,48,128]{2,1,0:T(8,128)(2,1)S(1)}, f32[6,8,128]{2,1,0:T(8,128)S(1)}) custom-call(bf16[2,2,8,32,128]{4,3,2,1,0:T(8,128)(2,1)S(1)} %copy-done.2, bf16[2,1024,128]{2,1,0:T(8,128)(2,1)S(1)} %copy-done, bf16[2,1024,128]{2,1,0:T(8,128)(2,1)S(1)} %copy-done.1, s32[2,32]{1,0:T(2,128)S(1)} %copy-done.6, bf16[2,2,32,128]{3,2,1,0:T(8,128)(2,1)S(1)} %copy-done.4, ...), custom_call_target="tpu_custom_call" | custom-call | tf_op jit(solution)/shard_map/pallas_call | solution.py:152
  8.7 19.9 %all_to_all.20.got_ref = bf16[32,48,128]{2,1,0:T(8,128)(2,1)S(1)} all-to-all(bf16[32,48,128]{2,1,0:T(8,128)(2,1)S(1)} %get-tuple-element.4), channel_id=1, replica_groups=mesh['seq'=32,'head'=16] {'seq'}, dimensions={0} | all-to-all | bytes 786432 | tf_op jit(solution)/shard_map/all_to_all | solution.py:145
  28.6 0.0 copy-done.7
  28.6 1.1 %broadcast_in_dim.2 = bf16[4,256,512]{2,1,0:T(8,128)(2,1)} broadcast(bf16[256,512]{1,0:T(8,128)(2,1)S(1)} %copy-done.7), dimensions={1,2} | broadcast | bytes 1310720 | tf_op jit(solution)/shard_map/broadcast_in_dim | solution.py:151
  29.7 3.5 %all-to-all-start.2 = ((bf16[4,256,512]{2,1,0:T(8,128)(2,1)}), bf16[4,256,512]{2,1,0:T(8,128)(2,1)S(1)}, u32[]{:S(2)}, u32[]{:S(2)}) async-start(bf16[4,256,512]{2,1,0:T(8,128)(2,1)} %broadcast_in_dim.2), calls=%async_computation.2 | async-start | bytes 2097152 | tf_op jit(solution)/shard_map/all_to_all | solution.py:145
  33.2 0.4 shard_map.96
  33.5 14.4 %all-to-all-done.2.w_ref = bf16[4,256,512]{2,1,0:T(8,128)(2,1)S(1)} async-done(((bf16[4,256,512]{2,1,0:T(8,128)(2,1)}), bf16[4,256,512]{2,1,0:T(8,128)(2,1)S(1)}, u32[]{:S(2)}, u32[]{:S(2)}) %all-to-all-start.2) | async-done | bytes 1048608 | tf_op jit(solution)/shard_map/all_to_all | solution.py:145
  48.0 25.4 %all_to_all.21.x_ref = bf16[16,32,128]{2,1,0:T(8,128)(2,1)S(1)} all-to-all(bf16[16,32,128]{2,1,0:T(8,128)(2,1)S(1)} %shard_map.96), channel_id=1, replica_groups=mesh['seq'=32,'head'=16] {'head'}, dimensions={0} | all-to-all | bytes 262144 | tf_op jit(solution)/shard_map/all_to_all | solution.py:145
  73.4 0.3 shard_map.97
  73.8 11.7 %all_to_all.22.got_ref = bf16[8,8,512]{2,1,0:T(8,128)(2,1)S(1)} all-to-all(bf16[8,8,512]{2,1,0:T(8,128)(2,1)S(1)} %shard_map.97), channel_id=1, replica_groups={{0,16,32,48,64,80,96,112},{128,144,160,176,192,208,224,240},{256,272,28..., dimensions={0} | all-to-all | bytes 131072 | tf_op jit(solution)/shard_map/all_to_all | solution.py:145
  85.4 0.6 shard_map.98
  (2 shorter events, 0.0 us)
Async XLA Ops:
  0.6 1.0 %copy-start = (bf16[2,1024,128]{2,1,0:T(8,128)(2,1)S(1)}, bf16[2,1024,128]{2,1,0:T(8,128)(2,1)}, u32[]{:S(2)}) copy-start(bf16[2,1024,128]{2,1,0:T(8,128)(2,1)} %k_ref.1) | copy-start | bytes 1572868
  1.7 1.0 %copy-start.1 = (bf16[2,1024,128]{2,1,0:T(8,128)(2,1)S(1)}, bf16[2,1024,128]{2,1,0:T(8,128)(2,1)}, u32[]{:S(2)}) copy-start(bf16[2,1024,128]{2,1,0:T(8,128)(2,1)} %v_ref.1) | copy-start | bytes 1572868
  2.7 0.9 %copy-start.2 = (bf16[2,2,8,32,128]{4,3,2,1,0:T(8,128)(2,1)S(1)}, bf16[2,2,8,32,128]{4,3,2,1,0:T(8,128)(2,1)}, u32[]{:S(2)}) copy-start(bf16[2,2,8,32,128]{4,3,2,1,0:T(8,128)(2,1)} %q_ref.1) | copy-start | bytes 786436
  3.7 0.8 copy-start.3
  4.5 0.8 copy-start.4
  5.3 0.8 copy-start.5
  6.0 0.7 copy-start.6
  8.7 19.9 %copy-start.7 = (bf16[256,512]{1,0:T(8,128)(2,1)S(1)}, bf16[256,512]{1,0:T(8,128)(2,1)}, u32[]{:S(2)}) copy-start(bf16[256,512]{1,0:T(8,128)(2,1)} %param.15) | copy-start | bytes 786436
  29.7 18.3 %all-to-all-start.2 = ((bf16[4,256,512]{2,1,0:T(8,128)(2,1)}), bf16[4,256,512]{2,1,0:T(8,128)(2,1)S(1)}, u32[]{:S(2)}, u32[]{:S(2)}) async-start(bf16[4,256,512]{2,1,0:T(8,128)(2,1)} %broadcast_in_dim.2), calls=%async_computation.2 | async-start | bytes 2097152 | tf_op jit(solution)/shard_map/all_to_all | solution.py:145

commit v2 on v1

--- a/solution.py
+++ b/solution.py
@@ -12,9 +12,10 @@
 F32 = jnp.float32
 BF16 = jnp.bfloat16
 Y_GROUPS = [[y * 8 + k for y in range(4)] for k in range(8)]
-XC_GROUPS = [[y * 8 + k for k in range(8)] for y in range(4)]
+Z_GROUPS = [[r * 4 + j for j in range(4) for r in range(4)]]
 NT = (((1,), (1,)), ((), ()))
 VMEM = pl.BlockSpec(memory_space=pltpu.VMEM)
+HBM = pl.BlockSpec(memory_space=pltpu.HBM)
 PARAMS = pltpu.CompilerParams(vmem_limit_bytes=32 * 1024 * 1024)
 
 
@@ -25,13 +26,31 @@
 
 
 def attend_kernel(
-    q_ref, k_ref, v_ref, ids_ref, tk_ref, tv_ref, anc_ref, send_ref, tree_ref, acc_ref, stat_ref
+    q_hbm, k_hbm, v_hbm, ids_hbm, tk_hbm, tv_hbm, anc_hbm,
+    send_ref, tree_ref,
+    q_ref, k_ref, v_ref, ids_ref, tk_ref, tv_ref, anc_ref, acc_ref, stat_ref, sems,
 ):
+    moves = [
+        (ids_hbm, ids_ref),
+        (k_hbm.at[0], k_ref.at[0]),
+        (q_hbm, q_ref),
+        (v_hbm.at[0], v_ref.at[0]),
+        (k_hbm.at[1], k_ref.at[1]),
+        (v_hbm.at[1], v_ref.at[1]),
+        (tk_hbm, tk_ref),
+        (tv_hbm, tv_ref),
+        (anc_hbm, anc_ref),
+    ]
+    moves = [pltpu.make_async_copy(a, b, sems.at[i]) for i, (a, b) in enumerate(moves)]
+    for move in moves:
+        move.start()
     seq = lax.axis_index("seq")
     head = lax.axis_index("head")
     lane = lax.broadcasted_iota(jnp.int32, (8, 128), 1)
     first_half = (lane % 32) < 16
     for p in range(2):
+        for at in ((0, 1, 2, 3), (4, 5))[p]:
+            moves[at].wait()
         keys = k_ref[p]
         values = jnp.concatenate([v_ref[p], jnp.ones((1024, 128), BF16)], axis=1)
         ids = ids_ref[p : p + 1, :]
@@ -62,6 +81,8 @@
                 high = tot.astype(BF16).astype(F32)
                 tot = jnp.where(first_half, high, tot - high)
                 send_ref[dest, 32:48, :] = jnp.concatenate([m, tot], axis=0).astype(BF16)
+    for move in moves[6:]:
+        move.wait()
     y, x, core = seq // 8, (seq % 8) // 2, seq % 2
     own, gp = x // 2, (x % 2) * 2 + core
     allowed = anc_ref[head // 4] > 0
@@ -116,26 +137,28 @@
 
 
 def project_kernel(x_ref, w_ref, out_ref, turn_ref):
-    total = jnp.zeros((64, 512), F32)
-    for j in range(4):
-        left = jnp.concatenate(
-            [
-                jnp.concatenate([x_ref[r * 4 + j, g2 * 16 : (g2 + 1) * 16, :] for r in range(4)], axis=0)
-                for g2 in range(2)
-            ],
-            axis=1,
-        )
-        total = total + jnp.dot(left, w_ref[j], preferred_element_type=F32)
-    for r in range(4):
-        for a in range(2):
-            at = (r * 2 + a) * 8
-            turn_ref[:, a * 4 + r, :] = total[at : at + 8]
+    left = jnp.concatenate(
+        [
+            jnp.concatenate(
+                [x_ref[q, r * 32 + g2 * 16 : r * 32 + g2 * 16 + 16, :] for q in range(4) for r in range(4)],
+                axis=0,
+            )
+            for g2 in range(2)
+        ],
+        axis=1,
+    )
+    total = jnp.dot(left, w_ref[...], preferred_element_type=F32)
+    for q in range(4):
+        for r in range(4):
+            for a in range(2):
+                at = ((q * 4 + r) * 2 + a) * 8
+                turn_ref[q * 8 : (q + 1) * 8, a * 4 + r, :] = total[at : at + 8]
     out_ref[...] = turn_ref[...].astype(BF16)
 
 
 def add_kernel(got_ref, draft_ref, verify_ref):
     total = got_ref[0].astype(F32)
-    for s in range(1, 8):
+    for s in range(1, 32):
         total = total + got_ref[s].astype(F32)
     draft_ref[0] = total[:4].astype(BF16)
     verify_ref[0] = total[4:].astype(BF16)
@@ -148,17 +171,27 @@
 def local(
     queries, tree_keys, tree_values, cache_keys, cache_values, block_ids, ancestors, out_weight
 ):
-    weights = swap(jnp.broadcast_to(out_weight[None], (4, 256, 512)), "seq", Y_GROUPS)
     send, tree = pl.pallas_call(
         attend_kernel,
         out_shape=(
             jax.ShapeDtypeStruct((32, 48, 128), BF16),
             jax.ShapeDtypeStruct((6, 8, 128), F32),
         ),
-        in_specs=[VMEM] * 7,
+        in_specs=[HBM] * 7,
         out_specs=(VMEM, VMEM),
-        scratch_shapes=[pltpu.VMEM((2, 2, 32, 128), F32), pltpu.VMEM((2, 2, 2, 32, 128), F32)],
-        compiler_params=PARAMS,
+        scratch_shapes=[
+            pltpu.VMEM((2, 2, 8, 32, 128), BF16),
+            pltpu.VMEM((2, 1024, 128), BF16),
+            pltpu.VMEM((2, 1024, 128), BF16),
+            pltpu.VMEM((2, 32), jnp.int32),
+            pltpu.VMEM((2, 2, 32, 128), BF16),
+            pltpu.VMEM((2, 2, 32, 128), BF16),
+            pltpu.VMEM((4, 32, 32), jnp.int32),
+            pltpu.VMEM((2, 2, 32, 128), F32),
+            pltpu.VMEM((2, 2, 2, 32, 128), F32),
+            pltpu.SemaphoreType.DMA((9,)),
+        ],
+        compiler_params=pltpu.CompilerParams(vmem_limit_bytes=55296 * 1024),
     )(queries, cache_keys, cache_values, block_ids, tree_keys, tree_values, ancestors)
     got = swap(send, "seq")
     rows = pl.pallas_call(
@@ -168,16 +201,17 @@
         out_specs=VMEM,
         compiler_params=PARAMS,
     )(got, tree)
-    gathered = swap(rows, "head")
+    gathered = swap(rows, "head", Z_GROUPS)
+    own = swap(gathered.reshape(4, 128, 128), "seq", Y_GROUPS)
     parts = pl.pallas_call(
         project_kernel,
-        out_shape=jax.ShapeDtypeStruct((8, 8, 512), BF16),
+        out_shape=jax.ShapeDtypeStruct((32, 8, 512), BF16),
         in_specs=[VMEM] * 2,
         out_specs=VMEM,
-        scratch_shapes=[pltpu.VMEM((8, 8, 512), F32)],
+        scratch_shapes=[pltpu.VMEM((32, 8, 512), F32)],
         compiler_params=PARAMS,
-    )(gathered, weights)
-    parts = swap(parts, "seq", XC_GROUPS)
+    )(own, out_weight)
+    parts = swap(parts, "seq")
     return pl.pallas_call(
         add_kernel,
         out_shape=(jax.ShapeDtypeStruct((1, 4, 512), BF16), jax.ShapeDtypeStruct((1, 4, 512), BF16)),

time: 86.6 us -> 76.1 us (0.88)
  waiting for transfers between devices: 14.4 us -> 0 us
  blocking collectives: 57 us -> 69.2 us
  local copies, waits for them, and re-layouts: 7.12 us -> 0.01 us
  starting transfers between devices: 3.51 us -> 0 us
  Pallas kernels: 3.24 us -> 5.85 us
    all_to_all x1 -> x0, waiting for transfers between devices: 14.4 us -> none  [swap(): lax.all_to_all(array, axis, 0, 0, tiled=True, axis_index_groups=groups)]
    all_to_all x3 -> x4, blocking collectives: 57 us -> 69.2 us  [swap(): lax.all_to_all(array, axis, 0, 0, tiled=True, axis_index_groups=groups)]
    unnamed x16 -> x4, local copies, waits for them, and re-layouts: 6.06 us -> 0.01 us
    all_to_all x1 -> x0, starting transfers between devices: 3.51 us -> none  [swap(): lax.all_to_all(array, axis, 0, 0, tiled=True, axis_index_groups=groups)]
    pallas_call x1, Pallas kernels: 1.96 us -> 4.56 us  [local(): pl.pallas_call(attend_kernel, out_shape=(jax.ShapeDtypeStruct((32, 48, 12...]
    broadcast_in_dim x1 -> x0, local copies, waits for them, and re-layouts: 1.06 us -> none  [local(): jnp.broadcast_to(out_weight[None], (4, 256, 512))]
  transfers between devices with their start and end apart: 1 -> 0, of which waited for: 1 -> 0; matrix products, arithmetic and copies ran while one was open for 0% -> 0% of each run, Pallas kernels for 0% -> 0%
where the time goes in v2:
time: 76.1 us; the launch traced here: 75.7 us
  blocking collectives  69.2 us (91%)
  Pallas kernels  5.85 us (8%)
    all_to_all x4, blocking collectives, swap(): lax.all_to_all(array, axis, 0, 0, tiled=True, axis_index_groups=groups)  69.2 us
    pallas_call x1, Pallas kernels, local(): pl.pallas_call(attend_kernel, out_shape=(jax.ShapeDtypeStruct((32, 48, 12...  4.56 us

profile of v2, /device:TPU:1, one launch (start us, length us, event | category | flops | bytes accessed | tf_op | source)
XLA Modules:
  0.0 75.7 jit_solution(6381223224298191941)
XLA Ops:
  0.6 4.6 %shard_map.95 = (bf16[32,48,128]{2,1,0:T(8,128)(2,1)}, f32[6,8,128]{2,1,0:T(8,128)}) custom-call(bf16[2,2,8,32,128]{4,3,2,1,0:T(8,128)(2,1)} %q_hbm.1, bf16[2,1024,128]{2,1,0:T(8,128)(2,1)} %k_hbm.1, bf16[2,1024,128]{2,1,0:T(8,128)(2,1)} %v_hbm.1, s32[2,32]{1,0:T(2,128)} %ids_hbm.1, bf16[2,2,32,128]{3,2,1,0:T(8,128)(2,1)} %tk_hbm.1, ...), custom_call_target="tpu_custom_call" | custom-call | tf_op jit(solution)/shard_map/pallas_call | solution.py:174
  5.2 0.0 copy-start.1
  5.2 20.7 %all_to_all.20.got_ref = bf16[32,48,128]{2,1,0:T(8,128)(2,1)S(1)} all-to-all(bf16[32,48,128]{2,1,0:T(8,128)(2,1)} %get-tuple-element.4), channel_id=1, replica_groups=mesh['seq'=32,'head'=16] {'seq'}, dimensions={0} | all-to-all | bytes 786432 | tf_op jit(solution)/shard_map/all_to_all | solution.py:168
  25.9 0.0 copy-done.1
  25.9 0.4 shard_map.96
  26.3 0.0 copy-start
  26.3 25.4 %all_to_all.21 = bf16[16,32,128]{2,1,0:T(8,128)(2,1)S(1)} all-to-all(bf16[16,32,128]{2,1,0:T(8,128)(2,1)S(1)} %shard_map.96), channel_id=1, replica_groups={{0,4,8,12,1,5,9,13,2,6,10,14,3,7,11,15},{16,20,24,28,17,21,25,29,18,22,..., dimensions={0} | all-to-all | bytes 262144 | tf_op jit(solution)/shard_map/all_to_all | solution.py:168
  51.7 7.5 %all_to_all.22.x_ref = bf16[4,128,128]{2,1,0:T(8,128)(2,1)S(1)} all-to-all(bf16[4,128,128]{2,1,0:T(8,128)(2,1)S(1)} %bitcast.1), channel_id=1, replica_groups={{0,128,256,384},{16,144,272,400},{32,160,288,416},{48,176,304,432},{64,..., dimensions={0} | all-to-all | bytes 262144 | tf_op jit(solution)/shard_map/all_to_all | solution.py:168
  59.2 0.0 copy-done
  59.2 0.3 shard_map.97
  59.5 15.6 %all_to_all.23.got_ref = bf16[32,8,512]{2,1,0:T(8,128)(2,1)S(1)} all-to-all(bf16[32,8,512]{2,1,0:T(8,128)(2,1)S(1)} %shard_map.97), channel_id=1, replica_groups=mesh['seq'=32,'head'=16] {'seq'}, dimensions={0} | all-to-all | bytes 524288 | tf_op jit(solution)/shard_map/all_to_all | solution.py:168
  75.1 0.6 shard_map.98
Async XLA Ops:
  5.2 20.7 %copy-start.1 = (f32[6,8,128]{2,1,0:T(8,128)S(1)}, f32[6,8,128]{2,1,0:T(8,128)}, u32[]{:S(2)}) copy-start(f32[6,8,128]{2,1,0:T(8,128)} %get-tuple-element.5.tree_ref) | copy-start | bytes 73732
  26.3 32.9 %copy-start = (bf16[256,512]{1,0:T(8,128)(2,1)S(1)}, bf16[256,512]{1,0:T(8,128)(2,1)}, u32[]{:S(2)}) copy-start(bf16[256,512]{1,0:T(8,128)(2,1)} %w_ref.1) | copy-start | bytes 786436

commit v3 on v1

--- a/solution.py
+++ b/solution.py
@@ -15,6 +15,7 @@
 XC_GROUPS = [[y * 8 + k for k in range(8)] for y in range(4)]
 NT = (((1,), (1,)), ((), ()))
 VMEM = pl.BlockSpec(memory_space=pltpu.VMEM)
+HBM = pl.BlockSpec(memory_space=pltpu.HBM)
 PARAMS = pltpu.CompilerParams(vmem_limit_bytes=32 * 1024 * 1024)
 
 
@@ -25,13 +26,31 @@
 
 
 def attend_kernel(
-    q_ref, k_ref, v_ref, ids_ref, tk_ref, tv_ref, anc_ref, send_ref, tree_ref, acc_ref, stat_ref
+    q_hbm, k_hbm, v_hbm, ids_hbm, tk_hbm, tv_hbm, anc_hbm,
+    send_ref, tree_ref,
+    q_ref, k_ref, v_ref, ids_ref, tk_ref, tv_ref, anc_ref, acc_ref, stat_ref, sems,
 ):
+    moves = [
+        (ids_hbm, ids_ref),
+        (k_hbm.at[0], k_ref.at[0]),
+        (q_hbm, q_ref),
+        (v_hbm.at[0], v_ref.at[0]),
+        (k_hbm.at[1], k_ref.at[1]),
+        (v_hbm.at[1], v_ref.at[1]),
+        (tk_hbm, tk_ref),
+        (tv_hbm, tv_ref),
+        (anc_hbm, anc_ref),
+    ]
+    moves = [pltpu.make_async_copy(a, b, sems.at[i]) for i, (a, b) in enumerate(moves)]
+    for move in moves:
+        move.start()
     seq = lax.axis_index("seq")
     head = lax.axis_index("head")
     lane = lax.broadcasted_iota(jnp.int32, (8, 128), 1)
     first_half = (lane % 32) < 16
     for p in range(2):
+        for at in ((0, 1, 2, 3), (4, 5))[p]:
+            moves[at].wait()
         keys = k_ref[p]
         values = jnp.concatenate([v_ref[p], jnp.ones((1024, 128), BF16)], axis=1)
         ids = ids_ref[p : p + 1, :]
@@ -62,6 +81,8 @@
                 high = tot.astype(BF16).astype(F32)
                 tot = jnp.where(first_half, high, tot - high)
                 send_ref[dest, 32:48, :] = jnp.concatenate([m, tot], axis=0).astype(BF16)
+    for move in moves[6:]:
+        move.wait()
     y, x, core = seq // 8, (seq % 8) // 2, seq % 2
     own, gp = x // 2, (x % 2) * 2 + core
     allowed = anc_ref[head // 4] > 0
@@ -148,17 +169,27 @@
 def local(
     queries, tree_keys, tree_values, cache_keys, cache_values, block_ids, ancestors, out_weight
 ):
-    weights = swap(jnp.broadcast_to(out_weight[None], (4, 256, 512)), "seq", Y_GROUPS)
     send, tree = pl.pallas_call(
         attend_kernel,
         out_shape=(
             jax.ShapeDtypeStruct((32, 48, 128), BF16),
             jax.ShapeDtypeStruct((6, 8, 128), F32),
         ),
-        in_specs=[VMEM] * 7,
+        in_specs=[HBM] * 7,
         out_specs=(VMEM, VMEM),
-        scratch_shapes=[pltpu.VMEM((2, 2, 32, 128), F32), pltpu.VMEM((2, 2, 2, 32, 128), F32)],
-        compiler_params=PARAMS,
+        scratch_shapes=[
+            pltpu.VMEM((2, 2, 8, 32, 128), BF16),
+            pltpu.VMEM((2, 1024, 128), BF16),
+            pltpu.VMEM((2, 1024, 128), BF16),
+            pltpu.VMEM((2, 32), jnp.int32),
+            pltpu.VMEM((2, 2, 32, 128), BF16),
+            pltpu.VMEM((2, 2, 32, 128), BF16),
+            pltpu.VMEM((4, 32, 32), jnp.int32),
+            pltpu.VMEM((2, 2, 32, 128), F32),
+            pltpu.VMEM((2, 2, 2, 32, 128), F32),
+            pltpu.SemaphoreType.DMA((9,)),
+        ],
+        compiler_params=pltpu.CompilerParams(vmem_limit_bytes=55296 * 1024),
     )(queries, cache_keys, cache_values, block_ids, tree_keys, tree_values, ancestors)
     got = swap(send, "seq")
     rows = pl.pallas_call(
@@ -169,6 +200,7 @@
         compiler_params=PARAMS,
     )(got, tree)
     gathered = swap(rows, "head")
+    weights = lax.all_gather(out_weight, "seq", axis_index_groups=Y_GROUPS)
     parts = pl.pallas_call(
         project_kernel,
         out_shape=jax.ShapeDtypeStruct((8, 8, 512), BF16),

time: 86.6 us -> 78.3 us (0.904)
  waiting for transfers between devices: 14.4 us -> 0.68 us
  between operations: 0.68 us -> 14.1 us
  local copies, waits for them, and re-layouts: 7.12 us -> 1.23 us
  starting transfers between devices: 3.51 us -> 0.04 us
  Pallas kernels: 3.24 us -> 5.84 us
  blocking collectives: 57 us -> 56.1 us
    all_to_all x1 -> x0, waiting for transfers between devices: 14.4 us -> none  [swap(): lax.all_to_all(array, axis, 0, 0, tiled=True, axis_index_groups=groups)]
    unnamed x16 -> x4, local copies, waits for them, and re-layouts: 6.06 us -> 1.23 us
    all_to_all x1 -> x0, starting transfers between devices: 3.51 us -> none  [swap(): lax.all_to_all(array, axis, 0, 0, tiled=True, axis_index_groups=groups)]
    pallas_call x1, Pallas kernels: 1.96 us -> 4.55 us  [local(): pl.pallas_call(attend_kernel, out_shape=(jax.ShapeDtypeStruct((32, 48, 12...]
    broadcast_in_dim x1 -> x0, local copies, waits for them, and re-layouts: 1.06 us -> none  [local(): jnp.broadcast_to(out_weight[None], (4, 256, 512))]
    all_to_all x3, blocking collectives: 57 us -> 56.1 us  [swap(): lax.all_to_all(array, axis, 0, 0, tiled=True, axis_index_groups=groups)]
  transfers between devices with their start and end apart: 1 -> 1, of which waited for: 1 -> 0; matrix products, arithmetic and copies ran while one was open for 0% -> 0% of each run, Pallas kernels for 0% -> 6%
where the time goes in v3:
time: 78.3 us; the launch traced here: 77.9 us
  blocking collectives  56.1 us (72%)
  between operations  14.1 us (18%)
  Pallas kernels  5.84 us (7%)
  local copies, waits for them, and re-layouts  1.23 us (2%)
    all_to_all x3, blocking collectives, swap(): lax.all_to_all(array, axis, 0, 0, tiled=True, axis_index_groups=groups)  56.1 us
    pallas_call x1, Pallas kernels, local(): pl.pallas_call(attend_kernel, out_shape=(jax.ShapeDtypeStruct((32, 48, 12...  4.55 us
  transfers between devices with their start and end apart: 1, of which 0 were waited for; matrix products, arithmetic and copies ran while one was open for 0% of the time, Pallas kernels for 6%

profile of v3, /device:TPU:1, one launch (start us, length us, event | category | flops | bytes accessed | tf_op | source)
XLA Modules:
  0.0 77.9 jit_solution(14858592423599114630)
XLA Ops:
  7.2 0.0 all-gather.3.cloned.1.call-start
  7.2 0.7 all-gather.3.cloned.1.call-update
  7.9 4.6 %shard_map.95 = (bf16[32,48,128]{2,1,0:T(8,128)(2,1)}, f32[6,8,128]{2,1,0:T(8,128)}) custom-call(bf16[2,2,8,32,128]{4,3,2,1,0:T(8,128)(2,1)} %q_hbm.1, bf16[2,1024,128]{2,1,0:T(8,128)(2,1)} %k_hbm.1, bf16[2,1024,128]{2,1,0:T(8,128)(2,1)} %v_hbm.1, s32[2,32]{1,0:T(2,128)} %ids_hbm.1, bf16[2,2,32,128]{3,2,1,0:T(8,128)(2,1)} %tk_hbm.1, ...), custom_call_target="tpu_custom_call" | custom-call | tf_op jit(solution)/shard_map/pallas_call | solution.py:172
  12.5 0.0 copy-start.1
  12.5 20.7 %all_to_all.15.got_ref = bf16[32,48,128]{2,1,0:T(8,128)(2,1)S(1)} all-to-all(bf16[32,48,128]{2,1,0:T(8,128)(2,1)} %get-tuple-element.4), channel_id=1, replica_groups=mesh['seq'=32,'head'=16] {'seq'}, dimensions={0} | all-to-all | bytes 786432 | tf_op jit(solution)/shard_map/all_to_all | solution.py:166
  33.2 0.0 copy-done.1
  33.2 0.4 shard_map.96
  33.5 24.9 %all_to_all.16.x_ref = bf16[16,32,128]{2,1,0:T(8,128)(2,1)S(1)} all-to-all(bf16[16,32,128]{2,1,0:T(8,128)(2,1)S(1)} %shard_map.96), channel_id=1, replica_groups=mesh['seq'=32,'head'=16] {'head'}, dimensions={0} | all-to-all | bytes 262144 | tf_op jit(solution)/shard_map/all_to_all | solution.py:166
  58.5 0.0 all-gather.3.cloned.1.call-done
  58.5 0.0 copy-start
  58.5 1.2 %copy-done = bf16[1024,512]{1,0:T(8,128)(2,1)S(1)} copy-done((bf16[1024,512]{1,0:T(8,128)(2,1)S(1)}, bf16[1024,512]{1,0:T(8,128)(2,1)}, u32[]{:S(2)}) %copy-start) | copy-done | bytes 1048600
  59.7 0.3 shard_map.97
  60.0 10.5 %all_to_all.17.got_ref = bf16[8,8,512]{2,1,0:T(8,128)(2,1)S(1)} all-to-all(bf16[8,8,512]{2,1,0:T(8,128)(2,1)S(1)} %shard_map.97), channel_id=1, replica_groups={{0,16,32,48,64,80,96,112},{128,144,160,176,192,208,224,240},{256,272,28..., dimensions={0} | all-to-all | bytes 131072 | tf_op jit(solution)/shard_map/all_to_all | solution.py:166
  70.5 0.6 shard_map.98
Async XLA Ops:
  7.2 51.3 %all-gather.3.cloned.1.call-start = ((), (), s32[]{:S(2)}) async-start(), calls=%async_computation.3 | async-start | bytes 1310720 | tf_op jit(solution)/shard_map/all_gather | solution.py:203
  12.5 20.7 %copy-start.1 = (f32[6,8,128]{2,1,0:T(8,128)S(1)}, f32[6,8,128]{2,1,0:T(8,128)}, u32[]{:S(2)}) copy-start(f32[6,8,128]{2,1,0:T(8,128)} %get-tuple-element.5.tree_ref) | copy-start | bytes 73732
  58.5 1.2 %copy-start = (bf16[1024,512]{1,0:T(8,128)(2,1)S(1)}, bf16[1024,512]{1,0:T(8,128)(2,1)}, u32[]{:S(2)}) copy-start(bf16[1024,512]{1,0:T(8,128)(2,1)} %all-gather.3.cloned.1.call-done) | copy-start | bytes 3145732
Sparse Core Ops, SparseCore 0:
  10.1 36.0 all-gather.2

commit v4 on v3

--- a/solution.py
+++ b/solution.py
@@ -11,10 +11,10 @@
 NEG = -(2.0**100)
 F32 = jnp.float32
 BF16 = jnp.bfloat16
-Y_GROUPS = [[y * 8 + k for y in range(4)] for k in range(8)]
 XC_GROUPS = [[y * 8 + k for k in range(8)] for y in range(4)]
 NT = (((1,), (1,)), ((), ()))
 VMEM = pl.BlockSpec(memory_space=pltpu.VMEM)
+ANY = pl.BlockSpec(memory_space=pl.ANY)
 HBM = pl.BlockSpec(memory_space=pltpu.HBM)
 PARAMS = pltpu.CompilerParams(vmem_limit_bytes=32 * 1024 * 1024)
 
@@ -109,7 +109,7 @@
         tree_ref[4 + k] = tile if k == 0 else jnp.where(first_half, tile, 0.0)
 
 
-def combine_kernel(got_ref, tree_ref, out_ref):
+def combine_kernel(got_ref, tree_ref, before_ref, after_ref, out_ref):
     def spread(tile, at):
         return jnp.broadcast_to(tile[:, at : at + 1], (8, 128))
 
@@ -136,17 +136,22 @@
         out_ref[h] = rows
 
 
-def project_kernel(x_ref, w_ref, out_ref, turn_ref):
+def project_kernel(x_ref, *refs):
+    w_refs, out_ref, turn_ref = refs[:4], refs[4], refs[5]
+    y = lax.axis_index("seq") // 8
     total = jnp.zeros((64, 512), F32)
-    for j in range(4):
+    for k in range(4):
+        j = (y + 4 - k) % 4
         left = jnp.concatenate(
             [
-                jnp.concatenate([x_ref[r * 4 + j, g2 * 16 : (g2 + 1) * 16, :] for r in range(4)], axis=0)
+                jnp.concatenate(
+                    [x_ref[r * 4 + j, g2 * 16 : (g2 + 1) * 16, :] for r in range(4)], axis=0
+                )
                 for g2 in range(2)
             ],
             axis=1,
         )
-        total = total + jnp.dot(left, w_ref[j], preferred_element_type=F32)
+        total = total + jnp.dot(left, w_refs[k][...], preferred_element_type=F32)
     for r in range(4):
         for a in range(2):
             at = (r * 2 + a) * 8
@@ -164,6 +169,10 @@
 
 def swap(array, axis, groups=None):
     return lax.all_to_all(array, axis, 0, 0, tiled=True, axis_index_groups=groups)
+
+
+def shift(array, k):
+    return lax.ppermute(array, "seq", [(s, (s + 8 * k) % 32) for s in range(32)])
 
 
 def local(
@@ -192,23 +201,24 @@
         compiler_params=pltpu.CompilerParams(vmem_limit_bytes=55296 * 1024),
     )(queries, cache_keys, cache_values, block_ids, tree_keys, tree_values, ancestors)
     got = swap(send, "seq")
+    one, three = shift(out_weight, 1), shift(out_weight, 3)
     rows = pl.pallas_call(
         combine_kernel,
         out_shape=jax.ShapeDtypeStruct((16, 32, 128), BF16),
-        in_specs=[VMEM] * 2,
+        in_specs=[VMEM, VMEM, ANY, ANY],
         out_specs=VMEM,
         compiler_params=PARAMS,
-    )(got, tree)
+    )(got, tree, one, three)
     gathered = swap(rows, "head")
-    weights = lax.all_gather(out_weight, "seq", axis_index_groups=Y_GROUPS)
+    two = shift(out_weight, 2)
     parts = pl.pallas_call(
         project_kernel,
         out_shape=jax.ShapeDtypeStruct((8, 8, 512), BF16),
-        in_specs=[VMEM] * 2,
+        in_specs=[VMEM] * 5,
         out_specs=VMEM,
         scratch_shapes=[pltpu.VMEM((8, 8, 512), F32)],
         compiler_params=PARAMS,
-    )(gathered, weights)
+    )(gathered, out_weight, one, two, three)
     parts = swap(parts, "seq", XC_GROUPS)
     return pl.pallas_call(
         add_kernel,

time: 78.3 us -> 69.5 us (0.89)
  blocking collectives: 56.1 us -> 12.2 us
  starting transfers between devices: 0.04 us -> 33.7 us
  waiting for transfers between devices: 0.68 us -> 15.9 us
  between operations: 14.1 us -> 0.72 us
  local copies, waits for them, and re-layouts: 1.23 us -> 0.01 us
    all_to_all x3 -> x1, blocking collectives: 56.1 us -> 12.2 us  [swap(): lax.all_to_all(array, axis, 0, 0, tiled=True, axis_index_groups=groups)]
    all_to_all x0 -> x2, starting transfers between devices: none -> 23.5 us  [swap(): lax.all_to_all(array, axis, 0, 0, tiled=True, axis_index_groups=groups)]
    ppermute x0 -> x3, waiting for transfers between devices: none -> 14.1 us  [shift(): lax.ppermute(array, 'seq', [(s, (s + 8 * k) % 32) for s in range(32)])]
    ppermute x0 -> x3, starting transfers between devices: none -> 10.2 us  [shift(): lax.ppermute(array, 'seq', [(s, (s + 8 * k) % 32) for s in range(32)])]
    all_to_all x0 -> x2, waiting for transfers between devices: none -> 1.78 us  [swap(): lax.all_to_all(array, axis, 0, 0, tiled=True, axis_index_groups=groups)]
    unnamed x4, local copies, waits for them, and re-layouts: 1.23 us -> 0.01 us
  transfers between devices with their start and end apart: 1 -> 5, of which waited for: 0 -> 3; matrix products, arithmetic and copies ran while one was open for 0% -> 0% of each run, Pallas kernels for 6% -> 0%
where the time goes in v4:
time: 69.5 us; the launch traced here: 69.1 us
  starting transfers between devices  33.7 us (48%)
  waiting for transfers between devices  15.9 us (23%)
  blocking collectives  12.2 us (18%)
  Pallas kernels  6.49 us (9%)
  between operations  0.72 us (1%)
    all_to_all x2, starting transfers between devices, swap(): lax.all_to_all(array, axis, 0, 0, tiled=True, axis_index_groups=groups)  23.5 us
    ppermute x3, waiting for transfers between devices, shift(): lax.ppermute(array, 'seq', [(s, (s + 8 * k) % 32) for s in range(32)])  14.1 us
    all_to_all x1, blocking collectives, swap(): lax.all_to_all(array, axis, 0, 0, tiled=True, axis_index_groups=groups)  12.2 us
    ppermute x3, starting transfers between devices, shift(): lax.ppermute(array, 'seq', [(s, (s + 8 * k) % 32) for s in range(32)])  10.2 us
    pallas_call x1, Pallas kernels, local(): pl.pallas_call(attend_kernel, out_shape=(jax.ShapeDtypeStruct((32, 48, 12...  4.56 us
    all_to_all x2, waiting for transfers between devices, swap(): lax.all_to_all(array, axis, 0, 0, tiled=True, axis_index_groups=groups)  1.78 us
  transfers between devices with their start and end apart: 5, of which 3 were waited for; matrix products, arithmetic and copies ran while one was open for 0% of the time, Pallas kernels for 0%

profile of v4, /device:TPU:1, one launch (start us, length us, event | category | flops | bytes accessed | tf_op | source)
XLA Modules:
  0.0 69.1 jit_solution(17775881915810763817)
XLA Ops:
  0.6 4.6 %shard_map.95 = (bf16[32,48,128]{2,1,0:T(8,128)(2,1)}, f32[6,8,128]{2,1,0:T(8,128)}) custom-call(bf16[2,2,8,32,128]{4,3,2,1,0:T(8,128)(2,1)} %q_hbm.1, bf16[2,1024,128]{2,1,0:T(8,128)(2,1)} %k_hbm.1, bf16[2,1024,128]{2,1,0:T(8,128)(2,1)} %v_hbm.1, s32[2,32]{1,0:T(2,128)} %ids_hbm.1, bf16[2,2,32,128]{3,2,1,0:T(8,128)(2,1)} %tk_hbm.1, ...), custom_call_target="tpu_custom_call" | custom-call | tf_op jit(solution)/shard_map/pallas_call | solution.py:181
  5.2 0.0 copy-start
  5.2 0.0 copy-start.1
  5.2 10.6 %all-to-all-start = ((bf16[32,48,128]{2,1,0:T(8,128)(2,1)}), bf16[32,48,128]{2,1,0:T(8,128)(2,1)S(1)}, u32[]{:S(2)}, u32[]{:S(2)}) async-start(bf16[32,48,128]{2,1,0:T(8,128)(2,1)} %get-tuple-element.4), calls=%async_computation | async-start | bytes 786432 | tf_op jit(solution)/shard_map/all_to_all | solution.py:171
  15.8 0.0 copy-done
  15.8 3.3 %collective-permute-start = (bf16[256,512]{1,0:T(8,128)(2,1)S(1)}, bf16[256,512]{1,0:T(8,128)(2,1)S(1)}, u32[]{:S(2)}, u32[]{:S(2)}) collective-permute-start(bf16[256,512]{1,0:T(8,128)(2,1)S(1)} %copy-done), channel_id=1, source_target_pairs={{0,128},{16,144},{32,160},{48,176},{64,192},{80,208},{96,224},{112... | collective-permute-start | bytes 786440 | tf_op jit(solution)/shard_map/ppermute | solution.py:175
  19.1 3.2 %collective-permute-start.1 = (bf16[256,512]{1,0:T(8,128)(2,1)S(1)}, bf16[256,512]{1,0:T(8,128)(2,1)S(1)}, u32[]{:S(2)}, u32[]{:S(2)}) collective-permute-start(bf16[256,512]{1,0:T(8,128)(2,1)S(1)} %copy-done), channel_id=1, source_target_pairs={{0,384},{16,400},{32,416},{48,432},{64,448},{80,464},{96,480},{112... | collective-permute-start | bytes 786440 | tf_op jit(solution)/shard_map/ppermute | solution.py:175
  22.4 7.5 %collective-permute-done.before_ref.refs_1_ = bf16[256,512]{1,0:T(8,128)(2,1)S(1)} collective-permute-done((bf16[256,512]{1,0:T(8,128)(2,1)S(1)}, bf16[256,512]{1,0:T(8,128)(2,1)S(1)}, u32[]{:S(2)}, u32[]{:S(2)}) %collective-permute-start) | collective-permute-done | bytes 262176 | tf_op jit(solution)/shard_map/ppermute | solution.py:175
  29.9 0.0 collective-permute-done.1.after_ref.refs_3_
  29.9 0.0 all-to-all-done.got_ref
  29.9 0.0 copy-done.1
  29.9 1.0 %shard_map.96 = bf16[16,32,128]{2,1,0:T(8,128)(2,1)} custom-call(bf16[32,48,128]{2,1,0:T(8,128)(2,1)S(1)} %all-to-all-done.got_ref, f32[6,8,128]{2,1,0:T(8,128)S(1)} %copy-done.1, bf16[256,512]{1,0:T(8,128)(2,1)S(1)} %collective-permute-done.before_ref.refs_1_, bf16[256,512]{1,0:T(8,128)(2,1)S(1)} %collective-permute-done.1.after_ref.refs_3_), custom_call_target="tpu_custom_call" | custom-call | tf_op jit(solution)/shard_map/pallas_call | solution.py:205
  30.9 13.0 %all-to-all-start.1 = ((bf16[16,32,128]{2,1,0:T(8,128)(2,1)}), bf16[16,32,128]{2,1,0:T(8,128)(2,1)S(1)}, u32[]{:S(2)}, u32[]{:S(2)}) async-start(bf16[16,32,128]{2,1,0:T(8,128)(2,1)} %shard_map.96), calls=%async_computation.1 | async-start | bytes 262144 | tf_op jit(solution)/shard_map/all_to_all | solution.py:171
  43.9 3.6 %collective-permute-start.2 = (bf16[256,512]{1,0:T(8,128)(2,1)S(1)}, bf16[256,512]{1,0:T(8,128)(2,1)S(1)}, u32[]{:S(2)}, u32[]{:S(2)}) collective-permute-start(bf16[256,512]{1,0:T(8,128)(2,1)S(1)} %copy-done), channel_id=1, source_target_pairs={{0,256},{16,272},{32,288},{48,304},{64,320},{80,336},{96,352},{112... | collective-permute-start | bytes 786440 | tf_op jit(solution)/shard_map/ppermute | solution.py:175
  47.5 6.6 %collective-permute-done.2.refs_2_ = bf16[256,512]{1,0:T(8,128)(2,1)S(1)} collective-permute-done((bf16[256,512]{1,0:T(8,128)(2,1)S(1)}, bf16[256,512]{1,0:T(8,128)(2,1)S(1)}, u32[]{:S(2)}, u32[]{:S(2)}) %collective-permute-start.2) | collective-permute-done | bytes 262176 | tf_op jit(solution)/shard_map/ppermute | solution.py:175
  54.1 1.8 %all-to-all-done.1.x_ref = bf16[16,32,128]{2,1,0:T(8,128)(2,1)S(1)} async-done(((bf16[16,32,128]{2,1,0:T(8,128)(2,1)}), bf16[16,32,128]{2,1,0:T(8,128)(2,1)S(1)}, u32[]{:S(2)}, u32[]{:S(2)}) %all-to-all-start.1) | async-done | bytes 131104 | tf_op jit(solution)/shard_map/all_to_all | solution.py:171
  55.9 0.3 shard_map.97
  56.2 12.2 %all_to_all.15.got_ref = bf16[8,8,512]{2,1,0:T(8,128)(2,1)S(1)} all-to-all(bf16[8,8,512]{2,1,0:T(8,128)(2,1)S(1)} %shard_map.97), channel_id=1, replica_groups={{0,16,32,48,64,80,96,112},{128,144,160,176,192,208,224,240},{256,272,28..., dimensions={0} | all-to-all | bytes 131072 | tf_op jit(solution)/shard_map/all_to_all | solution.py:171
  68.4 0.6 shard_map.98
Async XLA Ops:
  5.2 10.6 %copy-start = (bf16[256,512]{1,0:T(8,128)(2,1)S(1)}, bf16[256,512]{1,0:T(8,128)(2,1)}, u32[]{:S(2)}) copy-start(bf16[256,512]{1,0:T(8,128)(2,1)} %refs_0_.1) | copy-start | bytes 786436
  5.2 24.7 %copy-start.1 = (f32[6,8,128]{2,1,0:T(8,128)S(1)}, f32[6,8,128]{2,1,0:T(8,128)}, u32[]{:S(2)}) copy-start(f32[6,8,128]{2,1,0:T(8,128)} %get-tuple-element.5.tree_ref) | copy-start | bytes 73732
  5.2 24.7 %all-to-all-start = ((bf16[32,48,128]{2,1,0:T(8,128)(2,1)}), bf16[32,48,128]{2,1,0:T(8,128)(2,1)S(1)}, u32[]{:S(2)}, u32[]{:S(2)}) async-start(bf16[32,48,128]{2,1,0:T(8,128)(2,1)} %get-tuple-element.4), calls=%async_computation | async-start | bytes 786432 | tf_op jit(solution)/shard_map/all_to_all | solution.py:171
  15.8 14.1 %collective-permute-start = (bf16[256,512]{1,0:T(8,128)(2,1)S(1)}, bf16[256,512]{1,0:T(8,128)(2,1)S(1)}, u32[]{:S(2)}, u32[]{:S(2)}) collective-permute-start(bf16[256,512]{1,0:T(8,128)(2,1)S(1)} %copy-done), channel_id=1, source_target_pairs={{0,128},{16,144},{32,160},{48,176},{64,192},{80,208},{96,224},{112... | collective-permute-start | bytes 786440 | tf_op jit(solution)/shard_map/ppermute | solution.py:175
  19.1 10.8 %collective-permute-start.1 = (bf16[256,512]{1,0:T(8,128)(2,1)S(1)}, bf16[256,512]{1,0:T(8,128)(2,1)S(1)}, u32[]{:S(2)}, u32[]{:S(2)}) collective-permute-start(bf16[256,512]{1,0:T(8,128)(2,1)S(1)} %copy-done), channel_id=1, source_target_pairs={{0,384},{16,400},{32,416},{48,432},{64,448},{80,464},{96,480},{112... | collective-permute-start | bytes 786440 | tf_op jit(solution)/shard_map/ppermute | solution.py:175
  30.9 25.0 %all-to-all-start.1 = ((bf16[16,32,128]{2,1,0:T(8,128)(2,1)}), bf16[16,32,128]{2,1,0:T(8,128)(2,1)S(1)}, u32[]{:S(2)}, u32[]{:S(2)}) async-start(bf16[16,32,128]{2,1,0:T(8,128)(2,1)} %shard_map.96), calls=%async_computation.1 | async-start | bytes 262144 | tf_op jit(solution)/shard_map/all_to_all | solution.py:171
  43.9 10.2 %collective-permute-start.2 = (bf16[256,512]{1,0:T(8,128)(2,1)S(1)}, bf16[256,512]{1,0:T(8,128)(2,1)S(1)}, u32[]{:S(2)}, u32[]{:S(2)}) collective-permute-start(bf16[256,512]{1,0:T(8,128)(2,1)S(1)} %copy-done), channel_id=1, source_target_pairs={{0,256},{16,272},{32,288},{48,304},{64,320},{80,336},{96,352},{112... | collective-permute-start | bytes 786440 | tf_op jit(solution)/shard_map/ppermute | solution.py:175

commit v5 on v4

--- a/solution.py
+++ b/solution.py
@@ -109,7 +109,7 @@
         tree_ref[4 + k] = tile if k == 0 else jnp.where(first_half, tile, 0.0)
 
 
-def combine_kernel(got_ref, tree_ref, before_ref, after_ref, out_ref):
+def combine_kernel(got_ref, tree_ref, before_ref, out_ref):
     def spread(tile, at):
         return jnp.broadcast_to(tile[:, at : at + 1], (8, 128))
 
@@ -205,10 +205,10 @@
     rows = pl.pallas_call(
         combine_kernel,
         out_shape=jax.ShapeDtypeStruct((16, 32, 128), BF16),
-        in_specs=[VMEM, VMEM, ANY, ANY],
+        in_specs=[VMEM, VMEM, ANY],
         out_specs=VMEM,
         compiler_params=PARAMS,
-    )(got, tree, one, three)
+    )(got, tree, one)
     gathered = swap(rows, "head")
     two = shift(out_weight, 2)
     parts = pl.pallas_call(

time: 69.5 us -> 69.8 us (level)
  waiting for transfers between devices: 15.9 us -> 19.4 us
  blocking collectives: 12.2 us -> 10.1 us
  starting transfers between devices: 33.7 us -> 32.6 us
    ppermute x3, waiting for transfers between devices: 14.1 us -> 19.4 us  [shift(): lax.ppermute(array, 'seq', [(s, (s + 8 * k) % 32) for s in range(32)])]
    all_to_all x1, blocking collectives: 12.2 us -> 10.1 us  [swap(): lax.all_to_all(array, axis, 0, 0, tiled=True, axis_index_groups=groups)]
    all_to_all x2, waiting for transfers between devices: 1.78 us -> 0.01 us  [swap(): lax.all_to_all(array, axis, 0, 0, tiled=True, axis_index_groups=groups)]
    ppermute x3, starting transfers between devices: 10.2 us -> 9.1 us  [shift(): lax.ppermute(array, 'seq', [(s, (s + 8 * k) % 32) for s in range(32)])]
where the time goes in v5:
time: 69.8 us; the launch traced here: 69.4 us
  starting transfers between devices  32.6 us (47%)
  waiting for transfers between devices  19.4 us (28%)
  blocking collectives  10.1 us (14%)
  Pallas kernels  6.49 us (9%)
  between operations  0.71 us (1%)
    all_to_all x2, starting transfers between devices, swap(): lax.all_to_all(array, axis, 0, 0, tiled=True, axis_index_groups=groups)  23.5 us
    ppermute x3, waiting for transfers between devices, shift(): lax.ppermute(array, 'seq', [(s, (s + 8 * k) % 32) for s in range(32)])  19.4 us
    all_to_all x1, blocking collectives, swap(): lax.all_to_all(array, axis, 0, 0, tiled=True, axis_index_groups=groups)  10.1 us
    ppermute x3, starting transfers between devices, shift(): lax.ppermute(array, 'seq', [(s, (s + 8 * k) % 32) for s in range(32)])  9.1 us
    pallas_call x1, Pallas kernels, local(): pl.pallas_call(attend_kernel, out_shape=(jax.ShapeDtypeStruct((32, 48, 12...  4.56 us
  transfers between devices with their start and end apart: 5, of which 3 were waited for; matrix products, arithmetic and copies ran while one was open for 0% of the time, Pallas kernels for 0%

profile of v5, /device:TPU:1, one launch (start us, length us, event | category | flops | bytes accessed | tf_op | source)
XLA Modules:
  0.0 69.4 jit_solution(3208944782048151444)
XLA Ops:
  0.6 4.6 %shard_map.95 = (bf16[32,48,128]{2,1,0:T(8,128)(2,1)}, f32[6,8,128]{2,1,0:T(8,128)}) custom-call(bf16[2,2,8,32,128]{4,3,2,1,0:T(8,128)(2,1)} %q_hbm.1, bf16[2,1024,128]{2,1,0:T(8,128)(2,1)} %k_hbm.1, bf16[2,1024,128]{2,1,0:T(8,128)(2,1)} %v_hbm.1, s32[2,32]{1,0:T(2,128)} %ids_hbm.1, bf16[2,2,32,128]{3,2,1,0:T(8,128)(2,1)} %tk_hbm.1, ...), custom_call_target="tpu_custom_call" | custom-call | tf_op jit(solution)/shard_map/pallas_call | solution.py:181
  5.2 0.0 copy-start
  5.2 0.0 copy-start.1
  5.2 10.6 %all-to-all-start = ((bf16[32,48,128]{2,1,0:T(8,128)(2,1)}), bf16[32,48,128]{2,1,0:T(8,128)(2,1)S(1)}, u32[]{:S(2)}, u32[]{:S(2)}) async-start(bf16[32,48,128]{2,1,0:T(8,128)(2,1)} %get-tuple-element.4), calls=%async_computation | async-start | bytes 786432 | tf_op jit(solution)/shard_map/all_to_all | solution.py:171
  15.8 0.0 copy-done
  15.8 3.3 %collective-permute-start = (bf16[256,512]{1,0:T(8,128)(2,1)S(1)}, bf16[256,512]{1,0:T(8,128)(2,1)S(1)}, u32[]{:S(2)}, u32[]{:S(2)}) collective-permute-start(bf16[256,512]{1,0:T(8,128)(2,1)S(1)} %copy-done), channel_id=1, source_target_pairs={{0,128},{16,144},{32,160},{48,176},{64,192},{80,208},{96,224},{112... | collective-permute-start | bytes 786440 | tf_op jit(solution)/shard_map/ppermute | solution.py:175
  19.1 10.8 %collective-permute-done.before_ref.refs_1_ = bf16[256,512]{1,0:T(8,128)(2,1)S(1)} collective-permute-done((bf16[256,512]{1,0:T(8,128)(2,1)S(1)}, bf16[256,512]{1,0:T(8,128)(2,1)S(1)}, u32[]{:S(2)}, u32[]{:S(2)}) %collective-permute-start) | collective-permute-done | bytes 262176 | tf_op jit(solution)/shard_map/ppermute | solution.py:175
  29.9 0.0 all-to-all-done.got_ref
  29.9 0.0 copy-done.1
  29.9 1.0 %shard_map.96 = bf16[16,32,128]{2,1,0:T(8,128)(2,1)} custom-call(bf16[32,48,128]{2,1,0:T(8,128)(2,1)S(1)} %all-to-all-done.got_ref, f32[6,8,128]{2,1,0:T(8,128)S(1)} %copy-done.1, bf16[256,512]{1,0:T(8,128)(2,1)S(1)} %collective-permute-done.before_ref.refs_1_), custom_call_target="tpu_custom_call" | custom-call | tf_op jit(solution)/shard_map/pallas_call | solution.py:205
  30.9 13.0 %all-to-all-start.1 = ((bf16[16,32,128]{2,1,0:T(8,128)(2,1)}), bf16[16,32,128]{2,1,0:T(8,128)(2,1)S(1)}, u32[]{:S(2)}, u32[]{:S(2)}) async-start(bf16[16,32,128]{2,1,0:T(8,128)(2,1)} %shard_map.96), calls=%async_computation.1 | async-start | bytes 262144 | tf_op jit(solution)/shard_map/all_to_all | solution.py:171
  43.9 3.0 %collective-permute-start.1 = (bf16[256,512]{1,0:T(8,128)(2,1)S(1)}, bf16[256,512]{1,0:T(8,128)(2,1)S(1)}, u32[]{:S(2)}, u32[]{:S(2)}) collective-permute-start(bf16[256,512]{1,0:T(8,128)(2,1)S(1)} %copy-done), channel_id=1, source_target_pairs={{0,256},{16,272},{32,288},{48,304},{64,320},{80,336},{96,352},{112... | collective-permute-start | bytes 786440 | tf_op jit(solution)/shard_map/ppermute | solution.py:175
  46.9 2.8 %collective-permute-start.2 = (bf16[256,512]{1,0:T(8,128)(2,1)S(1)}, bf16[256,512]{1,0:T(8,128)(2,1)S(1)}, u32[]{:S(2)}, u32[]{:S(2)}) collective-permute-start(bf16[256,512]{1,0:T(8,128)(2,1)S(1)} %copy-done), channel_id=1, source_target_pairs={{0,384},{16,400},{32,416},{48,432},{64,448},{80,464},{96,480},{112... | collective-permute-start | bytes 786440 | tf_op jit(solution)/shard_map/ppermute | solution.py:175
  49.7 4.4 %collective-permute-done.1.refs_2_ = bf16[256,512]{1,0:T(8,128)(2,1)S(1)} collective-permute-done((bf16[256,512]{1,0:T(8,128)(2,1)S(1)}, bf16[256,512]{1,0:T(8,128)(2,1)S(1)}, u32[]{:S(2)}, u32[]{:S(2)}) %collective-permute-start.1) | collective-permute-done | bytes 262176 | tf_op jit(solution)/shard_map/ppermute | solution.py:175
  54.1 4.2 %collective-permute-done.2.refs_3_ = bf16[256,512]{1,0:T(8,128)(2,1)S(1)} collective-permute-done((bf16[256,512]{1,0:T(8,128)(2,1)S(1)}, bf16[256,512]{1,0:T(8,128)(2,1)S(1)}, u32[]{:S(2)}, u32[]{:S(2)}) %collective-permute-start.2) | collective-permute-done | bytes 262176 | tf_op jit(solution)/shard_map/ppermute | solution.py:175
  58.3 0.0 all-to-all-done.1.x_ref
  58.3 0.3 shard_map.97
  58.6 10.1 %all_to_all.15.got_ref = bf16[8,8,512]{2,1,0:T(8,128)(2,1)S(1)} all-to-all(bf16[8,8,512]{2,1,0:T(8,128)(2,1)S(1)} %shard_map.97), channel_id=1, replica_groups={{0,16,32,48,64,80,96,112},{128,144,160,176,192,208,224,240},{256,272,28..., dimensions={0} | all-to-all | bytes 131072 | tf_op jit(solution)/shard_map/all_to_all | solution.py:171
  68.7 0.6 shard_map.98
Async XLA Ops:
  5.2 10.6 %copy-start = (bf16[256,512]{1,0:T(8,128)(2,1)S(1)}, bf16[256,512]{1,0:T(8,128)(2,1)}, u32[]{:S(2)}) copy-start(bf16[256,512]{1,0:T(8,128)(2,1)} %refs_0_.1) | copy-start | bytes 786436
  5.2 24.7 %copy-start.1 = (f32[6,8,128]{2,1,0:T(8,128)S(1)}, f32[6,8,128]{2,1,0:T(8,128)}, u32[]{:S(2)}) copy-start(f32[6,8,128]{2,1,0:T(8,128)} %get-tuple-element.5.tree_ref) | copy-start | bytes 73732
  5.2 24.7 %all-to-all-start = ((bf16[32,48,128]{2,1,0:T(8,128)(2,1)}), bf16[32,48,128]{2,1,0:T(8,128)(2,1)S(1)}, u32[]{:S(2)}, u32[]{:S(2)}) async-start(bf16[32,48,128]{2,1,0:T(8,128)(2,1)} %get-tuple-element.4), calls=%async_computation | async-start | bytes 786432 | tf_op jit(solution)/shard_map/all_to_all | solution.py:171
  15.8 14.1 %collective-permute-start = (bf16[256,512]{1,0:T(8,128)(2,1)S(1)}, bf16[256,512]{1,0:T(8,128)(2,1)S(1)}, u32[]{:S(2)}, u32[]{:S(2)}) collective-permute-start(bf16[256,512]{1,0:T(8,128)(2,1)S(1)} %copy-done), channel_id=1, source_target_pairs={{0,128},{16,144},{32,160},{48,176},{64,192},{80,208},{96,224},{112... | collective-permute-start | bytes 786440 | tf_op jit(solution)/shard_map/ppermute | solution.py:175
  30.9 27.4 %all-to-all-start.1 = ((bf16[16,32,128]{2,1,0:T(8,128)(2,1)}), bf16[16,32,128]{2,1,0:T(8,128)(2,1)S(1)}, u32[]{:S(2)}, u32[]{:S(2)}) async-start(bf16[16,32,128]{2,1,0:T(8,128)(2,1)} %shard_map.96), calls=%async_computation.1 | async-start | bytes 262144 | tf_op jit(solution)/shard_map/all_to_all | solution.py:171
  43.9 10.2 %collective-permute-start.1 = (bf16[256,512]{1,0:T(8,128)(2,1)S(1)}, bf16[256,512]{1,0:T(8,128)(2,1)S(1)}, u32[]{:S(2)}, u32[]{:S(2)}) collective-permute-start(bf16[256,512]{1,0:T(8,128)(2,1)S(1)} %copy-done), channel_id=1, source_target_pairs={{0,256},{16,272},{32,288},{48,304},{64,320},{80,336},{96,352},{112... | collective-permute-start | bytes 786440 | tf_op jit(solution)/shard_map/ppermute | solution.py:175
  46.9 11.4 %collective-permute-start.2 = (bf16[256,512]{1,0:T(8,128)(2,1)S(1)}, bf16[256,512]{1,0:T(8,128)(2,1)S(1)}, u32[]{:S(2)}, u32[]{:S(2)}) collective-permute-start(bf16[256,512]{1,0:T(8,128)(2,1)S(1)} %copy-done), channel_id=1, source_target_pairs={{0,384},{16,400},{32,416},{48,432},{64,448},{80,464},{96,480},{112... | collective-permute-start | bytes 786440 | tf_op jit(solution)/shard_map/ppermute | solution.py:175

commit v6 on v5

--- a/solution.py
+++ b/solution.py
@@ -109,7 +109,7 @@
         tree_ref[4 + k] = tile if k == 0 else jnp.where(first_half, tile, 0.0)
 
 
-def combine_kernel(got_ref, tree_ref, before_ref, out_ref):
+def combine_kernel(got_ref, tree_ref, out_ref):
     def spread(tile, at):
         return jnp.broadcast_to(tile[:, at : at + 1], (8, 128))
 
@@ -205,12 +205,12 @@
     rows = pl.pallas_call(
         combine_kernel,
         out_shape=jax.ShapeDtypeStruct((16, 32, 128), BF16),
-        in_specs=[VMEM, VMEM, ANY],
+        in_specs=[VMEM, VMEM],
         out_specs=VMEM,
         compiler_params=PARAMS,
-    )(got, tree, one)
+    )(got, tree)
     gathered = swap(rows, "head")
-    two = shift(out_weight, 2)
+    two = shift(one, 1)
     parts = pl.pallas_call(
         project_kernel,
         out_shape=jax.ShapeDtypeStruct((8, 8, 512), BF16),

time: 69.8 us -> 64.1 us (0.918)
  waiting for transfers between devices: 19.4 us -> 14.8 us
    ppermute x3, waiting for transfers between devices: 19.4 us -> 7.84 us  [shift(): lax.ppermute(array, 'seq', [(s, (s + 8 * k) % 32) for s in range(32)])]
    all_to_all x2, waiting for transfers between devices: 0.01 us -> 6.95 us  [swap(): lax.all_to_all(array, axis, 0, 0, tiled=True, axis_index_groups=groups)]
  transfers between devices with their start and end apart: 5 -> 5, of which waited for: 3 -> 3; matrix products, arithmetic and copies ran while one was open for 0% -> 0% of each run, Pallas kernels for 0% -> 2%
where the time goes in v6:
time: 64.1 us; the launch traced here: 63.6 us
  starting transfers between devices  32.2 us (50%)
  waiting for transfers between devices  14.8 us (23%)
  blocking collectives  9.45 us (15%)
  Pallas kernels  6.49 us (10%)
  between operations  0.72 us (1%)
    all_to_all x2, starting transfers between devices, swap(): lax.all_to_all(array, axis, 0, 0, tiled=True, axis_index_groups=groups)  23.5 us
    all_to_all x1, blocking collectives, swap(): lax.all_to_all(array, axis, 0, 0, tiled=True, axis_index_groups=groups)  9.45 us
    ppermute x3, starting transfers between devices, shift(): lax.ppermute(array, 'seq', [(s, (s + 8 * k) % 32) for s in range(32)])  8.62 us
    ppermute x3, waiting for transfers between devices, shift(): lax.ppermute(array, 'seq', [(s, (s + 8 * k) % 32) for s in range(32)])  7.84 us
    all_to_all x2, waiting for transfers between devices, swap(): lax.all_to_all(array, axis, 0, 0, tiled=True, axis_index_groups=groups)  6.95 us
    pallas_call x1, Pallas kernels, local(): pl.pallas_call(attend_kernel, out_shape=(jax.ShapeDtypeStruct((32, 48, 12...  4.56 us
  transfers between devices with their start and end apart: 5, of which 3 were waited for; matrix products, arithmetic and copies ran while one was open for 0% of the time, Pallas kernels for 2%

profile of v6, /device:TPU:1, one launch (start us, length us, event | category | flops | bytes accessed | tf_op | source)
XLA Modules:
  0.0 63.6 jit_solution(7360217742931855348)
XLA Ops:
  0.6 4.6 %shard_map.95 = (bf16[32,48,128]{2,1,0:T(8,128)(2,1)}, f32[6,8,128]{2,1,0:T(8,128)}) custom-call(bf16[2,2,8,32,128]{4,3,2,1,0:T(8,128)(2,1)} %q_hbm.1, bf16[2,1024,128]{2,1,0:T(8,128)(2,1)} %k_hbm.1, bf16[2,1024,128]{2,1,0:T(8,128)(2,1)} %v_hbm.1, s32[2,32]{1,0:T(2,128)} %ids_hbm.1, bf16[2,2,32,128]{3,2,1,0:T(8,128)(2,1)} %tk_hbm.1, ...), custom_call_target="tpu_custom_call" | custom-call | tf_op jit(solution)/shard_map/pallas_call | solution.py:181
  5.2 0.0 copy-start
  5.2 0.0 copy-start.1
  5.2 10.6 %all-to-all-start = ((bf16[32,48,128]{2,1,0:T(8,128)(2,1)}), bf16[32,48,128]{2,1,0:T(8,128)(2,1)S(1)}, u32[]{:S(2)}, u32[]{:S(2)}) async-start(bf16[32,48,128]{2,1,0:T(8,128)(2,1)} %get-tuple-element.4), calls=%async_computation | async-start | bytes 786432 | tf_op jit(solution)/shard_map/all_to_all | solution.py:171
  15.8 0.0 copy-done
  15.8 3.3 %collective-permute-start = (bf16[256,512]{1,0:T(8,128)(2,1)S(1)}, bf16[256,512]{1,0:T(8,128)(2,1)S(1)}, u32[]{:S(2)}, u32[]{:S(2)}) collective-permute-start(bf16[256,512]{1,0:T(8,128)(2,1)S(1)} %copy-done), channel_id=1, source_target_pairs={{0,128},{16,144},{32,160},{48,176},{64,192},{80,208},{96,224},{112... | collective-permute-start | bytes 786440 | tf_op jit(solution)/shard_map/ppermute | solution.py:175
  19.1 7.0 %all-to-all-done.got_ref = bf16[32,48,128]{2,1,0:T(8,128)(2,1)S(1)} async-done(((bf16[32,48,128]{2,1,0:T(8,128)(2,1)}), bf16[32,48,128]{2,1,0:T(8,128)(2,1)S(1)}, u32[]{:S(2)}, u32[]{:S(2)}) %all-to-all-start) | async-done | bytes 393248 | tf_op jit(solution)/shard_map/all_to_all | solution.py:171
  26.1 0.0 copy-done.1
  26.1 1.0 %shard_map.96 = bf16[16,32,128]{2,1,0:T(8,128)(2,1)} custom-call(bf16[32,48,128]{2,1,0:T(8,128)(2,1)S(1)} %all-to-all-done.got_ref, f32[6,8,128]{2,1,0:T(8,128)S(1)} %copy-done.1), custom_call_target="tpu_custom_call" | custom-call | tf_op jit(solution)/shard_map/pallas_call | solution.py:205
  27.1 13.0 %all-to-all-start.1 = ((bf16[16,32,128]{2,1,0:T(8,128)(2,1)}), bf16[16,32,128]{2,1,0:T(8,128)(2,1)S(1)}, u32[]{:S(2)}, u32[]{:S(2)}) async-start(bf16[16,32,128]{2,1,0:T(8,128)(2,1)} %shard_map.96), calls=%async_computation.1 | async-start | bytes 262144 | tf_op jit(solution)/shard_map/all_to_all | solution.py:171
  40.1 2.8 %collective-permute-start.2 = (bf16[256,512]{1,0:T(8,128)(2,1)S(1)}, bf16[256,512]{1,0:T(8,128)(2,1)S(1)}, u32[]{:S(2)}, u32[]{:S(2)}) collective-permute-start(bf16[256,512]{1,0:T(8,128)(2,1)S(1)} %copy-done), channel_id=1, source_target_pairs={{0,384},{16,400},{32,416},{48,432},{64,448},{80,464},{96,480},{112... | collective-permute-start | bytes 786440 | tf_op jit(solution)/shard_map/ppermute | solution.py:175
  42.9 0.0 collective-permute-done.refs_1_
  42.9 2.5 %collective-permute-start.1 = (bf16[256,512]{1,0:T(8,128)(2,1)S(1)}, bf16[256,512]{1,0:T(8,128)(2,1)S(1)}, u32[]{:S(2)}, u32[]{:S(2)}) collective-permute-start(bf16[256,512]{1,0:T(8,128)(2,1)S(1)} %collective-permute-done.refs_1_), channel_id=1, source_target_pairs={{0,128},{16,144},{32,160},{48,176},{64,192},{80,208},{96,224},{112... | collective-permute-start | bytes 786440 | tf_op jit(solution)/shard_map/ppermute | solution.py:175
  45.4 3.8 %collective-permute-done.2.refs_3_ = bf16[256,512]{1,0:T(8,128)(2,1)S(1)} collective-permute-done((bf16[256,512]{1,0:T(8,128)(2,1)S(1)}, bf16[256,512]{1,0:T(8,128)(2,1)S(1)}, u32[]{:S(2)}, u32[]{:S(2)}) %collective-permute-start.2) | collective-permute-done | bytes 262176 | tf_op jit(solution)/shard_map/ppermute | solution.py:175
  49.2 4.0 %collective-permute-done.1.refs_2_ = bf16[256,512]{1,0:T(8,128)(2,1)S(1)} collective-permute-done((bf16[256,512]{1,0:T(8,128)(2,1)S(1)}, bf16[256,512]{1,0:T(8,128)(2,1)S(1)}, u32[]{:S(2)}, u32[]{:S(2)}) %collective-permute-start.1) | collective-permute-done | bytes 262176 | tf_op jit(solution)/shard_map/ppermute | solution.py:175
  53.2 0.0 all-to-all-done.1.x_ref
  53.2 0.3 shard_map.97
  53.6 9.5 %all_to_all.15.got_ref = bf16[8,8,512]{2,1,0:T(8,128)(2,1)S(1)} all-to-all(bf16[8,8,512]{2,1,0:T(8,128)(2,1)S(1)} %shard_map.97), channel_id=1, replica_groups={{0,16,32,48,64,80,96,112},{128,144,160,176,192,208,224,240},{256,272,28..., dimensions={0} | all-to-all | bytes 131072 | tf_op jit(solution)/shard_map/all_to_all | solution.py:171
  63.0 0.6 shard_map.98
Async XLA Ops:
  5.2 10.6 %copy-start = (bf16[256,512]{1,0:T(8,128)(2,1)S(1)}, bf16[256,512]{1,0:T(8,128)(2,1)}, u32[]{:S(2)}) copy-start(bf16[256,512]{1,0:T(8,128)(2,1)} %refs_0_.1) | copy-start | bytes 786436
  5.2 20.9 %copy-start.1 = (f32[6,8,128]{2,1,0:T(8,128)S(1)}, f32[6,8,128]{2,1,0:T(8,128)}, u32[]{:S(2)}) copy-start(f32[6,8,128]{2,1,0:T(8,128)} %get-tuple-element.5.tree_ref) | copy-start | bytes 73732
  5.2 20.9 %all-to-all-start = ((bf16[32,48,128]{2,1,0:T(8,128)(2,1)}), bf16[32,48,128]{2,1,0:T(8,128)(2,1)S(1)}, u32[]{:S(2)}, u32[]{:S(2)}) async-start(bf16[32,48,128]{2,1,0:T(8,128)(2,1)} %get-tuple-element.4), calls=%async_computation | async-start | bytes 786432 | tf_op jit(solution)/shard_map/all_to_all | solution.py:171
  15.8 27.1 %collective-permute-start = (bf16[256,512]{1,0:T(8,128)(2,1)S(1)}, bf16[256,512]{1,0:T(8,128)(2,1)S(1)}, u32[]{:S(2)}, u32[]{:S(2)}) collective-permute-start(bf16[256,512]{1,0:T(8,128)(2,1)S(1)} %copy-done), channel_id=1, source_target_pairs={{0,128},{16,144},{32,160},{48,176},{64,192},{80,208},{96,224},{112... | collective-permute-start | bytes 786440 | tf_op jit(solution)/shard_map/ppermute | solution.py:175
  27.1 26.1 %all-to-all-start.1 = ((bf16[16,32,128]{2,1,0:T(8,128)(2,1)}), bf16[16,32,128]{2,1,0:T(8,128)(2,1)S(1)}, u32[]{:S(2)}, u32[]{:S(2)}) async-start(bf16[16,32,128]{2,1,0:T(8,128)(2,1)} %shard_map.96), calls=%async_computation.1 | async-start | bytes 262144 | tf_op jit(solution)/shard_map/all_to_all | solution.py:171
  40.1 9.1 %collective-permute-start.2 = (bf16[256,512]{1,0:T(8,128)(2,1)S(1)}, bf16[256,512]{1,0:T(8,128)(2,1)S(1)}, u32[]{:S(2)}, u32[]{:S(2)}) collective-permute-start(bf16[256,512]{1,0:T(8,128)(2,1)S(1)} %copy-done), channel_id=1, source_target_pairs={{0,384},{16,400},{32,416},{48,432},{64,448},{80,464},{96,480},{112... | collective-permute-start | bytes 786440 | tf_op jit(solution)/shard_map/ppermute | solution.py:175
  42.9 10.4 %collective-permute-start.1 = (bf16[256,512]{1,0:T(8,128)(2,1)S(1)}, bf16[256,512]{1,0:T(8,128)(2,1)S(1)}, u32[]{:S(2)}, u32[]{:S(2)}) collective-permute-start(bf16[256,512]{1,0:T(8,128)(2,1)S(1)} %collective-permute-done.refs_1_), channel_id=1, source_target_pairs={{0,128},{16,144},{32,160},{48,176},{64,192},{80,208},{96,224},{112... | collective-permute-start | bytes 786440 | tf_op jit(solution)/shard_map/ppermute | solution.py:175

commit v7 on v6

--- a/solution.py
+++ b/solution.py
@@ -136,6 +136,11 @@
         out_ref[h] = rows
 
 
+def onward_kernel(one_ref, three_ref, out_ref):
+    del three_ref
+    out_ref[...] = one_ref[...]
+
+
 def project_kernel(x_ref, *refs):
     w_refs, out_ref, turn_ref = refs[:4], refs[4], refs[5]
     y = lax.axis_index("seq") // 8
@@ -210,7 +215,15 @@
         compiler_params=PARAMS,
     )(got, tree)
     gathered = swap(rows, "head")
-    two = shift(one, 1)
+    onward = pl.pallas_call(
+        onward_kernel,
+        out_shape=jax.ShapeDtypeStruct((256, 512), BF16),
+        in_specs=[VMEM, ANY],
+        out_specs=VMEM,
+        cost_estimate=pl.CostEstimate(flops=10**10, bytes_accessed=0, transcendentals=0),
+        compiler_params=PARAMS,
+    )(one, three)
+    two = shift(onward, 1)
     parts = pl.pallas_call(
         project_kernel,
         out_shape=jax.ShapeDtypeStruct((8, 8, 512), BF16),

time: 64.1 us -> 64.1 us (level)
  waiting for transfers between devices: 14.8 us -> 13.6 us
  blocking collectives: 9.45 us -> 10.5 us
    all_to_all x2, waiting for transfers between devices: 6.95 us -> 5.46 us  [swap(): lax.all_to_all(array, axis, 0, 0, tiled=True, axis_index_groups=groups)]
    all_to_all x1, blocking collectives: 9.45 us -> 10.5 us  [swap(): lax.all_to_all(array, axis, 0, 0, tiled=True, axis_index_groups=groups)]
where the time goes in v7:
time: 64.1 us; the launch traced here: 63.6 us
  starting transfers between devices  32.4 us (51%)
  waiting for transfers between devices  13.6 us (21%)
  blocking collectives  10.5 us (16%)
  Pallas kernels  6.51 us (10%)
  between operations  0.74 us (1%)
    all_to_all x2, starting transfers between devices, swap(): lax.all_to_all(array, axis, 0, 0, tiled=True, axis_index_groups=groups)  23.5 us
    all_to_all x1, blocking collectives, swap(): lax.all_to_all(array, axis, 0, 0, tiled=True, axis_index_groups=groups)  10.5 us
    ppermute x3, starting transfers between devices, shift(): lax.ppermute(array, 'seq', [(s, (s + 8 * k) % 32) for s in range(32)])  8.81 us
    ppermute x3, waiting for transfers between devices, shift(): lax.ppermute(array, 'seq', [(s, (s + 8 * k) % 32) for s in range(32)])  8.1 us
    all_to_all x2, waiting for transfers between devices, swap(): lax.all_to_all(array, axis, 0, 0, tiled=True, axis_index_groups=groups)  5.46 us
    pallas_call x1, Pallas kernels, local(): pl.pallas_call(attend_kernel, out_shape=(jax.ShapeDtypeStruct((32, 48, 12...  4.56 us
  transfers between devices with their start and end apart: 5, of which 3 were waited for; matrix products, arithmetic and copies ran while one was open for 0% of the time, Pallas kernels for 2%

profile of v7, /device:TPU:1, one launch (start us, length us, event | category | flops | bytes accessed | tf_op | source)
XLA Modules:
  0.0 63.6 jit_solution(7970860940199749692)
XLA Ops:
  0.6 4.6 %shard_map.95 = (bf16[32,48,128]{2,1,0:T(8,128)(2,1)}, f32[6,8,128]{2,1,0:T(8,128)}) custom-call(bf16[2,2,8,32,128]{4,3,2,1,0:T(8,128)(2,1)} %q_hbm.1, bf16[2,1024,128]{2,1,0:T(8,128)(2,1)} %k_hbm.1, bf16[2,1024,128]{2,1,0:T(8,128)(2,1)} %v_hbm.1, s32[2,32]{1,0:T(2,128)} %ids_hbm.1, bf16[2,2,32,128]{3,2,1,0:T(8,128)(2,1)} %tk_hbm.1, ...), custom_call_target="tpu_custom_call" | custom-call | tf_op jit(solution)/shard_map/pallas_call | solution.py:186
  5.2 0.0 copy-start
  5.2 0.0 copy-start.1
  5.2 10.6 %all-to-all-start = ((bf16[32,48,128]{2,1,0:T(8,128)(2,1)}), bf16[32,48,128]{2,1,0:T(8,128)(2,1)S(1)}, u32[]{:S(2)}, u32[]{:S(2)}) async-start(bf16[32,48,128]{2,1,0:T(8,128)(2,1)} %get-tuple-element.4), calls=%async_computation | async-start | bytes 786432 | tf_op jit(solution)/shard_map/all_to_all | solution.py:176
  15.8 0.0 copy-done
  15.8 3.3 %collective-permute-start = (bf16[256,512]{1,0:T(8,128)(2,1)S(1)}, bf16[256,512]{1,0:T(8,128)(2,1)S(1)}, u32[]{:S(2)}, u32[]{:S(2)}) collective-permute-start(bf16[256,512]{1,0:T(8,128)(2,1)S(1)} %copy-done), channel_id=1, source_target_pairs={{0,128},{16,144},{32,160},{48,176},{64,192},{80,208},{96,224},{112... | collective-permute-start | bytes 786440 | tf_op jit(solution)/shard_map/ppermute | solution.py:180
  19.1 3.2 %collective-permute-start.1 = (bf16[256,512]{1,0:T(8,128)(2,1)S(1)}, bf16[256,512]{1,0:T(8,128)(2,1)S(1)}, u32[]{:S(2)}, u32[]{:S(2)}) collective-permute-start(bf16[256,512]{1,0:T(8,128)(2,1)S(1)} %copy-done), channel_id=1, source_target_pairs={{0,384},{16,400},{32,416},{48,432},{64,448},{80,464},{96,480},{112... | collective-permute-start | bytes 786440 | tf_op jit(solution)/shard_map/ppermute | solution.py:180
  22.4 3.7 %all-to-all-done.got_ref = bf16[32,48,128]{2,1,0:T(8,128)(2,1)S(1)} async-done(((bf16[32,48,128]{2,1,0:T(8,128)(2,1)}), bf16[32,48,128]{2,1,0:T(8,128)(2,1)S(1)}, u32[]{:S(2)}, u32[]{:S(2)}) %all-to-all-start) | async-done | bytes 393248 | tf_op jit(solution)/shard_map/all_to_all | solution.py:176
  26.1 0.0 copy-done.1
  26.1 1.0 %shard_map.96 = bf16[16,32,128]{2,1,0:T(8,128)(2,1)} custom-call(bf16[32,48,128]{2,1,0:T(8,128)(2,1)S(1)} %all-to-all-done.got_ref, f32[6,8,128]{2,1,0:T(8,128)S(1)} %copy-done.1), custom_call_target="tpu_custom_call" | custom-call | tf_op jit(solution)/shard_map/pallas_call | solution.py:210
  27.1 13.0 %all-to-all-start.1 = ((bf16[16,32,128]{2,1,0:T(8,128)(2,1)}), bf16[16,32,128]{2,1,0:T(8,128)(2,1)S(1)}, u32[]{:S(2)}, u32[]{:S(2)}) async-start(bf16[16,32,128]{2,1,0:T(8,128)(2,1)} %shard_map.96), calls=%async_computation.1 | async-start | bytes 262144 | tf_op jit(solution)/shard_map/all_to_all | solution.py:176
  40.1 0.0 collective-permute-done.one_ref.refs_1_
  40.1 0.0 collective-permute-done.1.three_ref.refs_3_
  40.1 2.2 %collective-permute-start.2 = (bf16[256,512]{1,0:T(8,128)(2,1)S(1)}, bf16[256,512]{1,0:T(8,128)(2,1)S(1)}, u32[]{:S(2)}, u32[]{:S(2)}) collective-permute-start(bf16[256,512]{1,0:T(8,128)(2,1)S(1)} %shard_map.97), channel_id=1, source_target_pairs={{0,128},{16,144},{32,160},{48,176},{64,192},{80,208},{96,224},{112... | collective-permute-start | bytes 786440 | tf_op jit(solution)/shard_map/ppermute | solution.py:180
  42.4 8.1 %collective-permute-done.2.refs_2_ = bf16[256,512]{1,0:T(8,128)(2,1)S(1)} collective-permute-done((bf16[256,512]{1,0:T(8,128)(2,1)S(1)}, bf16[256,512]{1,0:T(8,128)(2,1)S(1)}, u32[]{:S(2)}, u32[]{:S(2)}) %collective-permute-start.2) | collective-permute-done | bytes 262176 | tf_op jit(solution)/shard_map/ppermute | solution.py:180
  50.5 1.8 %all-to-all-done.1.x_ref = bf16[16,32,128]{2,1,0:T(8,128)(2,1)S(1)} async-done(((bf16[16,32,128]{2,1,0:T(8,128)(2,1)}), bf16[16,32,128]{2,1,0:T(8,128)(2,1)S(1)}, u32[]{:S(2)}, u32[]{:S(2)}) %all-to-all-start.1) | async-done | bytes 131104 | tf_op jit(solution)/shard_map/all_to_all | solution.py:176
  52.2 0.3 shard_map.98
  52.6 10.5 %all_to_all.15.got_ref = bf16[8,8,512]{2,1,0:T(8,128)(2,1)S(1)} all-to-all(bf16[8,8,512]{2,1,0:T(8,128)(2,1)S(1)} %shard_map.98), channel_id=1, replica_groups={{0,16,32,48,64,80,96,112},{128,144,160,176,192,208,224,240},{256,272,28..., dimensions={0} | all-to-all | bytes 131072 | tf_op jit(solution)/shard_map/all_to_all | solution.py:176
  63.0 0.6 shard_map.99
  (1 shorter events, 0.0 us)
Async XLA Ops:
  5.2 10.6 %copy-start = (bf16[256,512]{1,0:T(8,128)(2,1)S(1)}, bf16[256,512]{1,0:T(8,128)(2,1)}, u32[]{:S(2)}) copy-start(bf16[256,512]{1,0:T(8,128)(2,1)} %refs_0_.1) | copy-start | bytes 786436
  5.2 20.9 %copy-start.1 = (f32[6,8,128]{2,1,0:T(8,128)S(1)}, f32[6,8,128]{2,1,0:T(8,128)}, u32[]{:S(2)}) copy-start(f32[6,8,128]{2,1,0:T(8,128)} %get-tuple-element.5.tree_ref) | copy-start | bytes 73732
  5.2 20.9 %all-to-all-start = ((bf16[32,48,128]{2,1,0:T(8,128)(2,1)}), bf16[32,48,128]{2,1,0:T(8,128)(2,1)S(1)}, u32[]{:S(2)}, u32[]{:S(2)}) async-start(bf16[32,48,128]{2,1,0:T(8,128)(2,1)} %get-tuple-element.4), calls=%async_computation | async-start | bytes 786432 | tf_op jit(solution)/shard_map/all_to_all | solution.py:176
  15.8 24.3 %collective-permute-start = (bf16[256,512]{1,0:T(8,128)(2,1)S(1)}, bf16[256,512]{1,0:T(8,128)(2,1)S(1)}, u32[]{:S(2)}, u32[]{:S(2)}) collective-permute-start(bf16[256,512]{1,0:T(8,128)(2,1)S(1)} %copy-done), channel_id=1, source_target_pairs={{0,128},{16,144},{32,160},{48,176},{64,192},{80,208},{96,224},{112... | collective-permute-start | bytes 786440 | tf_op jit(solution)/shard_map/ppermute | solution.py:180
  19.1 21.0 %collective-permute-start.1 = (bf16[256,512]{1,0:T(8,128)(2,1)S(1)}, bf16[256,512]{1,0:T(8,128)(2,1)S(1)}, u32[]{:S(2)}, u32[]{:S(2)}) collective-permute-start(bf16[256,512]{1,0:T(8,128)(2,1)S(1)} %copy-done), channel_id=1, source_target_pairs={{0,384},{16,400},{32,416},{48,432},{64,448},{80,464},{96,480},{112... | collective-permute-start | bytes 786440 | tf_op jit(solution)/shard_map/ppermute | solution.py:180
  27.1 25.1 %all-to-all-start.1 = ((bf16[16,32,128]{2,1,0:T(8,128)(2,1)}), bf16[16,32,128]{2,1,0:T(8,128)(2,1)S(1)}, u32[]{:S(2)}, u32[]{:S(2)}) async-start(bf16[16,32,128]{2,1,0:T(8,128)(2,1)} %shard_map.96), calls=%async_computation.1 | async-start | bytes 262144 | tf_op jit(solution)/shard_map/all_to_all | solution.py:176
  40.1 10.3 %collective-permute-start.2 = (bf16[256,512]{1,0:T(8,128)(2,1)S(1)}, bf16[256,512]{1,0:T(8,128)(2,1)S(1)}, u32[]{:S(2)}, u32[]{:S(2)}) collective-permute-start(bf16[256,512]{1,0:T(8,128)(2,1)S(1)} %shard_map.97), channel_id=1, source_target_pairs={{0,128},{16,144},{32,160},{48,176},{64,192},{80,208},{96,224},{112... | collective-permute-start | bytes 786440 | tf_op jit(solution)/shard_map/ppermute | solution.py:180

commit v8 on v7

--- a/solution.py
+++ b/solution.py
@@ -27,19 +27,20 @@
 
 def attend_kernel(
     q_hbm, k_hbm, v_hbm, ids_hbm, tk_hbm, tv_hbm, anc_hbm,
-    send_ref, tree_ref,
-    q_ref, k_ref, v_ref, ids_ref, tk_ref, tv_ref, anc_ref, acc_ref, stat_ref, sems,
+    send_hbm, tree_hbm,
+    q_ref, k_ref, v_ref, ids_ref, tk_ref, tv_ref, anc_ref,
+    send_ref, tree_ref, acc_ref, stat_ref, sems, out_sems,
 ):
     moves = [
-        (ids_hbm, ids_ref),
         (k_hbm.at[0], k_ref.at[0]),
         (q_hbm, q_ref),
+        (ids_hbm, ids_ref),
         (v_hbm.at[0], v_ref.at[0]),
-        (k_hbm.at[1], k_ref.at[1]),
-        (v_hbm.at[1], v_ref.at[1]),
         (tk_hbm, tk_ref),
         (tv_hbm, tv_ref),
         (anc_hbm, anc_ref),
+        (k_hbm.at[1], k_ref.at[1]),
+        (v_hbm.at[1], v_ref.at[1]),
     ]
     moves = [pltpu.make_async_copy(a, b, sems.at[i]) for i, (a, b) in enumerate(moves)]
     for move in moves:
@@ -47,28 +48,71 @@
     seq = lax.axis_index("seq")
     head = lax.axis_index("head")
     lane = lax.broadcasted_iota(jnp.int32, (8, 128), 1)
-    first_half = (lane % 32) < 16
+    part = (lane % 32) // 8
+    leaving = []
+
+    def leave(source, target):
+        copy = pltpu.make_async_copy(source, target, out_sems.at[len(leaving)])
+        copy.start()
+        leaving.append(copy)
+
+    def tree_part():
+        y, x, core = seq // 8, (seq % 8) // 2, seq % 2
+        own, gp = x // 2, (x % 2) * 2 + core
+        allowed = anc_ref[head // 4] > 0
+        allowed = jnp.concatenate([allowed, allowed], axis=0)
+        for a in range(2):
+            q = q_ref[a, own, pl.ds(gp * 2, 2)].reshape(64, 128)
+            t = lax.dot_general(q, tk_ref[a, own], NT, preferred_element_type=F32) * SCALE
+            t = jnp.where(allowed, t, NEG)
+            peak = jnp.max(t, axis=1, keepdims=True)
+            w = jnp.where(allowed, jnp.exp2(t - peak), 0.0)
+            total = jnp.sum(w, axis=1, keepdims=True)
+            summed = jnp.dot(w.astype(BF16), tv_ref[a, own], preferred_element_type=F32)
+            acc_ref[a] = summed.reshape(2, 32, 128)
+            stat_ref[0, a] = jnp.broadcast_to(peak, (64, 128)).reshape(2, 32, 128)
+            stat_ref[1, a] = jnp.broadcast_to(total, (64, 128)).reshape(2, 32, 128)
+        start = pl.multiple_of(y * 8, 8)
+        for a in range(2):
+            for g2 in range(2):
+                tree_ref[a * 2 + g2] = acc_ref[a, g2, pl.ds(start, 8), :]
+        peak, total = (
+            four_lanes(
+                lane, [stat_ref[k, a, g2, pl.ds(start, 8), :] for a in range(2) for g2 in range(2)]
+            )
+            for k in range(2)
+        )
+        tree_ref[4] = peak
+        tree_ref[5] = jnp.where(part == 2, total, 0.0)
+
+    for move in moves[:3]:
+        move.wait()
     for p in range(2):
-        for at in ((0, 1, 2, 3), (4, 5))[p]:
-            moves[at].wait()
+        if p == 1:
+            for move in moves[4:]:
+                move.wait()
         keys = k_ref[p]
-        values = jnp.concatenate([v_ref[p], jnp.ones((1024, 128), BF16)], axis=1)
         ids = ids_ref[p : p + 1, :]
         bias = []
         for b in range(8):
             hit = jnp.max(jnp.where(ids == seq * 8 + b, 1.0, 0.0), axis=1, keepdims=True)
             bias.append(jnp.broadcast_to(jnp.where(hit > 0.5, 0.0, NEG), (1, BLOCK)))
         bias = jnp.concatenate(bias, axis=1)
-        peaks, sums = [], []
+        peaks, weights = [], []
         for a in range(2):
             q = q_ref[a, p].reshape(256, 128)
             t = lax.dot_general(q, keys, NT, preferred_element_type=F32) * SCALE
             if a == 0:
                 t = t + bias
             peak = jnp.max(t, axis=1, keepdims=True).astype(BF16).astype(F32)
-            w = jnp.exp2(t - peak).astype(BF16)
+            weights.append(jnp.exp2(t - peak).astype(BF16))
             peaks.append(peak)
-            sums.append(jnp.dot(w, values, preferred_element_type=F32))
+        if p == 0:
+            moves[3].wait()
+        values = jnp.concatenate([v_ref[p], jnp.ones((1024, 128), BF16)], axis=1)
+        sums = [jnp.dot(w, values, preferred_element_type=F32) for w in weights]
+        if p == 1:
+            tree_part()
         for y in range(4):
             for gp in range(4):
                 dest = y * 8 + p * 4 + gp
@@ -79,34 +123,13 @@
                 m = four_lanes(lane, [peaks[a][r : r + 8] for a in range(2) for r in rows])
                 tot = four_lanes(lane, [sums[a][r : r + 8, 128:] for a in range(2) for r in rows])
                 high = tot.astype(BF16).astype(F32)
-                tot = jnp.where(first_half, high, tot - high)
-                send_ref[dest, 32:48, :] = jnp.concatenate([m, tot], axis=0).astype(BF16)
-    for move in moves[6:]:
-        move.wait()
-    y, x, core = seq // 8, (seq % 8) // 2, seq % 2
-    own, gp = x // 2, (x % 2) * 2 + core
-    allowed = anc_ref[head // 4] > 0
-    allowed = jnp.concatenate([allowed, allowed], axis=0)
-    for a in range(2):
-        q = q_ref[a, own, pl.ds(gp * 2, 2)].reshape(64, 128)
-        t = lax.dot_general(q, tk_ref[a, own], NT, preferred_element_type=F32) * SCALE
-        t = jnp.where(allowed, t, NEG)
-        peak = jnp.max(t, axis=1, keepdims=True)
-        w = jnp.where(allowed, jnp.exp2(t - peak), 0.0)
-        total = jnp.sum(w, axis=1, keepdims=True)
-        summed = jnp.dot(w.astype(BF16), tv_ref[a, own], preferred_element_type=F32)
-        acc_ref[a] = summed.reshape(2, 32, 128)
-        stat_ref[0, a] = jnp.broadcast_to(peak, (64, 128)).reshape(2, 32, 128)
-        stat_ref[1, a] = jnp.broadcast_to(total, (64, 128)).reshape(2, 32, 128)
-    start = pl.multiple_of(y * 8, 8)
-    for a in range(2):
-        for g2 in range(2):
-            tree_ref[a * 2 + g2] = acc_ref[a, g2, pl.ds(start, 8), :]
-    for k in range(2):
-        tile = four_lanes(
-            lane, [stat_ref[k, a, g2, pl.ds(start, 8), :] for a in range(2) for g2 in range(2)]
-        )
-        tree_ref[4 + k] = tile if k == 0 else jnp.where(first_half, tile, 0.0)
+                stat = jnp.where(part < 2, m, jnp.where(part == 2, high, tot - high))
+                send_ref[dest, 32:40, :] = stat.astype(BF16)
+            chunk = pl.ds(y * 8 + p * 4, 4)
+            leave(send_ref.at[chunk], send_hbm.at[chunk])
+    leave(tree_ref, tree_hbm)
+    for copy in leaving:
+        copy.wait()
 
 
 def combine_kernel(got_ref, tree_ref, out_ref):
@@ -115,21 +138,21 @@
 
     peak = tree_ref[4]
     for s in range(32):
-        peak = jnp.maximum(peak, got_ref[s, 32:48, :].astype(F32)[:8])
+        peak = jnp.maximum(peak, got_ref[s, 32:40, :].astype(F32))
     factor = jnp.exp2(tree_ref[4] - peak)
-    total = factor * tree_ref[5]
+    total = pltpu.roll(factor, 16, 1) * tree_ref[5]
     summed = [spread(factor, k * 32) * tree_ref[k] for k in range(4)]
     for s in range(32):
-        stat = got_ref[s, 32:48, :].astype(F32)
-        factor = jnp.exp2(stat[:8] - peak)
-        total = total + factor * stat[8:]
+        stat = got_ref[s, 32:40, :].astype(F32)
+        factor = jnp.exp2(stat - peak)
+        total = total + pltpu.roll(factor, 16, 1) * stat
         for a in range(2):
             part = got_ref[s, a * 16 : (a + 1) * 16, :].astype(F32)
             for g2 in range(2):
                 k = a * 2 + g2
                 summed[k] = summed[k] + spread(factor, k * 32) * part[g2 * 8 : (g2 + 1) * 8]
     done = [
-        summed[k] / (spread(total, k * 32) + spread(total, k * 32 + 16)) for k in range(4)
+        summed[k] / (spread(total, k * 32 + 16) + spread(total, k * 32 + 24)) for k in range(4)
     ]
     rows = jnp.concatenate([done[0], done[2], done[1], done[3]], axis=0).astype(BF16)
     for h in range(16):
@@ -176,21 +199,17 @@
     return lax.all_to_all(array, axis, 0, 0, tiled=True, axis_index_groups=groups)
 
 
-def shift(array, k):
-    return lax.ppermute(array, "seq", [(s, (s + 8 * k) % 32) for s in range(32)])
-
-
-def local(
-    queries, tree_keys, tree_values, cache_keys, cache_values, block_ids, ancestors, out_weight
+def attend(
+    queries, cache_keys, cache_values, block_ids, tree_keys, tree_values, ancestors
 ):
-    send, tree = pl.pallas_call(
+    return pl.pallas_call(
         attend_kernel,
         out_shape=(
-            jax.ShapeDtypeStruct((32, 48, 128), BF16),
+            jax.ShapeDtypeStruct((32, 40, 128), BF16),
             jax.ShapeDtypeStruct((6, 8, 128), F32),
         ),
         in_specs=[HBM] * 7,
-        out_specs=(VMEM, VMEM),
+        out_specs=(HBM, HBM),
         scratch_shapes=[
             pltpu.VMEM((2, 2, 8, 32, 128), BF16),
             pltpu.VMEM((2, 1024, 128), BF16),
@@ -199,12 +218,27 @@
             pltpu.VMEM((2, 2, 32, 128), BF16),
             pltpu.VMEM((2, 2, 32, 128), BF16),
             pltpu.VMEM((4, 32, 32), jnp.int32),
+            pltpu.VMEM((32, 40, 128), BF16),
+            pltpu.VMEM((6, 8, 128), F32),
             pltpu.VMEM((2, 2, 32, 128), F32),
             pltpu.VMEM((2, 2, 2, 32, 128), F32),
+            pltpu.SemaphoreType.DMA((9,)),
             pltpu.SemaphoreType.DMA((9,)),
         ],
         compiler_params=pltpu.CompilerParams(vmem_limit_bytes=55296 * 1024),
     )(queries, cache_keys, cache_values, block_ids, tree_keys, tree_values, ancestors)
+
+
+def shift(array, k):
+    return lax.ppermute(array, "seq", [(s, (s + 8 * k) % 32) for s in range(32)])
+
+
+def local(
+    queries, tree_keys, tree_values, cache_keys, cache_values, block_ids, ancestors, out_weight
+):
+    send, tree = attend(
+        queries, cache_keys, cache_values, block_ids, tree_keys, tree_values, ancestors
+    )
     got = swap(send, "seq")
     one, three = shift(out_weight, 1), shift(out_weight, 3)
     rows = pl.pallas_call(

time: 64.1 us -> 62.8 us (0.980)
  waiting for transfers between devices: 13.6 us -> 12.8 us
    all_to_all x2, waiting for transfers between devices: 5.46 us -> 4.78 us  [swap(): lax.all_to_all(array, axis, 0, 0, tiled=True, axis_index_groups=groups)]
    pallas_call x1, Pallas kernels: 4.56 us -> 3.89 us  [attend(): pl.pallas_call(attend_kernel, out_shape=(jax.ShapeDtypeStruct((32, 40, 12...]
where the time goes in v8:
time: 62.8 us; the launch traced here: 62.4 us
  starting transfers between devices  32.5 us (52%)
  waiting for transfers between devices  12.8 us (20%)
  blocking collectives  10.4 us (17%)
  Pallas kernels  5.95 us (9%)
  between operations  0.74 us (1%)
    all_to_all x2, starting transfers between devices, swap(): lax.all_to_all(array, axis, 0, 0, tiled=True, axis_index_groups=groups)  23.5 us
    all_to_all x1, blocking collectives, swap(): lax.all_to_all(array, axis, 0, 0, tiled=True, axis_index_groups=groups)  10.4 us
    ppermute x3, starting transfers between devices, shift(): lax.ppermute(array, 'seq', [(s, (s + 8 * k) % 32) for s in range(32)])  8.96 us
    ppermute x3, waiting for transfers between devices, shift(): lax.ppermute(array, 'seq', [(s, (s + 8 * k) % 32) for s in range(32)])  8 us
    all_to_all x2, waiting for transfers between devices, swap(): lax.all_to_all(array, axis, 0, 0, tiled=True, axis_index_groups=groups)  4.78 us
    pallas_call x1, Pallas kernels, attend(): pl.pallas_call(attend_kernel, out_shape=(jax.ShapeDtypeStruct((32, 40, 12...  3.89 us
  transfers between devices with their start and end apart: 5, of which 3 were waited for; matrix products, arithmetic and copies ran while one was open for 0% of the time, Pallas kernels for 2%

profile of v8, /device:TPU:1, one launch (start us, length us, event | category | flops | bytes accessed | tf_op | source)
XLA Modules:
  0.0 62.4 jit_solution(11509394123482024070)
XLA Ops:
  0.6 3.9 %shard_map.95 = (bf16[32,40,128]{2,1,0:T(8,128)(2,1)}, f32[6,8,128]{2,1,0:T(8,128)}) custom-call(bf16[2,2,8,32,128]{4,3,2,1,0:T(8,128)(2,1)} %q_hbm.1, bf16[2,1024,128]{2,1,0:T(8,128)(2,1)} %k_hbm.1, bf16[2,1024,128]{2,1,0:T(8,128)(2,1)} %v_hbm.1, s32[2,32]{1,0:T(2,128)} %ids_hbm.1, bf16[2,2,32,128]{3,2,1,0:T(8,128)(2,1)} %tk_hbm.1, ...), custom_call_target="tpu_custom_call" | custom-call | tf_op jit(solution)/shard_map/pallas_call | solution.py:205
  4.5 0.0 copy-start
  4.5 0.0 copy-start.1
  4.5 10.6 %all-to-all-start = ((bf16[32,40,128]{2,1,0:T(8,128)(2,1)}), bf16[32,40,128]{2,1,0:T(8,128)(2,1)S(1)}, u32[]{:S(2)}, u32[]{:S(2)}) async-start(bf16[32,40,128]{2,1,0:T(8,128)(2,1)} %get-tuple-element.4), calls=%async_computation | async-start | bytes 655360 | tf_op jit(solution)/shard_map/all_to_all | solution.py:199
  15.1 0.0 copy-done
  15.1 3.3 %collective-permute-start = (bf16[256,512]{1,0:T(8,128)(2,1)S(1)}, bf16[256,512]{1,0:T(8,128)(2,1)S(1)}, u32[]{:S(2)}, u32[]{:S(2)}) collective-permute-start(bf16[256,512]{1,0:T(8,128)(2,1)S(1)} %copy-done), channel_id=1, source_target_pairs={{0,128},{16,144},{32,160},{48,176},{64,192},{80,208},{96,224},{112... | collective-permute-start | bytes 786440 | tf_op jit(solution)/shard_map/ppermute | solution.py:233
  18.5 3.2 %collective-permute-start.1 = (bf16[256,512]{1,0:T(8,128)(2,1)S(1)}, bf16[256,512]{1,0:T(8,128)(2,1)S(1)}, u32[]{:S(2)}, u32[]{:S(2)}) collective-permute-start(bf16[256,512]{1,0:T(8,128)(2,1)S(1)} %copy-done), channel_id=1, source_target_pairs={{0,384},{16,400},{32,416},{48,432},{64,448},{80,464},{96,480},{112... | collective-permute-start | bytes 786440 | tf_op jit(solution)/shard_map/ppermute | solution.py:233
  21.7 3.1 %all-to-all-done.got_ref = bf16[32,40,128]{2,1,0:T(8,128)(2,1)S(1)} async-done(((bf16[32,40,128]{2,1,0:T(8,128)(2,1)}), bf16[32,40,128]{2,1,0:T(8,128)(2,1)S(1)}, u32[]{:S(2)}, u32[]{:S(2)}) %all-to-all-start) | async-done | bytes 327712 | tf_op jit(solution)/shard_map/all_to_all | solution.py:199
  24.8 0.0 copy-done.1
  24.8 1.1 %shard_map.96 = bf16[16,32,128]{2,1,0:T(8,128)(2,1)} custom-call(bf16[32,40,128]{2,1,0:T(8,128)(2,1)S(1)} %all-to-all-done.got_ref, f32[6,8,128]{2,1,0:T(8,128)S(1)} %copy-done.1), custom_call_target="tpu_custom_call" | custom-call | tf_op jit(solution)/shard_map/pallas_call | solution.py:244
  25.9 13.0 %all-to-all-start.1 = ((bf16[16,32,128]{2,1,0:T(8,128)(2,1)}), bf16[16,32,128]{2,1,0:T(8,128)(2,1)S(1)}, u32[]{:S(2)}, u32[]{:S(2)}) async-start(bf16[16,32,128]{2,1,0:T(8,128)(2,1)} %shard_map.96), calls=%async_computation.1 | async-start | bytes 262144 | tf_op jit(solution)/shard_map/all_to_all | solution.py:199
  38.9 0.0 collective-permute-done.one_ref.refs_1_
  38.9 0.0 collective-permute-done.1.three_ref.refs_3_
  38.9 2.4 %collective-permute-start.2 = (bf16[256,512]{1,0:T(8,128)(2,1)S(1)}, bf16[256,512]{1,0:T(8,128)(2,1)S(1)}, u32[]{:S(2)}, u32[]{:S(2)}) collective-permute-start(bf16[256,512]{1,0:T(8,128)(2,1)S(1)} %shard_map.97), channel_id=1, source_target_pairs={{0,128},{16,144},{32,160},{48,176},{64,192},{80,208},{96,224},{112... | collective-permute-start | bytes 786440 | tf_op jit(solution)/shard_map/ppermute | solution.py:233
  41.3 8.0 %collective-permute-done.2.refs_2_ = bf16[256,512]{1,0:T(8,128)(2,1)S(1)} collective-permute-done((bf16[256,512]{1,0:T(8,128)(2,1)S(1)}, bf16[256,512]{1,0:T(8,128)(2,1)S(1)}, u32[]{:S(2)}, u32[]{:S(2)}) %collective-permute-start.2) | collective-permute-done | bytes 262176 | tf_op jit(solution)/shard_map/ppermute | solution.py:233
  49.3 1.7 %all-to-all-done.1.x_ref = bf16[16,32,128]{2,1,0:T(8,128)(2,1)S(1)} async-done(((bf16[16,32,128]{2,1,0:T(8,128)(2,1)}), bf16[16,32,128]{2,1,0:T(8,128)(2,1)S(1)}, u32[]{:S(2)}, u32[]{:S(2)}) %all-to-all-start.1) | async-done | bytes 131104 | tf_op jit(solution)/shard_map/all_to_all | solution.py:199
  51.0 0.3 shard_map.98
  51.4 10.4 %all_to_all.15.got_ref = bf16[8,8,512]{2,1,0:T(8,128)(2,1)S(1)} all-to-all(bf16[8,8,512]{2,1,0:T(8,128)(2,1)S(1)} %shard_map.98), channel_id=1, replica_groups={{0,16,32,48,64,80,96,112},{128,144,160,176,192,208,224,240},{256,272,28..., dimensions={0} | all-to-all | bytes 131072 | tf_op jit(solution)/shard_map/all_to_all | solution.py:199
  61.8 0.6 shard_map.99
  (1 shorter events, 0.0 us)
Async XLA Ops:
  4.5 10.6 %copy-start = (bf16[256,512]{1,0:T(8,128)(2,1)S(1)}, bf16[256,512]{1,0:T(8,128)(2,1)}, u32[]{:S(2)}) copy-start(bf16[256,512]{1,0:T(8,128)(2,1)} %refs_0_.1) | copy-start | bytes 786436
  4.5 20.2 %copy-start.1 = (f32[6,8,128]{2,1,0:T(8,128)S(1)}, f32[6,8,128]{2,1,0:T(8,128)}, u32[]{:S(2)}) copy-start(f32[6,8,128]{2,1,0:T(8,128)} %get-tuple-element.5.tree_ref) | copy-start | bytes 73732
  4.5 20.2 %all-to-all-start = ((bf16[32,40,128]{2,1,0:T(8,128)(2,1)}), bf16[32,40,128]{2,1,0:T(8,128)(2,1)S(1)}, u32[]{:S(2)}, u32[]{:S(2)}) async-start(bf16[32,40,128]{2,1,0:T(8,128)(2,1)} %get-tuple-element.4), calls=%async_computation | async-start | bytes 655360 | tf_op jit(solution)/shard_map/all_to_all | solution.py:199
  15.1 23.8 %collective-permute-start = (bf16[256,512]{1,0:T(8,128)(2,1)S(1)}, bf16[256,512]{1,0:T(8,128)(2,1)S(1)}, u32[]{:S(2)}, u32[]{:S(2)}) collective-permute-start(bf16[256,512]{1,0:T(8,128)(2,1)S(1)} %copy-done), channel_id=1, source_target_pairs={{0,128},{16,144},{32,160},{48,176},{64,192},{80,208},{96,224},{112... | collective-permute-start | bytes 786440 | tf_op jit(solution)/shard_map/ppermute | solution.py:233
  18.5 20.4 %collective-permute-start.1 = (bf16[256,512]{1,0:T(8,128)(2,1)S(1)}, bf16[256,512]{1,0:T(8,128)(2,1)S(1)}, u32[]{:S(2)}, u32[]{:S(2)}) collective-permute-start(bf16[256,512]{1,0:T(8,128)(2,1)S(1)} %copy-done), channel_id=1, source_target_pairs={{0,384},{16,400},{32,416},{48,432},{64,448},{80,464},{96,480},{112... | collective-permute-start | bytes 786440 | tf_op jit(solution)/shard_map/ppermute | solution.py:233
  25.9 25.1 %all-to-all-start.1 = ((bf16[16,32,128]{2,1,0:T(8,128)(2,1)}), bf16[16,32,128]{2,1,0:T(8,128)(2,1)S(1)}, u32[]{:S(2)}, u32[]{:S(2)}) async-start(bf16[16,32,128]{2,1,0:T(8,128)(2,1)} %shard_map.96), calls=%async_computation.1 | async-start | bytes 262144 | tf_op jit(solution)/shard_map/all_to_all | solution.py:199
  38.9 10.4 %collective-permute-start.2 = (bf16[256,512]{1,0:T(8,128)(2,1)S(1)}, bf16[256,512]{1,0:T(8,128)(2,1)S(1)}, u32[]{:S(2)}, u32[]{:S(2)}) collective-permute-start(bf16[256,512]{1,0:T(8,128)(2,1)S(1)} %shard_map.97), channel_id=1, source_target_pairs={{0,128},{16,144},{32,160},{48,176},{64,192},{80,208},{96,224},{112... | collective-permute-start | bytes 786440 | tf_op jit(solution)/shard_map/ppermute | solution.py:233

commit v9 on v8

--- a/solution.py
+++ b/solution.py
@@ -85,7 +85,7 @@
         tree_ref[4] = peak
         tree_ref[5] = jnp.where(part == 2, total, 0.0)
 
-    for move in moves[:3]:
+    for move in moves[:4]:
         move.wait()
     for p in range(2):
         if p == 1:
@@ -107,8 +107,6 @@
             peak = jnp.max(t, axis=1, keepdims=True).astype(BF16).astype(F32)
             weights.append(jnp.exp2(t - peak).astype(BF16))
             peaks.append(peak)
-        if p == 0:
-            moves[3].wait()
         values = jnp.concatenate([v_ref[p], jnp.ones((1024, 128), BF16)], axis=1)
         sums = [jnp.dot(w, values, preferred_element_type=F32) for w in weights]
         if p == 1:
@@ -159,27 +157,29 @@
         out_ref[h] = rows
 
 
-def onward_kernel(one_ref, three_ref, out_ref):
-    del three_ref
-    out_ref[...] = one_ref[...]
-
-
-def project_kernel(x_ref, *refs):
-    w_refs, out_ref, turn_ref = refs[:4], refs[4], refs[5]
+def onward_kernel(one_ref, three_ref, low_ref, high_ref):
+    low_ref[...] = one_ref[:128]
+    high_ref[...] = three_ref[128:]
+
+
+def project_kernel(x_ref, own_ref, one_ref, three_ref, low_ref, high_ref, out_ref, turn_ref):
     y = lax.axis_index("seq") // 8
     total = jnp.zeros((64, 512), F32)
     for k in range(4):
         j = (y + 4 - k) % 4
-        left = jnp.concatenate(
-            [
-                jnp.concatenate(
-                    [x_ref[r * 4 + j, g2 * 16 : (g2 + 1) * 16, :] for r in range(4)], axis=0
-                )
-                for g2 in range(2)
-            ],
-            axis=1,
-        )
-        total = total + jnp.dot(left, w_refs[k][...], preferred_element_type=F32)
+        left = [
+            jnp.concatenate(
+                [x_ref[r * 4 + j, g2 * 16 : (g2 + 1) * 16, :] for r in range(4)], axis=0
+            )
+            for g2 in range(2)
+        ]
+        right = (own_ref, one_ref, None, three_ref)[k]
+        if right is None:
+            right = jnp.concatenate([low_ref[...], high_ref[...]], axis=0)
+        else:
+            right = right[...]
+        left = jnp.concatenate(left, axis=1)
+        total = total + jnp.dot(left, right, preferred_element_type=F32)
     for r in range(4):
         for a in range(2):
             at = (r * 2 + a) * 8
@@ -249,23 +249,23 @@
         compiler_params=PARAMS,
     )(got, tree)
     gathered = swap(rows, "head")
-    onward = pl.pallas_call(
+    low, high = pl.pallas_call(
         onward_kernel,
-        out_shape=jax.ShapeDtypeStruct((256, 512), BF16),
-        in_specs=[VMEM, ANY],
-        out_specs=VMEM,
+        out_shape=(jax.ShapeDtypeStruct((128, 512), BF16),) * 2,
+        in_specs=[VMEM] * 2,
+        out_specs=(VMEM, VMEM),
         cost_estimate=pl.CostEstimate(flops=10**10, bytes_accessed=0, transcendentals=0),
         compiler_params=PARAMS,
     )(one, three)
-    two = shift(onward, 1)
+    low, high = shift(low, 1), shift(high, 3)
     parts = pl.pallas_call(
         project_kernel,
         out_shape=jax.ShapeDtypeStruct((8, 8, 512), BF16),
-        in_specs=[VMEM] * 5,
+        in_specs=[VMEM] * 6,
         out_specs=VMEM,
         scratch_shapes=[pltpu.VMEM((8, 8, 512), F32)],
         compiler_params=PARAMS,
-    )(gathered, out_weight, one, two, three)
+    )(gathered, out_weight, one, three, low, high)
     parts = swap(parts, "seq", XC_GROUPS)
     return pl.pallas_call(
         add_kernel,

time: 62.8 us -> 62.7 us (level)
  waiting for transfers between devices: 12.8 us -> 8.65 us
  starting transfers between devices: 32.5 us -> 36.6 us
    ppermute x3 -> x4, waiting for transfers between devices: 8 us -> 2.49 us  [shift(): lax.ppermute(array, 'seq', [(s, (s + 8 * k) % 32) for s in range(32)])]
    ppermute x3 -> x4, starting transfers between devices: 8.96 us -> 13.1 us  [shift(): lax.ppermute(array, 'seq', [(s, (s + 8 * k) % 32) for s in range(32)])]
    all_to_all x2, waiting for transfers between devices: 4.78 us -> 6.15 us  [swap(): lax.all_to_all(array, axis, 0, 0, tiled=True, axis_index_groups=groups)]
  transfers between devices with their start and end apart: 5 -> 6, of which waited for: 3 -> 4; matrix products, arithmetic and copies ran while one was open for 0% -> 0% of each run, Pallas kernels for 2% -> 2%
where the time goes in v9:
time: 62.7 us; the launch traced here: 62.3 us
  starting transfers between devices  36.6 us (58%)
  blocking collectives  10.4 us (17%)
  waiting for transfers between devices  8.65 us (14%)
  Pallas kernels  5.86 us (9%)
  between operations  0.74 us (1%)
    all_to_all x2, starting transfers between devices, swap(): lax.all_to_all(array, axis, 0, 0, tiled=True, axis_index_groups=groups)  23.5 us
    ppermute x4, starting transfers between devices, shift(): lax.ppermute(array, 'seq', [(s, (s + 8 * k) % 32) for s in range(32)])  13.1 us
    all_to_all x1, blocking collectives, swap(): lax.all_to_all(array, axis, 0, 0, tiled=True, axis_index_groups=groups)  10.4 us
    all_to_all x2, waiting for transfers between devices, swap(): lax.all_to_all(array, axis, 0, 0, tiled=True, axis_index_groups=groups)  6.15 us
    pallas_call x1, Pallas kernels, attend(): pl.pallas_call(attend_kernel, out_shape=(jax.ShapeDtypeStruct((32, 40, 12...  3.81 us
    ppermute x4, waiting for transfers between devices, shift(): lax.ppermute(array, 'seq', [(s, (s + 8 * k) % 32) for s in range(32)])  2.49 us
  transfers between devices with their start and end apart: 6, of which 4 were waited for; matrix products, arithmetic and copies ran while one was open for 0% of the time, Pallas kernels for 2%

profile of v9, /device:TPU:1, one launch (start us, length us, event | category | flops | bytes accessed | tf_op | source)
XLA Modules:
  0.0 62.3 jit_solution(632229572207222602)
XLA Ops:
  0.6 3.8 %shard_map.95 = (bf16[32,40,128]{2,1,0:T(8,128)(2,1)}, f32[6,8,128]{2,1,0:T(8,128)}) custom-call(bf16[2,2,8,32,128]{4,3,2,1,0:T(8,128)(2,1)} %q_hbm.1, bf16[2,1024,128]{2,1,0:T(8,128)(2,1)} %k_hbm.1, bf16[2,1024,128]{2,1,0:T(8,128)(2,1)} %v_hbm.1, s32[2,32]{1,0:T(2,128)} %ids_hbm.1, bf16[2,2,32,128]{3,2,1,0:T(8,128)(2,1)} %tk_hbm.1, ...), custom_call_target="tpu_custom_call" | custom-call | tf_op jit(solution)/shard_map/pallas_call | solution.py:205
  4.4 0.0 copy-start
  4.5 0.0 copy-start.1
  4.5 10.6 %all-to-all-start = ((bf16[32,40,128]{2,1,0:T(8,128)(2,1)}), bf16[32,40,128]{2,1,0:T(8,128)(2,1)S(1)}, u32[]{:S(2)}, u32[]{:S(2)}) async-start(bf16[32,40,128]{2,1,0:T(8,128)(2,1)} %get-tuple-element.6), calls=%async_computation | async-start | bytes 655360 | tf_op jit(solution)/shard_map/all_to_all | solution.py:199
  15.0 0.0 copy-done
  15.0 3.3 %collective-permute-start = (bf16[256,512]{1,0:T(8,128)(2,1)S(1)}, bf16[256,512]{1,0:T(8,128)(2,1)S(1)}, u32[]{:S(2)}, u32[]{:S(2)}) collective-permute-start(bf16[256,512]{1,0:T(8,128)(2,1)S(1)} %copy-done), channel_id=1, source_target_pairs={{0,128},{16,144},{32,160},{48,176},{64,192},{80,208},{96,224},{112... | collective-permute-start | bytes 786440 | tf_op jit(solution)/shard_map/ppermute | solution.py:233
  18.4 3.2 %collective-permute-start.1 = (bf16[256,512]{1,0:T(8,128)(2,1)S(1)}, bf16[256,512]{1,0:T(8,128)(2,1)S(1)}, u32[]{:S(2)}, u32[]{:S(2)}) collective-permute-start(bf16[256,512]{1,0:T(8,128)(2,1)S(1)} %copy-done), channel_id=1, source_target_pairs={{0,384},{16,400},{32,416},{48,432},{64,448},{80,464},{96,480},{112... | collective-permute-start | bytes 786440 | tf_op jit(solution)/shard_map/ppermute | solution.py:233
  21.6 3.1 %all-to-all-done.got_ref = bf16[32,40,128]{2,1,0:T(8,128)(2,1)S(1)} async-done(((bf16[32,40,128]{2,1,0:T(8,128)(2,1)}), bf16[32,40,128]{2,1,0:T(8,128)(2,1)S(1)}, u32[]{:S(2)}, u32[]{:S(2)}) %all-to-all-start) | async-done | bytes 327712 | tf_op jit(solution)/shard_map/all_to_all | solution.py:199
  24.7 0.0 copy-done.1
  24.7 1.1 %shard_map.96 = bf16[16,32,128]{2,1,0:T(8,128)(2,1)} custom-call(bf16[32,40,128]{2,1,0:T(8,128)(2,1)S(1)} %all-to-all-done.got_ref, f32[6,8,128]{2,1,0:T(8,128)S(1)} %copy-done.1), custom_call_target="tpu_custom_call" | custom-call | tf_op jit(solution)/shard_map/pallas_call | solution.py:244
  25.8 13.0 %all-to-all-start.1 = ((bf16[16,32,128]{2,1,0:T(8,128)(2,1)}), bf16[16,32,128]{2,1,0:T(8,128)(2,1)S(1)}, u32[]{:S(2)}, u32[]{:S(2)}) async-start(bf16[16,32,128]{2,1,0:T(8,128)(2,1)} %shard_map.96), calls=%async_computation.1 | async-start | bytes 262144 | tf_op jit(solution)/shard_map/all_to_all | solution.py:199
  38.8 0.0 collective-permute-done.one_ref
  38.8 0.0 collective-permute-done.1.three_ref
  38.8 2.4 %collective-permute-start.2 = (bf16[128,512]{1,0:T(8,128)(2,1)S(1)}, bf16[128,512]{1,0:T(8,128)(2,1)S(1)}, u32[]{:S(2)}, u32[]{:S(2)}) collective-permute-start(bf16[128,512]{1,0:T(8,128)(2,1)S(1)} %get-tuple-element.8), channel_id=1, source_target_pairs={{0,128},{16,144},{32,160},{48,176},{64,192},{80,208},{96,224},{112... | collective-permute-start | bytes 393224 | tf_op jit(solution)/shard_map/ppermute | solution.py:233
  41.2 4.1 %collective-permute-start.3 = (bf16[128,512]{1,0:T(8,128)(2,1)S(1)}, bf16[128,512]{1,0:T(8,128)(2,1)S(1)}, u32[]{:S(2)}, u32[]{:S(2)}) collective-permute-start(bf16[128,512]{1,0:T(8,128)(2,1)S(1)} %get-tuple-element.9), channel_id=1, source_target_pairs={{0,384},{16,400},{32,416},{48,432},{64,448},{80,464},{96,480},{112... | collective-permute-start | bytes 393224 | tf_op jit(solution)/shard_map/ppermute | solution.py:233
  45.4 1.1 %collective-permute-done.2.low_ref = bf16[128,512]{1,0:T(8,128)(2,1)S(1)} collective-permute-done((bf16[128,512]{1,0:T(8,128)(2,1)S(1)}, bf16[128,512]{1,0:T(8,128)(2,1)S(1)}, u32[]{:S(2)}, u32[]{:S(2)}) %collective-permute-start.2) | collective-permute-done | bytes 131104 | tf_op jit(solution)/shard_map/ppermute | solution.py:233
  46.4 1.4 %collective-permute-done.3.high_ref = bf16[128,512]{1,0:T(8,128)(2,1)S(1)} collective-permute-done((bf16[128,512]{1,0:T(8,128)(2,1)S(1)}, bf16[128,512]{1,0:T(8,128)(2,1)S(1)}, u32[]{:S(2)}, u32[]{:S(2)}) %collective-permute-start.3) | collective-permute-done | bytes 131104 | tf_op jit(solution)/shard_map/ppermute | solution.py:233
  47.8 3.1 %all-to-all-done.1.x_ref = bf16[16,32,128]{2,1,0:T(8,128)(2,1)S(1)} async-done(((bf16[16,32,128]{2,1,0:T(8,128)(2,1)}), bf16[16,32,128]{2,1,0:T(8,128)(2,1)S(1)}, u32[]{:S(2)}, u32[]{:S(2)}) %all-to-all-start.1) | async-done | bytes 131104 | tf_op jit(solution)/shard_map/all_to_all | solution.py:199
  50.9 0.3 shard_map.98
  51.3 10.4 %all_to_all.15.got_ref = bf16[8,8,512]{2,1,0:T(8,128)(2,1)S(1)} all-to-all(bf16[8,8,512]{2,1,0:T(8,128)(2,1)S(1)} %shard_map.98), channel_id=1, replica_groups={{0,16,32,48,64,80,96,112},{128,144,160,176,192,208,224,240},{256,272,28..., dimensions={0} | all-to-all | bytes 131072 | tf_op jit(solution)/shard_map/all_to_all | solution.py:199
  61.7 0.6 shard_map.99
  (1 shorter events, 0.0 us)
Async XLA Ops:
  4.4 10.6 %copy-start = (bf16[256,512]{1,0:T(8,128)(2,1)S(1)}, bf16[256,512]{1,0:T(8,128)(2,1)}, u32[]{:S(2)}) copy-start(bf16[256,512]{1,0:T(8,128)(2,1)} %own_ref.1) | copy-start | bytes 786436
  4.5 20.2 %copy-start.1 = (f32[6,8,128]{2,1,0:T(8,128)S(1)}, f32[6,8,128]{2,1,0:T(8,128)}, u32[]{:S(2)}) copy-start(f32[6,8,128]{2,1,0:T(8,128)} %get-tuple-element.7.tree_ref) | copy-start | bytes 73732
  4.5 20.2 %all-to-all-start = ((bf16[32,40,128]{2,1,0:T(8,128)(2,1)}), bf16[32,40,128]{2,1,0:T(8,128)(2,1)S(1)}, u32[]{:S(2)}, u32[]{:S(2)}) async-start(bf16[32,40,128]{2,1,0:T(8,128)(2,1)} %get-tuple-element.6), calls=%async_computation | async-start | bytes 655360 | tf_op jit(solution)/shard_map/all_to_all | solution.py:199
  15.0 23.8 %collective-permute-start = (bf16[256,512]{1,0:T(8,128)(2,1)S(1)}, bf16[256,512]{1,0:T(8,128)(2,1)S(1)}, u32[]{:S(2)}, u32[]{:S(2)}) collective-permute-start(bf16[256,512]{1,0:T(8,128)(2,1)S(1)} %copy-done), channel_id=1, source_target_pairs={{0,128},{16,144},{32,160},{48,176},{64,192},{80,208},{96,224},{112... | collective-permute-start | bytes 786440 | tf_op jit(solution)/shard_map/ppermute | solution.py:233
  18.4 20.4 %collective-permute-start.1 = (bf16[256,512]{1,0:T(8,128)(2,1)S(1)}, bf16[256,512]{1,0:T(8,128)(2,1)S(1)}, u32[]{:S(2)}, u32[]{:S(2)}) collective-permute-start(bf16[256,512]{1,0:T(8,128)(2,1)S(1)} %copy-done), channel_id=1, source_target_pairs={{0,384},{16,400},{32,416},{48,432},{64,448},{80,464},{96,480},{112... | collective-permute-start | bytes 786440 | tf_op jit(solution)/shard_map/ppermute | solution.py:233
  25.8 25.1 %all-to-all-start.1 = ((bf16[16,32,128]{2,1,0:T(8,128)(2,1)}), bf16[16,32,128]{2,1,0:T(8,128)(2,1)S(1)}, u32[]{:S(2)}, u32[]{:S(2)}) async-start(bf16[16,32,128]{2,1,0:T(8,128)(2,1)} %shard_map.96), calls=%async_computation.1 | async-start | bytes 262144 | tf_op jit(solution)/shard_map/all_to_all | solution.py:199
  38.8 7.6 %collective-permute-start.2 = (bf16[128,512]{1,0:T(8,128)(2,1)S(1)}, bf16[128,512]{1,0:T(8,128)(2,1)S(1)}, u32[]{:S(2)}, u32[]{:S(2)}) collective-permute-start(bf16[128,512]{1,0:T(8,128)(2,1)S(1)} %get-tuple-element.8), channel_id=1, source_target_pairs={{0,128},{16,144},{32,160},{48,176},{64,192},{80,208},{96,224},{112... | collective-permute-start | bytes 393224 | tf_op jit(solution)/shard_map/ppermute | solution.py:233
  41.2 6.6 %collective-permute-start.3 = (bf16[128,512]{1,0:T(8,128)(2,1)S(1)}, bf16[128,512]{1,0:T(8,128)(2,1)S(1)}, u32[]{:S(2)}, u32[]{:S(2)}) collective-permute-start(bf16[128,512]{1,0:T(8,128)(2,1)S(1)} %get-tuple-element.9), channel_id=1, source_target_pairs={{0,384},{16,400},{32,416},{48,432},{64,448},{80,464},{96,480},{112... | collective-permute-start | bytes 393224 | tf_op jit(solution)/shard_map/ppermute | solution.py:233

commit v10 on v9

--- a/solution.py
+++ b/solution.py
@@ -11,6 +11,7 @@
 NEG = -(2.0**100)
 F32 = jnp.float32
 BF16 = jnp.bfloat16
+Z_GROUPS = [[k // 2 + (k % 2) * 8 for k in range(16)]]
 XC_GROUPS = [[y * 8 + k for k in range(8)] for y in range(4)]
 NT = (((1,), (1,)), ((), ()))
 VMEM = pl.BlockSpec(memory_space=pltpu.VMEM)
@@ -85,13 +86,12 @@
         tree_ref[4] = peak
         tree_ref[5] = jnp.where(part == 2, total, 0.0)
 
-    for move in moves[:4]:
-        move.wait()
-    for p in range(2):
-        if p == 1:
-            for move in moves[4:]:
-                move.wait()
-        keys = k_ref[p]
+
+    def scores(p):
+        q = q_ref[:, p].reshape(512, 128)
+        return lax.dot_general(q, k_ref[p], NT, preferred_element_type=F32)
+
+    def softmax(raw, p):
         ids = ids_ref[p : p + 1, :]
         bias = []
         for b in range(8):
@@ -99,16 +99,26 @@
             bias.append(jnp.broadcast_to(jnp.where(hit > 0.5, 0.0, NEG), (1, BLOCK)))
         bias = jnp.concatenate(bias, axis=1)
         peaks, weights = [], []
-        for a in range(2):
-            q = q_ref[a, p].reshape(256, 128)
-            t = lax.dot_general(q, keys, NT, preferred_element_type=F32) * SCALE
-            if a == 0:
+        for at in range(0, 512, 64):
+            t = raw[at : at + 64] * SCALE
+            if at < 256:
                 t = t + bias
             peak = jnp.max(t, axis=1, keepdims=True).astype(BF16).astype(F32)
+            peaks.append(peak)
             weights.append(jnp.exp2(t - peak).astype(BF16))
-            peaks.append(peak)
+        return jnp.concatenate(peaks, axis=0), jnp.concatenate(weights, axis=0)
+
+    def summed(w, p):
         values = jnp.concatenate([v_ref[p], jnp.ones((1024, 128), BF16)], axis=1)
-        sums = [jnp.dot(w, values, preferred_element_type=F32) for w in weights]
+        return jnp.dot(w, values, preferred_element_type=F32)
+
+    for move in moves:
+        move.wait()
+    raw = [scores(0), scores(1)]
+    for p in range(2):
+        peaks, w = softmax(raw[p], p)
+        sums = summed(w, p)
+        peaks, sums = [peaks[:256], peaks[256:]], [sums[:256], sums[256:]]
         if p == 1:
             tree_part()
         for y in range(4):
@@ -165,11 +175,15 @@
 def project_kernel(x_ref, own_ref, one_ref, three_ref, low_ref, high_ref, out_ref, turn_ref):
     y = lax.axis_index("seq") // 8
     total = jnp.zeros((64, 512), F32)
+
+    def place(r, j):
+        return ((r % 2) * 4 + j) * 2 + r // 2
+
     for k in range(4):
         j = (y + 4 - k) % 4
         left = [
             jnp.concatenate(
-                [x_ref[r * 4 + j, g2 * 16 : (g2 + 1) * 16, :] for r in range(4)], axis=0
+                [x_ref[place(r, j), g2 * 16 : (g2 + 1) * 16, :] for r in range(4)], axis=0
             )
             for g2 in range(2)
         ]
@@ -248,7 +262,7 @@
         out_specs=VMEM,
         compiler_params=PARAMS,
     )(got, tree)
-    gathered = swap(rows, "head")
+    gathered = swap(rows, "head", Z_GROUPS)
     low, high = pl.pallas_call(
         onward_kernel,
         out_shape=(jax.ShapeDtypeStruct((128, 512), BF16),) * 2,

time: 62.7 us -> 63.8 us (1.018)
  waiting for transfers between devices: 8.65 us -> 9.84 us
    all_to_all x2, waiting for transfers between devices: 6.15 us -> 7.35 us  [swap(): lax.all_to_all(array, axis, 0, 0, tiled=True, axis_index_groups=groups)]
where the time goes in v10:
time: 63.8 us; the launch traced here: 63.4 us
  starting transfers between devices  36.6 us (57%)
  blocking collectives  10.4 us (16%)
  waiting for transfers between devices  9.84 us (15%)
  Pallas kernels  5.75 us (9%)
  between operations  0.74 us (1%)
    all_to_all x2, starting transfers between devices, swap(): lax.all_to_all(array, axis, 0, 0, tiled=True, axis_index_groups=groups)  23.5 us
    ppermute x4, starting transfers between devices, shift(): lax.ppermute(array, 'seq', [(s, (s + 8 * k) % 32) for s in range(32)])  13.1 us
    all_to_all x1, blocking collectives, swap(): lax.all_to_all(array, axis, 0, 0, tiled=True, axis_index_groups=groups)  10.4 us
    all_to_all x2, waiting for transfers between devices, swap(): lax.all_to_all(array, axis, 0, 0, tiled=True, axis_index_groups=groups)  7.35 us
    pallas_call x1, Pallas kernels, attend(): pl.pallas_call(attend_kernel, out_shape=(jax.ShapeDtypeStruct((32, 40, 12...  3.7 us
    ppermute x4, waiting for transfers between devices, shift(): lax.ppermute(array, 'seq', [(s, (s + 8 * k) % 32) for s in range(32)])  2.49 us
  transfers between devices with their start and end apart: 6, of which 4 were waited for; matrix products, arithmetic and copies ran while one was open for 0% of the time, Pallas kernels for 2%

profile of v10, /device:TPU:1, one launch (start us, length us, event | category | flops | bytes accessed | tf_op | source)
XLA Modules:
  0.0 63.4 jit_solution(8669046509196112167)
XLA Ops:
  0.6 3.7 %shard_map.95 = (bf16[32,40,128]{2,1,0:T(8,128)(2,1)}, f32[6,8,128]{2,1,0:T(8,128)}) custom-call(bf16[2,2,8,32,128]{4,3,2,1,0:T(8,128)(2,1)} %q_hbm.1, bf16[2,1024,128]{2,1,0:T(8,128)(2,1)} %k_hbm.1, bf16[2,1024,128]{2,1,0:T(8,128)(2,1)} %v_hbm.1, s32[2,32]{1,0:T(2,128)} %ids_hbm.1, bf16[2,2,32,128]{3,2,1,0:T(8,128)(2,1)} %tk_hbm.1, ...), custom_call_target="tpu_custom_call" | custom-call | tf_op jit(solution)/shard_map/pallas_call | solution.py:219
  4.3 0.0 copy-start
  4.4 0.0 copy-start.1
  4.4 10.6 %all-to-all-start = ((bf16[32,40,128]{2,1,0:T(8,128)(2,1)}), bf16[32,40,128]{2,1,0:T(8,128)(2,1)S(1)}, u32[]{:S(2)}, u32[]{:S(2)}) async-start(bf16[32,40,128]{2,1,0:T(8,128)(2,1)} %get-tuple-element.6), calls=%async_computation | async-start | bytes 655360 | tf_op jit(solution)/shard_map/all_to_all | solution.py:213
  14.9 0.0 copy-done
  14.9 3.3 %collective-permute-start = (bf16[256,512]{1,0:T(8,128)(2,1)S(1)}, bf16[256,512]{1,0:T(8,128)(2,1)S(1)}, u32[]{:S(2)}, u32[]{:S(2)}) collective-permute-start(bf16[256,512]{1,0:T(8,128)(2,1)S(1)} %copy-done), channel_id=1, source_target_pairs={{0,128},{16,144},{32,160},{48,176},{64,192},{80,208},{96,224},{112... | collective-permute-start | bytes 786440 | tf_op jit(solution)/shard_map/ppermute | solution.py:247
  18.3 3.2 %collective-permute-start.1 = (bf16[256,512]{1,0:T(8,128)(2,1)S(1)}, bf16[256,512]{1,0:T(8,128)(2,1)S(1)}, u32[]{:S(2)}, u32[]{:S(2)}) collective-permute-start(bf16[256,512]{1,0:T(8,128)(2,1)S(1)} %copy-done), channel_id=1, source_target_pairs={{0,384},{16,400},{32,416},{48,432},{64,448},{80,464},{96,480},{112... | collective-permute-start | bytes 786440 | tf_op jit(solution)/shard_map/ppermute | solution.py:247
  21.5 3.1 %all-to-all-done.got_ref = bf16[32,40,128]{2,1,0:T(8,128)(2,1)S(1)} async-done(((bf16[32,40,128]{2,1,0:T(8,128)(2,1)}), bf16[32,40,128]{2,1,0:T(8,128)(2,1)S(1)}, u32[]{:S(2)}, u32[]{:S(2)}) %all-to-all-start) | async-done | bytes 327712 | tf_op jit(solution)/shard_map/all_to_all | solution.py:213
  24.6 0.0 copy-done.1
  24.6 1.1 %shard_map.96 = bf16[16,32,128]{2,1,0:T(8,128)(2,1)} custom-call(bf16[32,40,128]{2,1,0:T(8,128)(2,1)S(1)} %all-to-all-done.got_ref, f32[6,8,128]{2,1,0:T(8,128)S(1)} %copy-done.1), custom_call_target="tpu_custom_call" | custom-call | tf_op jit(solution)/shard_map/pallas_call | solution.py:258
  25.7 13.0 %all-to-all-start.1 = ((bf16[16,32,128]{2,1,0:T(8,128)(2,1)}), bf16[16,32,128]{2,1,0:T(8,128)(2,1)S(1)}, u32[]{:S(2)}, u32[]{:S(2)}) async-start(bf16[16,32,128]{2,1,0:T(8,128)(2,1)} %shard_map.96), calls=%async_computation.1 | async-start | bytes 262144 | tf_op jit(solution)/shard_map/all_to_all | solution.py:213
  38.7 0.0 collective-permute-done.one_ref
  38.7 0.0 collective-permute-done.1.three_ref
  38.7 2.4 %collective-permute-start.2 = (bf16[128,512]{1,0:T(8,128)(2,1)S(1)}, bf16[128,512]{1,0:T(8,128)(2,1)S(1)}, u32[]{:S(2)}, u32[]{:S(2)}) collective-permute-start(bf16[128,512]{1,0:T(8,128)(2,1)S(1)} %get-tuple-element.8), channel_id=1, source_target_pairs={{0,128},{16,144},{32,160},{48,176},{64,192},{80,208},{96,224},{112... | collective-permute-start | bytes 393224 | tf_op jit(solution)/shard_map/ppermute | solution.py:247
  41.1 4.1 %collective-permute-start.3 = (bf16[128,512]{1,0:T(8,128)(2,1)S(1)}, bf16[128,512]{1,0:T(8,128)(2,1)S(1)}, u32[]{:S(2)}, u32[]{:S(2)}) collective-permute-start(bf16[128,512]{1,0:T(8,128)(2,1)S(1)} %get-tuple-element.9), channel_id=1, source_target_pairs={{0,384},{16,400},{32,416},{48,432},{64,448},{80,464},{96,480},{112... | collective-permute-start | bytes 393224 | tf_op jit(solution)/shard_map/ppermute | solution.py:247
  45.2 1.1 %collective-permute-done.2.low_ref = bf16[128,512]{1,0:T(8,128)(2,1)S(1)} collective-permute-done((bf16[128,512]{1,0:T(8,128)(2,1)S(1)}, bf16[128,512]{1,0:T(8,128)(2,1)S(1)}, u32[]{:S(2)}, u32[]{:S(2)}) %collective-permute-start.2) | collective-permute-done | bytes 131104 | tf_op jit(solution)/shard_map/ppermute | solution.py:247
  46.3 1.4 %collective-permute-done.3.high_ref = bf16[128,512]{1,0:T(8,128)(2,1)S(1)} collective-permute-done((bf16[128,512]{1,0:T(8,128)(2,1)S(1)}, bf16[128,512]{1,0:T(8,128)(2,1)S(1)}, u32[]{:S(2)}, u32[]{:S(2)}) %collective-permute-start.3) | collective-permute-done | bytes 131104 | tf_op jit(solution)/shard_map/ppermute | solution.py:247
  47.7 4.3 %all-to-all-done.1.x_ref = bf16[16,32,128]{2,1,0:T(8,128)(2,1)S(1)} async-done(((bf16[16,32,128]{2,1,0:T(8,128)(2,1)}), bf16[16,32,128]{2,1,0:T(8,128)(2,1)S(1)}, u32[]{:S(2)}, u32[]{:S(2)}) %all-to-all-start.1) | async-done | bytes 131104 | tf_op jit(solution)/shard_map/all_to_all | solution.py:213
  52.0 0.3 shard_map.98
  52.4 10.4 %all_to_all.15.got_ref = bf16[8,8,512]{2,1,0:T(8,128)(2,1)S(1)} all-to-all(bf16[8,8,512]{2,1,0:T(8,128)(2,1)S(1)} %shard_map.98), channel_id=1, replica_groups={{0,16,32,48,64,80,96,112},{128,144,160,176,192,208,224,240},{256,272,28..., dimensions={0} | all-to-all | bytes 131072 | tf_op jit(solution)/shard_map/all_to_all | solution.py:213
  62.8 0.6 shard_map.99
  (1 shorter events, 0.0 us)
Async XLA Ops:
  4.3 10.6 %copy-start = (bf16[256,512]{1,0:T(8,128)(2,1)S(1)}, bf16[256,512]{1,0:T(8,128)(2,1)}, u32[]{:S(2)}) copy-start(bf16[256,512]{1,0:T(8,128)(2,1)} %own_ref.1) | copy-start | bytes 786436
  4.4 20.2 %copy-start.1 = (f32[6,8,128]{2,1,0:T(8,128)S(1)}, f32[6,8,128]{2,1,0:T(8,128)}, u32[]{:S(2)}) copy-start(f32[6,8,128]{2,1,0:T(8,128)} %get-tuple-element.7.tree_ref) | copy-start | bytes 73732
  4.4 20.2 %all-to-all-start = ((bf16[32,40,128]{2,1,0:T(8,128)(2,1)}), bf16[32,40,128]{2,1,0:T(8,128)(2,1)S(1)}, u32[]{:S(2)}, u32[]{:S(2)}) async-start(bf16[32,40,128]{2,1,0:T(8,128)(2,1)} %get-tuple-element.6), calls=%async_computation | async-start | bytes 655360 | tf_op jit(solution)/shard_map/all_to_all | solution.py:213
  14.9 23.8 %collective-permute-start = (bf16[256,512]{1,0:T(8,128)(2,1)S(1)}, bf16[256,512]{1,0:T(8,128)(2,1)S(1)}, u32[]{:S(2)}, u32[]{:S(2)}) collective-permute-start(bf16[256,512]{1,0:T(8,128)(2,1)S(1)} %copy-done), channel_id=1, source_target_pairs={{0,128},{16,144},{32,160},{48,176},{64,192},{80,208},{96,224},{112... | collective-permute-start | bytes 786440 | tf_op jit(solution)/shard_map/ppermute | solution.py:247
  18.3 20.4 %collective-permute-start.1 = (bf16[256,512]{1,0:T(8,128)(2,1)S(1)}, bf16[256,512]{1,0:T(8,128)(2,1)S(1)}, u32[]{:S(2)}, u32[]{:S(2)}) collective-permute-start(bf16[256,512]{1,0:T(8,128)(2,1)S(1)} %copy-done), channel_id=1, source_target_pairs={{0,384},{16,400},{32,416},{48,432},{64,448},{80,464},{96,480},{112... | collective-permute-start | bytes 786440 | tf_op jit(solution)/shard_map/ppermute | solution.py:247
  25.7 26.3 %all-to-all-start.1 = ((bf16[16,32,128]{2,1,0:T(8,128)(2,1)}), bf16[16,32,128]{2,1,0:T(8,128)(2,1)S(1)}, u32[]{:S(2)}, u32[]{:S(2)}) async-start(bf16[16,32,128]{2,1,0:T(8,128)(2,1)} %shard_map.96), calls=%async_computation.1 | async-start | bytes 262144 | tf_op jit(solution)/shard_map/all_to_all | solution.py:213
  38.7 7.6 %collective-permute-start.2 = (bf16[128,512]{1,0:T(8,128)(2,1)S(1)}, bf16[128,512]{1,0:T(8,128)(2,1)S(1)}, u32[]{:S(2)}, u32[]{:S(2)}) collective-permute-start(bf16[128,512]{1,0:T(8,128)(2,1)S(1)} %get-tuple-element.8), channel_id=1, source_target_pairs={{0,128},{16,144},{32,160},{48,176},{64,192},{80,208},{96,224},{112... | collective-permute-start | bytes 393224 | tf_op jit(solution)/shard_map/ppermute | solution.py:247
  41.1 6.6 %collective-permute-start.3 = (bf16[128,512]{1,0:T(8,128)(2,1)S(1)}, bf16[128,512]{1,0:T(8,128)(2,1)S(1)}, u32[]{:S(2)}, u32[]{:S(2)}) collective-permute-start(bf16[128,512]{1,0:T(8,128)(2,1)S(1)} %get-tuple-element.9), channel_id=1, source_target_pairs={{0,384},{16,400},{32,416},{48,432},{64,448},{80,464},{96,480},{112... | collective-permute-start | bytes 393224 | tf_op jit(solution)/shard_map/ppermute | solution.py:247

commit v11 on v10

--- a/solution.py
+++ b/solution.py
@@ -11,7 +11,7 @@
 NEG = -(2.0**100)
 F32 = jnp.float32
 BF16 = jnp.bfloat16
-Z_GROUPS = [[k // 2 + (k % 2) * 8 for k in range(16)]]
+Z_GROUPS = [[0, 1, 15, 2, 14, 3, 13, 4, 12, 5, 11, 6, 10, 7, 9, 8]]
 XC_GROUPS = [[y * 8 + k for k in range(8)] for y in range(4)]
 NT = (((1,), (1,)), ((), ()))
 VMEM = pl.BlockSpec(memory_space=pltpu.VMEM)
@@ -177,7 +177,8 @@
     total = jnp.zeros((64, 512), F32)
 
     def place(r, j):
-        return ((r % 2) * 4 + j) * 2 + r // 2
+        h = r * 4 + j
+        return jnp.where(h > 8, 32 - 2 * h, jnp.maximum(2 * h - 1, 0))
 
     for k in range(4):
         j = (y + 4 - k) % 4

time: 63.8 us -> 63.4 us (level)
  waiting for transfers between devices: 9.84 us -> 7.99 us
  blocking collectives: 10.4 us -> 11.8 us
    all_to_all x2, waiting for transfers between devices: 7.35 us -> 5.49 us  [swap(): lax.all_to_all(array, axis, 0, 0, tiled=True, axis_index_groups=groups)]
    all_to_all x1, blocking collectives: 10.4 us -> 11.8 us  [swap(): lax.all_to_all(array, axis, 0, 0, tiled=True, axis_index_groups=groups)]
where the time goes in v11:
time: 63.4 us; the launch traced here: 62.9 us
  starting transfers between devices  36.6 us (58%)
  blocking collectives  11.8 us (19%)
  waiting for transfers between devices  7.99 us (13%)
  Pallas kernels  5.75 us (9%)
  between operations  0.74 us (1%)
    all_to_all x2, starting transfers between devices, swap(): lax.all_to_all(array, axis, 0, 0, tiled=True, axis_index_groups=groups)  23.5 us
    ppermute x4, starting transfers between devices, shift(): lax.ppermute(array, 'seq', [(s, (s + 8 * k) % 32) for s in range(32)])  13.1 us
    all_to_all x1, blocking collectives, swap(): lax.all_to_all(array, axis, 0, 0, tiled=True, axis_index_groups=groups)  11.8 us
    all_to_all x2, waiting for transfers between devices, swap(): lax.all_to_all(array, axis, 0, 0, tiled=True, axis_index_groups=groups)  5.49 us
    pallas_call x1, Pallas kernels, attend(): pl.pallas_call(attend_kernel, out_shape=(jax.ShapeDtypeStruct((32, 40, 12...  3.7 us
    ppermute x4, waiting for transfers between devices, shift(): lax.ppermute(array, 'seq', [(s, (s + 8 * k) % 32) for s in range(32)])  2.49 us
  transfers between devices with their start and end apart: 6, of which 4 were waited for; matrix products, arithmetic and copies ran while one was open for 0% of the time, Pallas kernels for 2%

profile of v11, /device:TPU:1, one launch (start us, length us, event | category | flops | bytes accessed | tf_op | source)
XLA Modules:
  0.0 62.9 jit_solution(17726486284668554141)
XLA Ops:
  0.6 3.7 %shard_map.95 = (bf16[32,40,128]{2,1,0:T(8,128)(2,1)}, f32[6,8,128]{2,1,0:T(8,128)}) custom-call(bf16[2,2,8,32,128]{4,3,2,1,0:T(8,128)(2,1)} %q_hbm.1, bf16[2,1024,128]{2,1,0:T(8,128)(2,1)} %k_hbm.1, bf16[2,1024,128]{2,1,0:T(8,128)(2,1)} %v_hbm.1, s32[2,32]{1,0:T(2,128)} %ids_hbm.1, bf16[2,2,32,128]{3,2,1,0:T(8,128)(2,1)} %tk_hbm.1, ...), custom_call_target="tpu_custom_call" | custom-call | tf_op jit(solution)/shard_map/pallas_call | solution.py:220
  4.3 0.0 copy-start
  4.4 0.0 copy-start.1
  4.4 10.6 %all-to-all-start = ((bf16[32,40,128]{2,1,0:T(8,128)(2,1)}), bf16[32,40,128]{2,1,0:T(8,128)(2,1)S(1)}, u32[]{:S(2)}, u32[]{:S(2)}) async-start(bf16[32,40,128]{2,1,0:T(8,128)(2,1)} %get-tuple-element.6), calls=%async_computation | async-start | bytes 655360 | tf_op jit(solution)/shard_map/all_to_all | solution.py:214
  14.9 0.0 copy-done
  14.9 3.3 %collective-permute-start = (bf16[256,512]{1,0:T(8,128)(2,1)S(1)}, bf16[256,512]{1,0:T(8,128)(2,1)S(1)}, u32[]{:S(2)}, u32[]{:S(2)}) collective-permute-start(bf16[256,512]{1,0:T(8,128)(2,1)S(1)} %copy-done), channel_id=1, source_target_pairs={{0,128},{16,144},{32,160},{48,176},{64,192},{80,208},{96,224},{112... | collective-permute-start | bytes 786440 | tf_op jit(solution)/shard_map/ppermute | solution.py:248
  18.3 3.2 %collective-permute-start.1 = (bf16[256,512]{1,0:T(8,128)(2,1)S(1)}, bf16[256,512]{1,0:T(8,128)(2,1)S(1)}, u32[]{:S(2)}, u32[]{:S(2)}) collective-permute-start(bf16[256,512]{1,0:T(8,128)(2,1)S(1)} %copy-done), channel_id=1, source_target_pairs={{0,384},{16,400},{32,416},{48,432},{64,448},{80,464},{96,480},{112... | collective-permute-start | bytes 786440 | tf_op jit(solution)/shard_map/ppermute | solution.py:248
  21.5 3.1 %all-to-all-done.got_ref = bf16[32,40,128]{2,1,0:T(8,128)(2,1)S(1)} async-done(((bf16[32,40,128]{2,1,0:T(8,128)(2,1)}), bf16[32,40,128]{2,1,0:T(8,128)(2,1)S(1)}, u32[]{:S(2)}, u32[]{:S(2)}) %all-to-all-start) | async-done | bytes 327712 | tf_op jit(solution)/shard_map/all_to_all | solution.py:214
  24.6 0.0 copy-done.1
  24.6 1.1 %shard_map.96 = bf16[16,32,128]{2,1,0:T(8,128)(2,1)} custom-call(bf16[32,40,128]{2,1,0:T(8,128)(2,1)S(1)} %all-to-all-done.got_ref, f32[6,8,128]{2,1,0:T(8,128)S(1)} %copy-done.1), custom_call_target="tpu_custom_call" | custom-call | tf_op jit(solution)/shard_map/pallas_call | solution.py:259
  25.7 13.0 %all-to-all-start.1 = ((bf16[16,32,128]{2,1,0:T(8,128)(2,1)}), bf16[16,32,128]{2,1,0:T(8,128)(2,1)S(1)}, u32[]{:S(2)}, u32[]{:S(2)}) async-start(bf16[16,32,128]{2,1,0:T(8,128)(2,1)} %shard_map.96), calls=%async_computation.1 | async-start | bytes 262144 | tf_op jit(solution)/shard_map/all_to_all | solution.py:214
  38.7 0.0 collective-permute-done.one_ref
  38.7 0.0 collective-permute-done.1.three_ref
  38.7 2.4 %collective-permute-start.2 = (bf16[128,512]{1,0:T(8,128)(2,1)S(1)}, bf16[128,512]{1,0:T(8,128)(2,1)S(1)}, u32[]{:S(2)}, u32[]{:S(2)}) collective-permute-start(bf16[128,512]{1,0:T(8,128)(2,1)S(1)} %get-tuple-element.8), channel_id=1, source_target_pairs={{0,128},{16,144},{32,160},{48,176},{64,192},{80,208},{96,224},{112... | collective-permute-start | bytes 393224 | tf_op jit(solution)/shard_map/ppermute | solution.py:248
  41.1 4.1 %collective-permute-start.3 = (bf16[128,512]{1,0:T(8,128)(2,1)S(1)}, bf16[128,512]{1,0:T(8,128)(2,1)S(1)}, u32[]{:S(2)}, u32[]{:S(2)}) collective-permute-start(bf16[128,512]{1,0:T(8,128)(2,1)S(1)} %get-tuple-element.9), channel_id=1, source_target_pairs={{0,384},{16,400},{32,416},{48,432},{64,448},{80,464},{96,480},{112... | collective-permute-start | bytes 393224 | tf_op jit(solution)/shard_map/ppermute | solution.py:248
  45.2 1.1 %collective-permute-done.2.low_ref = bf16[128,512]{1,0:T(8,128)(2,1)S(1)} collective-permute-done((bf16[128,512]{1,0:T(8,128)(2,1)S(1)}, bf16[128,512]{1,0:T(8,128)(2,1)S(1)}, u32[]{:S(2)}, u32[]{:S(2)}) %collective-permute-start.2) | collective-permute-done | bytes 131104 | tf_op jit(solution)/shard_map/ppermute | solution.py:248
  46.3 1.4 %collective-permute-done.3.high_ref = bf16[128,512]{1,0:T(8,128)(2,1)S(1)} collective-permute-done((bf16[128,512]{1,0:T(8,128)(2,1)S(1)}, bf16[128,512]{1,0:T(8,128)(2,1)S(1)}, u32[]{:S(2)}, u32[]{:S(2)}) %collective-permute-start.3) | collective-permute-done | bytes 131104 | tf_op jit(solution)/shard_map/ppermute | solution.py:248
  47.7 2.4 %all-to-all-done.1.x_ref = bf16[16,32,128]{2,1,0:T(8,128)(2,1)S(1)} async-done(((bf16[16,32,128]{2,1,0:T(8,128)(2,1)}), bf16[16,32,128]{2,1,0:T(8,128)(2,1)S(1)}, u32[]{:S(2)}, u32[]{:S(2)}) %all-to-all-start.1) | async-done | bytes 131104 | tf_op jit(solution)/shard_map/all_to_all | solution.py:214
  50.2 0.3 shard_map.98
  50.5 11.8 %all_to_all.15.got_ref = bf16[8,8,512]{2,1,0:T(8,128)(2,1)S(1)} all-to-all(bf16[8,8,512]{2,1,0:T(8,128)(2,1)S(1)} %shard_map.98), channel_id=1, replica_groups={{0,16,32,48,64,80,96,112},{128,144,160,176,192,208,224,240},{256,272,28..., dimensions={0} | all-to-all | bytes 131072 | tf_op jit(solution)/shard_map/all_to_all | solution.py:214
  62.3 0.6 shard_map.99
  (1 shorter events, 0.0 us)
Async XLA Ops:
  4.3 10.6 %copy-start = (bf16[256,512]{1,0:T(8,128)(2,1)S(1)}, bf16[256,512]{1,0:T(8,128)(2,1)}, u32[]{:S(2)}) copy-start(bf16[256,512]{1,0:T(8,128)(2,1)} %own_ref.1) | copy-start | bytes 786436
  4.4 20.2 %copy-start.1 = (f32[6,8,128]{2,1,0:T(8,128)S(1)}, f32[6,8,128]{2,1,0:T(8,128)}, u32[]{:S(2)}) copy-start(f32[6,8,128]{2,1,0:T(8,128)} %get-tuple-element.7.tree_ref) | copy-start | bytes 73732
  4.4 20.2 %all-to-all-start = ((bf16[32,40,128]{2,1,0:T(8,128)(2,1)}), bf16[32,40,128]{2,1,0:T(8,128)(2,1)S(1)}, u32[]{:S(2)}, u32[]{:S(2)}) async-start(bf16[32,40,128]{2,1,0:T(8,128)(2,1)} %get-tuple-element.6), calls=%async_computation | async-start | bytes 655360 | tf_op jit(solution)/shard_map/all_to_all | solution.py:214
  14.9 23.8 %collective-permute-start = (bf16[256,512]{1,0:T(8,128)(2,1)S(1)}, bf16[256,512]{1,0:T(8,128)(2,1)S(1)}, u32[]{:S(2)}, u32[]{:S(2)}) collective-permute-start(bf16[256,512]{1,0:T(8,128)(2,1)S(1)} %copy-done), channel_id=1, source_target_pairs={{0,128},{16,144},{32,160},{48,176},{64,192},{80,208},{96,224},{112... | collective-permute-start | bytes 786440 | tf_op jit(solution)/shard_map/ppermute | solution.py:248
  18.3 20.4 %collective-permute-start.1 = (bf16[256,512]{1,0:T(8,128)(2,1)S(1)}, bf16[256,512]{1,0:T(8,128)(2,1)S(1)}, u32[]{:S(2)}, u32[]{:S(2)}) collective-permute-start(bf16[256,512]{1,0:T(8,128)(2,1)S(1)} %copy-done), channel_id=1, source_target_pairs={{0,384},{16,400},{32,416},{48,432},{64,448},{80,464},{96,480},{112... | collective-permute-start | bytes 786440 | tf_op jit(solution)/shard_map/ppermute | solution.py:248
  25.7 24.5 %all-to-all-start.1 = ((bf16[16,32,128]{2,1,0:T(8,128)(2,1)}), bf16[16,32,128]{2,1,0:T(8,128)(2,1)S(1)}, u32[]{:S(2)}, u32[]{:S(2)}) async-start(bf16[16,32,128]{2,1,0:T(8,128)(2,1)} %shard_map.96), calls=%async_computation.1 | async-start | bytes 262144 | tf_op jit(solution)/shard_map/all_to_all | solution.py:214
  38.7 7.6 %collective-permute-start.2 = (bf16[128,512]{1,0:T(8,128)(2,1)S(1)}, bf16[128,512]{1,0:T(8,128)(2,1)S(1)}, u32[]{:S(2)}, u32[]{:S(2)}) collective-permute-start(bf16[128,512]{1,0:T(8,128)(2,1)S(1)} %get-tuple-element.8), channel_id=1, source_target_pairs={{0,128},{16,144},{32,160},{48,176},{64,192},{80,208},{96,224},{112... | collective-permute-start | bytes 393224 | tf_op jit(solution)/shard_map/ppermute | solution.py:248
  41.1 6.6 %collective-permute-start.3 = (bf16[128,512]{1,0:T(8,128)(2,1)S(1)}, bf16[128,512]{1,0:T(8,128)(2,1)S(1)}, u32[]{:S(2)}, u32[]{:S(2)}) collective-permute-start(bf16[128,512]{1,0:T(8,128)(2,1)S(1)} %get-tuple-element.9), channel_id=1, source_target_pairs={{0,384},{16,400},{32,416},{48,432},{64,448},{80,464},{96,480},{112... | collective-permute-start | bytes 393224 | tf_op jit(solution)/shard_map/ppermute | solution.py:248

commit v12 on v10

--- a/solution.py
+++ b/solution.py
@@ -11,7 +11,7 @@
 NEG = -(2.0**100)
 F32 = jnp.float32
 BF16 = jnp.bfloat16
-Z_GROUPS = [[k // 2 + (k % 2) * 8 for k in range(16)]]
+Z_GROUPS = [[s * 16 + (7 + s % 2 * 2) * k % 16 for k in range(16)] for s in range(32)]
 XC_GROUPS = [[y * 8 + k for k in range(8)] for y in range(4)]
 NT = (((1,), (1,)), ((), ()))
 VMEM = pl.BlockSpec(memory_space=pltpu.VMEM)
@@ -173,11 +173,12 @@
 
 
 def project_kernel(x_ref, own_ref, one_ref, three_ref, low_ref, high_ref, out_ref, turn_ref):
-    y = lax.axis_index("seq") // 8
+    seq = lax.axis_index("seq")
+    y = seq // 8
     total = jnp.zeros((64, 512), F32)
 
     def place(r, j):
-        return ((r % 2) * 4 + j) * 2 + r // 2
+        return (7 + seq % 2 * 2) * (r * 4 + j) % 16
 
     for k in range(4):
         j = (y + 4 - k) % 4
@@ -262,7 +263,7 @@
         out_specs=VMEM,
         compiler_params=PARAMS,
     )(got, tree)
-    gathered = swap(rows, "head", Z_GROUPS)
+    gathered = swap(rows, ("seq", "head"), Z_GROUPS)
     low, high = pl.pallas_call(
         onward_kernel,
         out_shape=(jax.ShapeDtypeStruct((128, 512), BF16),) * 2,

time: 63.8 us -> 62.4 us (0.978)
  the two profiles are of different devices: /device:TPU:1 before, /device:TPU:32 now
where the time goes in v12:
time: 62.4 us; the launch traced here: 62 us
  starting transfers between devices  36.8 us (59%)
  waiting for transfers between devices  10.7 us (17%)
  blocking collectives  8.04 us (13%)
  Pallas kernels  5.76 us (9%)
  between operations  0.73 us (1%)
    all_to_all x2, starting transfers between devices, swap(): lax.all_to_all(array, axis, 0, 0, tiled=True, axis_index_groups=groups)  22.7 us
    ppermute x4, starting transfers between devices, shift(): lax.ppermute(array, 'seq', [(s, (s + 8 * k) % 32) for s in range(32)])  14.1 us
    all_to_all x2, waiting for transfers between devices, swap(): lax.all_to_all(array, axis, 0, 0, tiled=True, axis_index_groups=groups)  8.16 us
    all_to_all x1, blocking collectives, swap(): lax.all_to_all(array, axis, 0, 0, tiled=True, axis_index_groups=groups)  8.04 us
    pallas_call x1, Pallas kernels, attend(): pl.pallas_call(attend_kernel, out_shape=(jax.ShapeDtypeStruct((32, 40, 12...  3.7 us
    ppermute x4, waiting for transfers between devices, shift(): lax.ppermute(array, 'seq', [(s, (s + 8 * k) % 32) for s in range(32)])  2.5 us
  transfers between devices with their start and end apart: 6, of which 4 were waited for; matrix products, arithmetic and copies ran while one was open for 0% of the time, Pallas kernels for 2%

profile of v12, /device:TPU:32, one launch (start us, length us, event | category | flops | bytes accessed | tf_op | source)
XLA Modules:
  0.0 62.0 jit_solution(7618660721337371350)
XLA Ops:
  0.6 3.7 %shard_map.95 = (bf16[32,40,128]{2,1,0:T(8,128)(2,1)}, f32[6,8,128]{2,1,0:T(8,128)}) custom-call(bf16[2,2,8,32,128]{4,3,2,1,0:T(8,128)(2,1)} %q_hbm.1, bf16[2,1024,128]{2,1,0:T(8,128)(2,1)} %k_hbm.1, bf16[2,1024,128]{2,1,0:T(8,128)(2,1)} %v_hbm.1, s32[2,32]{1,0:T(2,128)} %ids_hbm.1, bf16[2,2,32,128]{3,2,1,0:T(8,128)(2,1)} %tk_hbm.1, ...), custom_call_target="tpu_custom_call" | custom-call | tf_op jit(solution)/shard_map/pallas_call | solution.py:220
  4.3 0.0 copy-start
  4.4 0.0 copy-start.1
  4.4 7.5 %all-to-all-start = ((bf16[32,40,128]{2,1,0:T(8,128)(2,1)}), bf16[32,40,128]{2,1,0:T(8,128)(2,1)S(1)}, u32[]{:S(2)}, u32[]{:S(2)}) async-start(bf16[32,40,128]{2,1,0:T(8,128)(2,1)} %get-tuple-element.6), calls=%async_computation | async-start | bytes 655360 | tf_op jit(solution)/shard_map/all_to_all | solution.py:214
  11.8 0.0 copy-done
  11.9 3.7 %collective-permute-start = (bf16[256,512]{1,0:T(8,128)(2,1)S(1)}, bf16[256,512]{1,0:T(8,128)(2,1)S(1)}, u32[]{:S(2)}, u32[]{:S(2)}) collective-permute-start(bf16[256,512]{1,0:T(8,128)(2,1)S(1)} %copy-done), channel_id=1, source_target_pairs={{0,128},{16,144},{32,160},{48,176},{64,192},{80,208},{96,224},{112... | collective-permute-start | bytes 786440 | tf_op jit(solution)/shard_map/ppermute | solution.py:248
  15.6 3.4 %collective-permute-start.1 = (bf16[256,512]{1,0:T(8,128)(2,1)S(1)}, bf16[256,512]{1,0:T(8,128)(2,1)S(1)}, u32[]{:S(2)}, u32[]{:S(2)}) collective-permute-start(bf16[256,512]{1,0:T(8,128)(2,1)S(1)} %copy-done), channel_id=1, source_target_pairs={{0,384},{16,400},{32,416},{48,432},{64,448},{80,464},{96,480},{112... | collective-permute-start | bytes 786440 | tf_op jit(solution)/shard_map/ppermute | solution.py:248
  18.9 2.5 %all-to-all-done.got_ref = bf16[32,40,128]{2,1,0:T(8,128)(2,1)S(1)} async-done(((bf16[32,40,128]{2,1,0:T(8,128)(2,1)}), bf16[32,40,128]{2,1,0:T(8,128)(2,1)S(1)}, u32[]{:S(2)}, u32[]{:S(2)}) %all-to-all-start) | async-done | bytes 327712 | tf_op jit(solution)/shard_map/all_to_all | solution.py:214
  21.5 0.0 copy-done.1
  21.5 1.1 %shard_map.96 = bf16[16,32,128]{2,1,0:T(8,128)(2,1)} custom-call(bf16[32,40,128]{2,1,0:T(8,128)(2,1)S(1)} %all-to-all-done.got_ref, f32[6,8,128]{2,1,0:T(8,128)S(1)} %copy-done.1), custom_call_target="tpu_custom_call" | custom-call | tf_op jit(solution)/shard_map/pallas_call | solution.py:259
  22.6 15.2 %all-to-all-start.1 = ((bf16[16,32,128]{2,1,0:T(8,128)(2,1)}), bf16[16,32,128]{2,1,0:T(8,128)(2,1)S(1)}, u32[]{:S(2)}, u32[]{:S(2)}) async-start(bf16[16,32,128]{2,1,0:T(8,128)(2,1)} %shard_map.96), calls=%async_computation.1 | async-start | bytes 262144 | tf_op jit(solution)/shard_map/all_to_all | solution.py:214
  37.8 0.0 collective-permute-done.one_ref
  37.8 0.0 collective-permute-done.1.three_ref
  37.8 2.2 %collective-permute-start.2 = (bf16[128,512]{1,0:T(8,128)(2,1)S(1)}, bf16[128,512]{1,0:T(8,128)(2,1)S(1)}, u32[]{:S(2)}, u32[]{:S(2)}) collective-permute-start(bf16[128,512]{1,0:T(8,128)(2,1)S(1)} %get-tuple-element.8), channel_id=1, source_target_pairs={{0,128},{16,144},{32,160},{48,176},{64,192},{80,208},{96,224},{112... | collective-permute-start | bytes 393224 | tf_op jit(solution)/shard_map/ppermute | solution.py:248
  40.0 4.9 %collective-permute-start.3 = (bf16[128,512]{1,0:T(8,128)(2,1)S(1)}, bf16[128,512]{1,0:T(8,128)(2,1)S(1)}, u32[]{:S(2)}, u32[]{:S(2)}) collective-permute-start(bf16[128,512]{1,0:T(8,128)(2,1)S(1)} %get-tuple-element.9), channel_id=1, source_target_pairs={{0,384},{16,400},{32,416},{48,432},{64,448},{80,464},{96,480},{112... | collective-permute-start | bytes 393224 | tf_op jit(solution)/shard_map/ppermute | solution.py:248
  44.9 1.1 %collective-permute-done.2.low_ref = bf16[128,512]{1,0:T(8,128)(2,1)S(1)} collective-permute-done((bf16[128,512]{1,0:T(8,128)(2,1)S(1)}, bf16[128,512]{1,0:T(8,128)(2,1)S(1)}, u32[]{:S(2)}, u32[]{:S(2)}) %collective-permute-start.2) | collective-permute-done | bytes 131104 | tf_op jit(solution)/shard_map/ppermute | solution.py:248
  46.0 1.4 %collective-permute-done.3.high_ref = bf16[128,512]{1,0:T(8,128)(2,1)S(1)} collective-permute-done((bf16[128,512]{1,0:T(8,128)(2,1)S(1)}, bf16[128,512]{1,0:T(8,128)(2,1)S(1)}, u32[]{:S(2)}, u32[]{:S(2)}) %collective-permute-start.3) | collective-permute-done | bytes 131104 | tf_op jit(solution)/shard_map/ppermute | solution.py:248
  47.4 5.6 %all-to-all-done.1.x_ref = bf16[16,32,128]{2,1,0:T(8,128)(2,1)S(1)} async-done(((bf16[16,32,128]{2,1,0:T(8,128)(2,1)}), bf16[16,32,128]{2,1,0:T(8,128)(2,1)S(1)}, u32[]{:S(2)}, u32[]{:S(2)}) %all-to-all-start.1) | async-done | bytes 131104 | tf_op jit(solution)/shard_map/all_to_all | solution.py:214
  53.0 0.3 shard_map.98
  53.3 8.0 %all_to_all.15.got_ref = bf16[8,8,512]{2,1,0:T(8,128)(2,1)S(1)} all-to-all(bf16[8,8,512]{2,1,0:T(8,128)(2,1)S(1)} %shard_map.98), channel_id=1, replica_groups={{0,16,32,48,64,80,96,112},{128,144,160,176,192,208,224,240},{256,272,28..., dimensions={0} | all-to-all | bytes 131072 | tf_op jit(solution)/shard_map/all_to_all | solution.py:214
  61.4 0.6 shard_map.99
  (1 shorter events, 0.0 us)
Async XLA Ops:
  4.3 7.5 %copy-start = (bf16[256,512]{1,0:T(8,128)(2,1)S(1)}, bf16[256,512]{1,0:T(8,128)(2,1)}, u32[]{:S(2)}) copy-start(bf16[256,512]{1,0:T(8,128)(2,1)} %own_ref.1) | copy-start | bytes 786436
  4.4 17.1 %copy-start.1 = (f32[6,8,128]{2,1,0:T(8,128)S(1)}, f32[6,8,128]{2,1,0:T(8,128)}, u32[]{:S(2)}) copy-start(f32[6,8,128]{2,1,0:T(8,128)} %get-tuple-element.7.tree_ref) | copy-start | bytes 73732
  4.4 17.1 %all-to-all-start = ((bf16[32,40,128]{2,1,0:T(8,128)(2,1)}), bf16[32,40,128]{2,1,0:T(8,128)(2,1)S(1)}, u32[]{:S(2)}, u32[]{:S(2)}) async-start(bf16[32,40,128]{2,1,0:T(8,128)(2,1)} %get-tuple-element.6), calls=%async_computation | async-start | bytes 655360 | tf_op jit(solution)/shard_map/all_to_all | solution.py:214
  11.9 25.9 %collective-permute-start = (bf16[256,512]{1,0:T(8,128)(2,1)S(1)}, bf16[256,512]{1,0:T(8,128)(2,1)S(1)}, u32[]{:S(2)}, u32[]{:S(2)}) collective-permute-start(bf16[256,512]{1,0:T(8,128)(2,1)S(1)} %copy-done), channel_id=1, source_target_pairs={{0,128},{16,144},{32,160},{48,176},{64,192},{80,208},{96,224},{112... | collective-permute-start | bytes 786440 | tf_op jit(solution)/shard_map/ppermute | solution.py:248
  15.6 22.2 %collective-permute-start.1 = (bf16[256,512]{1,0:T(8,128)(2,1)S(1)}, bf16[256,512]{1,0:T(8,128)(2,1)S(1)}, u32[]{:S(2)}, u32[]{:S(2)}) collective-permute-start(bf16[256,512]{1,0:T(8,128)(2,1)S(1)} %copy-done), channel_id=1, source_target_pairs={{0,384},{16,400},{32,416},{48,432},{64,448},{80,464},{96,480},{112... | collective-permute-start | bytes 786440 | tf_op jit(solution)/shard_map/ppermute | solution.py:248
  22.6 30.4 %all-to-all-start.1 = ((bf16[16,32,128]{2,1,0:T(8,128)(2,1)}), bf16[16,32,128]{2,1,0:T(8,128)(2,1)S(1)}, u32[]{:S(2)}, u32[]{:S(2)}) async-start(bf16[16,32,128]{2,1,0:T(8,128)(2,1)} %shard_map.96), calls=%async_computation.1 | async-start | bytes 262144 | tf_op jit(solution)/shard_map/all_to_all | solution.py:214
  37.8 8.2 %collective-permute-start.2 = (bf16[128,512]{1,0:T(8,128)(2,1)S(1)}, bf16[128,512]{1,0:T(8,128)(2,1)S(1)}, u32[]{:S(2)}, u32[]{:S(2)}) collective-permute-start(bf16[128,512]{1,0:T(8,128)(2,1)S(1)} %get-tuple-element.8), channel_id=1, source_target_pairs={{0,128},{16,144},{32,160},{48,176},{64,192},{80,208},{96,224},{112... | collective-permute-start | bytes 393224 | tf_op jit(solution)/shard_map/ppermute | solution.py:248
  40.0 7.4 %collective-permute-start.3 = (bf16[128,512]{1,0:T(8,128)(2,1)S(1)}, bf16[128,512]{1,0:T(8,128)(2,1)S(1)}, u32[]{:S(2)}, u32[]{:S(2)}) collective-permute-start(bf16[128,512]{1,0:T(8,128)(2,1)S(1)} %get-tuple-element.9), channel_id=1, source_target_pairs={{0,384},{16,400},{32,416},{48,432},{64,448},{80,464},{96,480},{112... | collective-permute-start | bytes 393224 | tf_op jit(solution)/shard_map/ppermute | solution.py:248

commit v13 on v12

--- a/solution.py
+++ b/solution.py
@@ -11,7 +11,7 @@
 NEG = -(2.0**100)
 F32 = jnp.float32
 BF16 = jnp.bfloat16
-Z_GROUPS = [[s * 16 + (7 + s % 2 * 2) * k % 16 for k in range(16)] for s in range(32)]
+Z_GROUPS = [[s * 16 + (1 + s % 2 * 14) * k % 16 for k in range(16)] for s in range(32)]
 XC_GROUPS = [[y * 8 + k for k in range(8)] for y in range(4)]
 NT = (((1,), (1,)), ((), ()))
 VMEM = pl.BlockSpec(memory_space=pltpu.VMEM)
@@ -178,7 +178,7 @@
     total = jnp.zeros((64, 512), F32)
 
     def place(r, j):
-        return (7 + seq % 2 * 2) * (r * 4 + j) % 16
+        return (1 + seq % 2 * 14) * (r * 4 + j) % 16
 
     for k in range(4):
         j = (y + 4 - k) % 4

time: 62.4 us -> 62.5 us (level)
  the two profiles are of different devices: /device:TPU:32 before, /device:TPU:1 now
where the time goes in v13:
time: 62.5 us; the launch traced here: 62 us
  starting transfers between devices  36.6 us (59%)
  blocking collectives  11.1 us (18%)
  waiting for transfers between devices  7.84 us (13%)
  Pallas kernels  5.76 us (9%)
  between operations  0.74 us (1%)
    all_to_all x2, starting transfers between devices, swap(): lax.all_to_all(array, axis, 0, 0, tiled=True, axis_index_groups=groups)  23.5 us
    ppermute x4, starting transfers between devices, shift(): lax.ppermute(array, 'seq', [(s, (s + 8 * k) % 32) for s in range(32)])  13.1 us
    all_to_all x1, blocking collectives, swap(): lax.all_to_all(array, axis, 0, 0, tiled=True, axis_index_groups=groups)  11.1 us
    all_to_all x2, waiting for transfers between devices, swap(): lax.all_to_all(array, axis, 0, 0, tiled=True, axis_index_groups=groups)  5.35 us
    pallas_call x1, Pallas kernels, attend(): pl.pallas_call(attend_kernel, out_shape=(jax.ShapeDtypeStruct((32, 40, 12...  3.7 us
    ppermute x4, waiting for transfers between devices, shift(): lax.ppermute(array, 'seq', [(s, (s + 8 * k) % 32) for s in range(32)])  2.49 us
  transfers between devices with their start and end apart: 6, of which 4 were waited for; matrix products, arithmetic and copies ran while one was open for 0% of the time, Pallas kernels for 2%

profile of v13, /device:TPU:1, one launch (start us, length us, event | category | flops | bytes accessed | tf_op | source)
XLA Modules:
  0.0 62.0 jit_solution(9920700362600794795)
XLA Ops:
  0.6 3.7 %shard_map.95 = (bf16[32,40,128]{2,1,0:T(8,128)(2,1)}, f32[6,8,128]{2,1,0:T(8,128)}) custom-call(bf16[2,2,8,32,128]{4,3,2,1,0:T(8,128)(2,1)} %q_hbm.1, bf16[2,1024,128]{2,1,0:T(8,128)(2,1)} %k_hbm.1, bf16[2,1024,128]{2,1,0:T(8,128)(2,1)} %v_hbm.1, s32[2,32]{1,0:T(2,128)} %ids_hbm.1, bf16[2,2,32,128]{3,2,1,0:T(8,128)(2,1)} %tk_hbm.1, ...), custom_call_target="tpu_custom_call" | custom-call | tf_op jit(solution)/shard_map/pallas_call | solution.py:220
  4.3 0.0 copy-start
  4.4 0.0 copy-start.1
  4.4 10.6 %all-to-all-start = ((bf16[32,40,128]{2,1,0:T(8,128)(2,1)}), bf16[32,40,128]{2,1,0:T(8,128)(2,1)S(1)}, u32[]{:S(2)}, u32[]{:S(2)}) async-start(bf16[32,40,128]{2,1,0:T(8,128)(2,1)} %get-tuple-element.6), calls=%async_computation | async-start | bytes 655360 | tf_op jit(solution)/shard_map/all_to_all | solution.py:214
  14.9 0.0 copy-done
  14.9 3.3 %collective-permute-start = (bf16[256,512]{1,0:T(8,128)(2,1)S(1)}, bf16[256,512]{1,0:T(8,128)(2,1)S(1)}, u32[]{:S(2)}, u32[]{:S(2)}) collective-permute-start(bf16[256,512]{1,0:T(8,128)(2,1)S(1)} %copy-done), channel_id=1, source_target_pairs={{0,128},{16,144},{32,160},{48,176},{64,192},{80,208},{96,224},{112... | collective-permute-start | bytes 786440 | tf_op jit(solution)/shard_map/ppermute | solution.py:248
  18.3 3.2 %collective-permute-start.1 = (bf16[256,512]{1,0:T(8,128)(2,1)S(1)}, bf16[256,512]{1,0:T(8,128)(2,1)S(1)}, u32[]{:S(2)}, u32[]{:S(2)}) collective-permute-start(bf16[256,512]{1,0:T(8,128)(2,1)S(1)} %copy-done), channel_id=1, source_target_pairs={{0,384},{16,400},{32,416},{48,432},{64,448},{80,464},{96,480},{112... | collective-permute-start | bytes 786440 | tf_op jit(solution)/shard_map/ppermute | solution.py:248
  21.5 3.1 %all-to-all-done.got_ref = bf16[32,40,128]{2,1,0:T(8,128)(2,1)S(1)} async-done(((bf16[32,40,128]{2,1,0:T(8,128)(2,1)}), bf16[32,40,128]{2,1,0:T(8,128)(2,1)S(1)}, u32[]{:S(2)}, u32[]{:S(2)}) %all-to-all-start) | async-done | bytes 327712 | tf_op jit(solution)/shard_map/all_to_all | solution.py:214
  24.6 0.0 copy-done.1
  24.6 1.1 %shard_map.96 = bf16[16,32,128]{2,1,0:T(8,128)(2,1)} custom-call(bf16[32,40,128]{2,1,0:T(8,128)(2,1)S(1)} %all-to-all-done.got_ref, f32[6,8,128]{2,1,0:T(8,128)S(1)} %copy-done.1), custom_call_target="tpu_custom_call" | custom-call | tf_op jit(solution)/shard_map/pallas_call | solution.py:259
  25.7 13.0 %all-to-all-start.1 = ((bf16[16,32,128]{2,1,0:T(8,128)(2,1)}), bf16[16,32,128]{2,1,0:T(8,128)(2,1)S(1)}, u32[]{:S(2)}, u32[]{:S(2)}) async-start(bf16[16,32,128]{2,1,0:T(8,128)(2,1)} %shard_map.96), calls=%async_computation.1 | async-start | bytes 262144 | tf_op jit(solution)/shard_map/all_to_all | solution.py:214
  38.7 0.0 collective-permute-done.one_ref
  38.7 0.0 collective-permute-done.1.three_ref
  38.7 2.4 %collective-permute-start.2 = (bf16[128,512]{1,0:T(8,128)(2,1)S(1)}, bf16[128,512]{1,0:T(8,128)(2,1)S(1)}, u32[]{:S(2)}, u32[]{:S(2)}) collective-permute-start(bf16[128,512]{1,0:T(8,128)(2,1)S(1)} %get-tuple-element.8), channel_id=1, source_target_pairs={{0,128},{16,144},{32,160},{48,176},{64,192},{80,208},{96,224},{112... | collective-permute-start | bytes 393224 | tf_op jit(solution)/shard_map/ppermute | solution.py:248
  41.1 4.1 %collective-permute-start.3 = (bf16[128,512]{1,0:T(8,128)(2,1)S(1)}, bf16[128,512]{1,0:T(8,128)(2,1)S(1)}, u32[]{:S(2)}, u32[]{:S(2)}) collective-permute-start(bf16[128,512]{1,0:T(8,128)(2,1)S(1)} %get-tuple-element.9), channel_id=1, source_target_pairs={{0,384},{16,400},{32,416},{48,432},{64,448},{80,464},{96,480},{112... | collective-permute-start | bytes 393224 | tf_op jit(solution)/shard_map/ppermute | solution.py:248
  45.2 1.1 %collective-permute-done.2.low_ref = bf16[128,512]{1,0:T(8,128)(2,1)S(1)} collective-permute-done((bf16[128,512]{1,0:T(8,128)(2,1)S(1)}, bf16[128,512]{1,0:T(8,128)(2,1)S(1)}, u32[]{:S(2)}, u32[]{:S(2)}) %collective-permute-start.2) | collective-permute-done | bytes 131104 | tf_op jit(solution)/shard_map/ppermute | solution.py:248
  46.3 1.4 %collective-permute-done.3.high_ref = bf16[128,512]{1,0:T(8,128)(2,1)S(1)} collective-permute-done((bf16[128,512]{1,0:T(8,128)(2,1)S(1)}, bf16[128,512]{1,0:T(8,128)(2,1)S(1)}, u32[]{:S(2)}, u32[]{:S(2)}) %collective-permute-start.3) | collective-permute-done | bytes 131104 | tf_op jit(solution)/shard_map/ppermute | solution.py:248
  47.7 2.3 %all-to-all-done.1.x_ref = bf16[16,32,128]{2,1,0:T(8,128)(2,1)S(1)} async-done(((bf16[16,32,128]{2,1,0:T(8,128)(2,1)}), bf16[16,32,128]{2,1,0:T(8,128)(2,1)S(1)}, u32[]{:S(2)}, u32[]{:S(2)}) %all-to-all-start.1) | async-done | bytes 131104 | tf_op jit(solution)/shard_map/all_to_all | solution.py:214
  50.0 0.3 shard_map.98
  50.4 11.1 %all_to_all.15.got_ref = bf16[8,8,512]{2,1,0:T(8,128)(2,1)S(1)} all-to-all(bf16[8,8,512]{2,1,0:T(8,128)(2,1)S(1)} %shard_map.98), channel_id=1, replica_groups={{0,16,32,48,64,80,96,112},{128,144,160,176,192,208,224,240},{256,272,28..., dimensions={0} | all-to-all | bytes 131072 | tf_op jit(solution)/shard_map/all_to_all | solution.py:214
  61.4 0.6 shard_map.99
  (1 shorter events, 0.0 us)
Async XLA Ops:
  4.3 10.6 %copy-start = (bf16[256,512]{1,0:T(8,128)(2,1)S(1)}, bf16[256,512]{1,0:T(8,128)(2,1)}, u32[]{:S(2)}) copy-start(bf16[256,512]{1,0:T(8,128)(2,1)} %own_ref.1) | copy-start | bytes 786436
  4.4 20.2 %copy-start.1 = (f32[6,8,128]{2,1,0:T(8,128)S(1)}, f32[6,8,128]{2,1,0:T(8,128)}, u32[]{:S(2)}) copy-start(f32[6,8,128]{2,1,0:T(8,128)} %get-tuple-element.7.tree_ref) | copy-start | bytes 73732
  4.4 20.2 %all-to-all-start = ((bf16[32,40,128]{2,1,0:T(8,128)(2,1)}), bf16[32,40,128]{2,1,0:T(8,128)(2,1)S(1)}, u32[]{:S(2)}, u32[]{:S(2)}) async-start(bf16[32,40,128]{2,1,0:T(8,128)(2,1)} %get-tuple-element.6), calls=%async_computation | async-start | bytes 655360 | tf_op jit(solution)/shard_map/all_to_all | solution.py:214
  14.9 23.8 %collective-permute-start = (bf16[256,512]{1,0:T(8,128)(2,1)S(1)}, bf16[256,512]{1,0:T(8,128)(2,1)S(1)}, u32[]{:S(2)}, u32[]{:S(2)}) collective-permute-start(bf16[256,512]{1,0:T(8,128)(2,1)S(1)} %copy-done), channel_id=1, source_target_pairs={{0,128},{16,144},{32,160},{48,176},{64,192},{80,208},{96,224},{112... | collective-permute-start | bytes 786440 | tf_op jit(solution)/shard_map/ppermute | solution.py:248
  18.3 20.4 %collective-permute-start.1 = (bf16[256,512]{1,0:T(8,128)(2,1)S(1)}, bf16[256,512]{1,0:T(8,128)(2,1)S(1)}, u32[]{:S(2)}, u32[]{:S(2)}) collective-permute-start(bf16[256,512]{1,0:T(8,128)(2,1)S(1)} %copy-done), channel_id=1, source_target_pairs={{0,384},{16,400},{32,416},{48,432},{64,448},{80,464},{96,480},{112... | collective-permute-start | bytes 786440 | tf_op jit(solution)/shard_map/ppermute | solution.py:248
  25.7 24.3 %all-to-all-start.1 = ((bf16[16,32,128]{2,1,0:T(8,128)(2,1)}), bf16[16,32,128]{2,1,0:T(8,128)(2,1)S(1)}, u32[]{:S(2)}, u32[]{:S(2)}) async-start(bf16[16,32,128]{2,1,0:T(8,128)(2,1)} %shard_map.96), calls=%async_computation.1 | async-start | bytes 262144 | tf_op jit(solution)/shard_map/all_to_all | solution.py:214
  38.7 7.6 %collective-permute-start.2 = (bf16[128,512]{1,0:T(8,128)(2,1)S(1)}, bf16[128,512]{1,0:T(8,128)(2,1)S(1)}, u32[]{:S(2)}, u32[]{:S(2)}) collective-permute-start(bf16[128,512]{1,0:T(8,128)(2,1)S(1)} %get-tuple-element.8), channel_id=1, source_target_pairs={{0,128},{16,144},{32,160},{48,176},{64,192},{80,208},{96,224},{112... | collective-permute-start | bytes 393224 | tf_op jit(solution)/shard_map/ppermute | solution.py:248
  41.1 6.6 %collective-permute-start.3 = (bf16[128,512]{1,0:T(8,128)(2,1)S(1)}, bf16[128,512]{1,0:T(8,128)(2,1)S(1)}, u32[]{:S(2)}, u32[]{:S(2)}) collective-permute-start(bf16[128,512]{1,0:T(8,128)(2,1)S(1)} %get-tuple-element.9), channel_id=1, source_target_pairs={{0,384},{16,400},{32,416},{48,432},{64,448},{80,464},{96,480},{112... | collective-permute-start | bytes 393224 | tf_op jit(solution)/shard_map/ppermute | solution.py:248

commit v14 on v13

--- a/solution.py
+++ b/solution.py
@@ -49,7 +49,7 @@
     seq = lax.axis_index("seq")
     head = lax.axis_index("head")
     lane = lax.broadcasted_iota(jnp.int32, (8, 128), 1)
-    part = (lane % 32) // 8
+    first_half = (lane % 32) < 16
     leaving = []
 
     def leave(source, target):
@@ -84,7 +84,7 @@
             for k in range(2)
         )
         tree_ref[4] = peak
-        tree_ref[5] = jnp.where(part == 2, total, 0.0)
+        tree_ref[5] = jnp.where(first_half, total, 0.0)
 
 
     def scores(p):
@@ -131,8 +131,8 @@
                 m = four_lanes(lane, [peaks[a][r : r + 8] for a in range(2) for r in rows])
                 tot = four_lanes(lane, [sums[a][r : r + 8, 128:] for a in range(2) for r in rows])
                 high = tot.astype(BF16).astype(F32)
-                stat = jnp.where(part < 2, m, jnp.where(part == 2, high, tot - high))
-                send_ref[dest, 32:40, :] = stat.astype(BF16)
+                tot = jnp.where(first_half, high, tot - high)
+                send_ref[dest, 32:48, :] = jnp.concatenate([m, tot], axis=0).astype(BF16)
             chunk = pl.ds(y * 8 + p * 4, 4)
             leave(send_ref.at[chunk], send_hbm.at[chunk])
     leave(tree_ref, tree_hbm)
@@ -146,21 +146,21 @@
 
     peak = tree_ref[4]
     for s in range(32):
-        peak = jnp.maximum(peak, got_ref[s, 32:40, :].astype(F32))
+        peak = jnp.maximum(peak, got_ref[s, 32:48, :].astype(F32)[:8])
     factor = jnp.exp2(tree_ref[4] - peak)
-    total = pltpu.roll(factor, 16, 1) * tree_ref[5]
+    total = factor * tree_ref[5]
     summed = [spread(factor, k * 32) * tree_ref[k] for k in range(4)]
     for s in range(32):
-        stat = got_ref[s, 32:40, :].astype(F32)
-        factor = jnp.exp2(stat - peak)
-        total = total + pltpu.roll(factor, 16, 1) * stat
+        stat = got_ref[s, 32:48, :].astype(F32)
+        factor = jnp.exp2(stat[:8] - peak)
+        total = total + factor * stat[8:]
         for a in range(2):
             part = got_ref[s, a * 16 : (a + 1) * 16, :].astype(F32)
             for g2 in range(2):
                 k = a * 2 + g2
                 summed[k] = summed[k] + spread(factor, k * 32) * part[g2 * 8 : (g2 + 1) * 8]
     done = [
-        summed[k] / (spread(total, k * 32 + 16) + spread(total, k * 32 + 24)) for k in range(4)
+        summed[k] / (spread(total, k * 32) + spread(total, k * 32 + 16)) for k in range(4)
     ]
     rows = jnp.concatenate([done[0], done[2], done[1], done[3]], axis=0).astype(BF16)
     for h in range(16):
@@ -220,7 +220,7 @@
     return pl.pallas_call(
         attend_kernel,
         out_shape=(
-            jax.ShapeDtypeStruct((32, 40, 128), BF16),
+            jax.ShapeDtypeStruct((32, 48, 128), BF16),
             jax.ShapeDtypeStruct((6, 8, 128), F32),
         ),
         in_specs=[HBM] * 7,
@@ -233,7 +233,7 @@
             pltpu.VMEM((2, 2, 32, 128), BF16),
             pltpu.VMEM((2, 2, 32, 128), BF16),
             pltpu.VMEM((4, 32, 32), jnp.int32),
-            pltpu.VMEM((32, 40, 128), BF16),
+            pltpu.VMEM((32, 48, 128), BF16),
             pltpu.VMEM((6, 8, 128), F32),
             pltpu.VMEM((2, 2, 32, 128), F32),
             pltpu.VMEM((2, 2, 2, 32, 128), F32),

time: 62.5 us -> 63.2 us (1.011)
  waiting for transfers between devices: 7.84 us -> 8.49 us
    all_to_all x2, waiting for transfers between devices: 5.35 us -> 6.13 us  [swap(): lax.all_to_all(array, axis, 0, 0, tiled=True, axis_index_groups=groups)]
where the time goes in v14:
time: 63.2 us; the launch traced here: 62.7 us
  starting transfers between devices  36.6 us (58%)
  blocking collectives  11.2 us (18%)
  waiting for transfers between devices  8.49 us (13%)
  Pallas kernels  5.68 us (9%)
  between operations  0.74 us (1%)
    all_to_all x2, starting transfers between devices, swap(): lax.all_to_all(array, axis, 0, 0, tiled=True, axis_index_groups=groups)  23.5 us
    ppermute x4, starting transfers between devices, shift(): lax.ppermute(array, 'seq', [(s, (s + 8 * k) % 32) for s in range(32)])  13.1 us
    all_to_all x1, blocking collectives, swap(): lax.all_to_all(array, axis, 0, 0, tiled=True, axis_index_groups=groups)  11.2 us
    all_to_all x2, waiting for transfers between devices, swap(): lax.all_to_all(array, axis, 0, 0, tiled=True, axis_index_groups=groups)  6.13 us
    pallas_call x1, Pallas kernels, attend(): pl.pallas_call(attend_kernel, out_shape=(jax.ShapeDtypeStruct((32, 48, 12...  3.74 us
    ppermute x4, waiting for transfers between devices, shift(): lax.ppermute(array, 'seq', [(s, (s + 8 * k) % 32) for s in range(32)])  2.36 us
  transfers between devices with their start and end apart: 6, of which 4 were waited for; matrix products, arithmetic and copies ran while one was open for 0% of the time, Pallas kernels for 2%

profile of v14, /device:TPU:1, one launch (start us, length us, event | category | flops | bytes accessed | tf_op | source)
XLA Modules:
  0.0 62.7 jit_solution(3278662859074319351)
XLA Ops:
  0.6 3.7 %shard_map.95 = (bf16[32,48,128]{2,1,0:T(8,128)(2,1)}, f32[6,8,128]{2,1,0:T(8,128)}) custom-call(bf16[2,2,8,32,128]{4,3,2,1,0:T(8,128)(2,1)} %q_hbm.1, bf16[2,1024,128]{2,1,0:T(8,128)(2,1)} %k_hbm.1, bf16[2,1024,128]{2,1,0:T(8,128)(2,1)} %v_hbm.1, s32[2,32]{1,0:T(2,128)} %ids_hbm.1, bf16[2,2,32,128]{3,2,1,0:T(8,128)(2,1)} %tk_hbm.1, ...), custom_call_target="tpu_custom_call" | custom-call | tf_op jit(solution)/shard_map/pallas_call | solution.py:220
  4.4 0.0 copy-start
  4.4 0.0 copy-start.1
  4.4 10.6 %all-to-all-start = ((bf16[32,48,128]{2,1,0:T(8,128)(2,1)}), bf16[32,48,128]{2,1,0:T(8,128)(2,1)S(1)}, u32[]{:S(2)}, u32[]{:S(2)}) async-start(bf16[32,48,128]{2,1,0:T(8,128)(2,1)} %get-tuple-element.6), calls=%async_computation | async-start | bytes 786432 | tf_op jit(solution)/shard_map/all_to_all | solution.py:214
  15.0 0.0 copy-done
  15.0 3.3 %collective-permute-start = (bf16[256,512]{1,0:T(8,128)(2,1)S(1)}, bf16[256,512]{1,0:T(8,128)(2,1)S(1)}, u32[]{:S(2)}, u32[]{:S(2)}) collective-permute-start(bf16[256,512]{1,0:T(8,128)(2,1)S(1)} %copy-done), channel_id=1, source_target_pairs={{0,128},{16,144},{32,160},{48,176},{64,192},{80,208},{96,224},{112... | collective-permute-start | bytes 786440 | tf_op jit(solution)/shard_map/ppermute | solution.py:248
  18.3 3.2 %collective-permute-start.1 = (bf16[256,512]{1,0:T(8,128)(2,1)S(1)}, bf16[256,512]{1,0:T(8,128)(2,1)S(1)}, u32[]{:S(2)}, u32[]{:S(2)}) collective-permute-start(bf16[256,512]{1,0:T(8,128)(2,1)S(1)} %copy-done), channel_id=1, source_target_pairs={{0,384},{16,400},{32,416},{48,432},{64,448},{80,464},{96,480},{112... | collective-permute-start | bytes 786440 | tf_op jit(solution)/shard_map/ppermute | solution.py:248
  21.6 3.7 %all-to-all-done.got_ref = bf16[32,48,128]{2,1,0:T(8,128)(2,1)S(1)} async-done(((bf16[32,48,128]{2,1,0:T(8,128)(2,1)}), bf16[32,48,128]{2,1,0:T(8,128)(2,1)S(1)}, u32[]{:S(2)}, u32[]{:S(2)}) %all-to-all-start) | async-done | bytes 393248 | tf_op jit(solution)/shard_map/all_to_all | solution.py:214
  25.3 0.0 copy-done.1
  25.3 1.0 %shard_map.96 = bf16[16,32,128]{2,1,0:T(8,128)(2,1)} custom-call(bf16[32,48,128]{2,1,0:T(8,128)(2,1)S(1)} %all-to-all-done.got_ref, f32[6,8,128]{2,1,0:T(8,128)S(1)} %copy-done.1), custom_call_target="tpu_custom_call" | custom-call | tf_op jit(solution)/shard_map/pallas_call | solution.py:259
  26.3 13.0 %all-to-all-start.1 = ((bf16[16,32,128]{2,1,0:T(8,128)(2,1)}), bf16[16,32,128]{2,1,0:T(8,128)(2,1)S(1)}, u32[]{:S(2)}, u32[]{:S(2)}) async-start(bf16[16,32,128]{2,1,0:T(8,128)(2,1)} %shard_map.96), calls=%async_computation.1 | async-start | bytes 262144 | tf_op jit(solution)/shard_map/all_to_all | solution.py:214
  39.3 0.0 collective-permute-done.one_ref
  39.3 0.0 collective-permute-done.1.three_ref
  39.3 2.2 %collective-permute-start.2 = (bf16[128,512]{1,0:T(8,128)(2,1)S(1)}, bf16[128,512]{1,0:T(8,128)(2,1)S(1)}, u32[]{:S(2)}, u32[]{:S(2)}) collective-permute-start(bf16[128,512]{1,0:T(8,128)(2,1)S(1)} %get-tuple-element.8), channel_id=1, source_target_pairs={{0,128},{16,144},{32,160},{48,176},{64,192},{80,208},{96,224},{112... | collective-permute-start | bytes 393224 | tf_op jit(solution)/shard_map/ppermute | solution.py:248
  41.6 4.3 %collective-permute-start.3 = (bf16[128,512]{1,0:T(8,128)(2,1)S(1)}, bf16[128,512]{1,0:T(8,128)(2,1)S(1)}, u32[]{:S(2)}, u32[]{:S(2)}) collective-permute-start(bf16[128,512]{1,0:T(8,128)(2,1)S(1)} %get-tuple-element.9), channel_id=1, source_target_pairs={{0,384},{16,400},{32,416},{48,432},{64,448},{80,464},{96,480},{112... | collective-permute-start | bytes 393224 | tf_op jit(solution)/shard_map/ppermute | solution.py:248
  45.8 1.0 %collective-permute-done.2.low_ref = bf16[128,512]{1,0:T(8,128)(2,1)S(1)} collective-permute-done((bf16[128,512]{1,0:T(8,128)(2,1)S(1)}, bf16[128,512]{1,0:T(8,128)(2,1)S(1)}, u32[]{:S(2)}, u32[]{:S(2)}) %collective-permute-start.2) | collective-permute-done | bytes 131104 | tf_op jit(solution)/shard_map/ppermute | solution.py:248
  46.8 1.3 %collective-permute-done.3.high_ref = bf16[128,512]{1,0:T(8,128)(2,1)S(1)} collective-permute-done((bf16[128,512]{1,0:T(8,128)(2,1)S(1)}, bf16[128,512]{1,0:T(8,128)(2,1)S(1)}, u32[]{:S(2)}, u32[]{:S(2)}) %collective-permute-start.3) | collective-permute-done | bytes 131104 | tf_op jit(solution)/shard_map/ppermute | solution.py:248
  48.2 2.4 %all-to-all-done.1.x_ref = bf16[16,32,128]{2,1,0:T(8,128)(2,1)S(1)} async-done(((bf16[16,32,128]{2,1,0:T(8,128)(2,1)}), bf16[16,32,128]{2,1,0:T(8,128)(2,1)S(1)}, u32[]{:S(2)}, u32[]{:S(2)}) %all-to-all-start.1) | async-done | bytes 131104 | tf_op jit(solution)/shard_map/all_to_all | solution.py:214
  50.6 0.3 shard_map.98
  50.9 11.2 %all_to_all.15.got_ref = bf16[8,8,512]{2,1,0:T(8,128)(2,1)S(1)} all-to-all(bf16[8,8,512]{2,1,0:T(8,128)(2,1)S(1)} %shard_map.98), channel_id=1, replica_groups={{0,16,32,48,64,80,96,112},{128,144,160,176,192,208,224,240},{256,272,28..., dimensions={0} | all-to-all | bytes 131072 | tf_op jit(solution)/shard_map/all_to_all | solution.py:214
  62.1 0.6 shard_map.99
  (1 shorter events, 0.0 us)
Async XLA Ops:
  4.4 10.6 %copy-start = (bf16[256,512]{1,0:T(8,128)(2,1)S(1)}, bf16[256,512]{1,0:T(8,128)(2,1)}, u32[]{:S(2)}) copy-start(bf16[256,512]{1,0:T(8,128)(2,1)} %own_ref.1) | copy-start | bytes 786436
  4.4 20.9 %copy-start.1 = (f32[6,8,128]{2,1,0:T(8,128)S(1)}, f32[6,8,128]{2,1,0:T(8,128)}, u32[]{:S(2)}) copy-start(f32[6,8,128]{2,1,0:T(8,128)} %get-tuple-element.7.tree_ref) | copy-start | bytes 73732
  4.4 20.9 %all-to-all-start = ((bf16[32,48,128]{2,1,0:T(8,128)(2,1)}), bf16[32,48,128]{2,1,0:T(8,128)(2,1)S(1)}, u32[]{:S(2)}, u32[]{:S(2)}) async-start(bf16[32,48,128]{2,1,0:T(8,128)(2,1)} %get-tuple-element.6), calls=%async_computation | async-start | bytes 786432 | tf_op jit(solution)/shard_map/all_to_all | solution.py:214
  15.0 24.3 %collective-permute-start = (bf16[256,512]{1,0:T(8,128)(2,1)S(1)}, bf16[256,512]{1,0:T(8,128)(2,1)S(1)}, u32[]{:S(2)}, u32[]{:S(2)}) collective-permute-start(bf16[256,512]{1,0:T(8,128)(2,1)S(1)} %copy-done), channel_id=1, source_target_pairs={{0,128},{16,144},{32,160},{48,176},{64,192},{80,208},{96,224},{112... | collective-permute-start | bytes 786440 | tf_op jit(solution)/shard_map/ppermute | solution.py:248
  18.3 21.0 %collective-permute-start.1 = (bf16[256,512]{1,0:T(8,128)(2,1)S(1)}, bf16[256,512]{1,0:T(8,128)(2,1)S(1)}, u32[]{:S(2)}, u32[]{:S(2)}) collective-permute-start(bf16[256,512]{1,0:T(8,128)(2,1)S(1)} %copy-done), channel_id=1, source_target_pairs={{0,384},{16,400},{32,416},{48,432},{64,448},{80,464},{96,480},{112... | collective-permute-start | bytes 786440 | tf_op jit(solution)/shard_map/ppermute | solution.py:248
  26.3 24.3 %all-to-all-start.1 = ((bf16[16,32,128]{2,1,0:T(8,128)(2,1)}), bf16[16,32,128]{2,1,0:T(8,128)(2,1)S(1)}, u32[]{:S(2)}, u32[]{:S(2)}) async-start(bf16[16,32,128]{2,1,0:T(8,128)(2,1)} %shard_map.96), calls=%async_computation.1 | async-start | bytes 262144 | tf_op jit(solution)/shard_map/all_to_all | solution.py:214
  39.3 7.5 %collective-permute-start.2 = (bf16[128,512]{1,0:T(8,128)(2,1)S(1)}, bf16[128,512]{1,0:T(8,128)(2,1)S(1)}, u32[]{:S(2)}, u32[]{:S(2)}) collective-permute-start(bf16[128,512]{1,0:T(8,128)(2,1)S(1)} %get-tuple-element.8), channel_id=1, source_target_pairs={{0,128},{16,144},{32,160},{48,176},{64,192},{80,208},{96,224},{112... | collective-permute-start | bytes 393224 | tf_op jit(solution)/shard_map/ppermute | solution.py:248
  41.6 6.6 %collective-permute-start.3 = (bf16[128,512]{1,0:T(8,128)(2,1)S(1)}, bf16[128,512]{1,0:T(8,128)(2,1)S(1)}, u32[]{:S(2)}, u32[]{:S(2)}) collective-permute-start(bf16[128,512]{1,0:T(8,128)(2,1)S(1)} %get-tuple-element.9), channel_id=1, source_target_pairs={{0,384},{16,400},{32,416},{48,432},{64,448},{80,464},{96,480},{112... | collective-permute-start | bytes 393224 | tf_op jit(solution)/shard_map/ppermute | solution.py:248

commit v15 on v14

--- a/solution.py
+++ b/solution.py
@@ -140,7 +140,7 @@
         copy.wait()
 
 
-def combine_kernel(got_ref, tree_ref, out_ref):
+def combine_kernel(got_ref, tree_ref, out_hbm, rows_ref, sems):
     def spread(tile, at):
         return jnp.broadcast_to(tile[:, at : at + 1], (8, 128))
 
@@ -162,9 +162,12 @@
     done = [
         summed[k] / (spread(total, k * 32) + spread(total, k * 32 + 16)) for k in range(4)
     ]
-    rows = jnp.concatenate([done[0], done[2], done[1], done[3]], axis=0).astype(BF16)
-    for h in range(16):
-        out_ref[h] = rows
+    rows_ref[...] = jnp.concatenate([done[0], done[2], done[1], done[3]], axis=0).astype(BF16)
+    copies = [pltpu.make_async_copy(rows_ref, out_hbm.at[h], sems.at[h]) for h in range(16)]
+    for copy in copies:
+        copy.start()
+    for copy in copies:
+        copy.wait()
 
 
 def onward_kernel(one_ref, three_ref, low_ref, high_ref):
@@ -260,7 +263,8 @@
         combine_kernel,
         out_shape=jax.ShapeDtypeStruct((16, 32, 128), BF16),
         in_specs=[VMEM, VMEM],
-        out_specs=VMEM,
+        out_specs=HBM,
+        scratch_shapes=[pltpu.VMEM((32, 128), BF16), pltpu.SemaphoreType.DMA((16,))],
         compiler_params=PARAMS,
     )(got, tree)
     gathered = swap(rows, ("seq", "head"), Z_GROUPS)

time: 63.2 us -> 63.3 us (level)
  no operation moved by 1% of the time
where the time goes in v15:
time: 63.3 us; the launch traced here: 62.9 us
  starting transfers between devices  36.6 us (58%)
  blocking collectives  11.2 us (18%)
  waiting for transfers between devices  8.49 us (13%)
  Pallas kernels  5.84 us (9%)
  between operations  0.75 us (1%)
    all_to_all x2, starting transfers between devices, swap(): lax.all_to_all(array, axis, 0, 0, tiled=True, axis_index_groups=groups)  23.6 us
    ppermute x4, starting transfers between devices, shift(): lax.ppermute(array, 'seq', [(s, (s + 8 * k) % 32) for s in range(32)])  13.1 us
    all_to_all x1, blocking collectives, swap(): lax.all_to_all(array, axis, 0, 0, tiled=True, axis_index_groups=groups)  11.2 us
    all_to_all x2, waiting for transfers between devices, swap(): lax.all_to_all(array, axis, 0, 0, tiled=True, axis_index_groups=groups)  6.13 us
    pallas_call x1, Pallas kernels, attend(): pl.pallas_call(attend_kernel, out_shape=(jax.ShapeDtypeStruct((32, 48, 12...  3.74 us
    ppermute x4, waiting for transfers between devices, shift(): lax.ppermute(array, 'seq', [(s, (s + 8 * k) % 32) for s in range(32)])  2.36 us
  transfers between devices with their start and end apart: 6, of which 4 were waited for; matrix products, arithmetic and copies ran while one was open for 0% of the time, Pallas kernels for 2%

profile of v15, /device:TPU:1, one launch (start us, length us, event | category | flops | bytes accessed | tf_op | source)
XLA Modules:
  0.0 62.9 jit_solution(17619936916535988469)
XLA Ops:
  0.6 3.7 %shard_map.95 = (bf16[32,48,128]{2,1,0:T(8,128)(2,1)}, f32[6,8,128]{2,1,0:T(8,128)}) custom-call(bf16[2,2,8,32,128]{4,3,2,1,0:T(8,128)(2,1)} %q_hbm.1, bf16[2,1024,128]{2,1,0:T(8,128)(2,1)} %k_hbm.1, bf16[2,1024,128]{2,1,0:T(8,128)(2,1)} %v_hbm.1, s32[2,32]{1,0:T(2,128)} %ids_hbm.1, bf16[2,2,32,128]{3,2,1,0:T(8,128)(2,1)} %tk_hbm.1, ...), custom_call_target="tpu_custom_call" | custom-call | tf_op jit(solution)/shard_map/pallas_call | solution.py:223
  4.4 0.0 copy-start
  4.4 0.0 copy-start.1
  4.4 10.6 %all-to-all-start = ((bf16[32,48,128]{2,1,0:T(8,128)(2,1)}), bf16[32,48,128]{2,1,0:T(8,128)(2,1)S(1)}, u32[]{:S(2)}, u32[]{:S(2)}) async-start(bf16[32,48,128]{2,1,0:T(8,128)(2,1)} %get-tuple-element.6), calls=%async_computation | async-start | bytes 786432 | tf_op jit(solution)/shard_map/all_to_all | solution.py:217
  15.0 0.0 copy-done
  15.0 3.3 %collective-permute-start = (bf16[256,512]{1,0:T(8,128)(2,1)S(1)}, bf16[256,512]{1,0:T(8,128)(2,1)S(1)}, u32[]{:S(2)}, u32[]{:S(2)}) collective-permute-start(bf16[256,512]{1,0:T(8,128)(2,1)S(1)} %copy-done), channel_id=1, source_target_pairs={{0,128},{16,144},{32,160},{48,176},{64,192},{80,208},{96,224},{112... | collective-permute-start | bytes 786440 | tf_op jit(solution)/shard_map/ppermute | solution.py:251
  18.3 3.2 %collective-permute-start.1 = (bf16[256,512]{1,0:T(8,128)(2,1)S(1)}, bf16[256,512]{1,0:T(8,128)(2,1)S(1)}, u32[]{:S(2)}, u32[]{:S(2)}) collective-permute-start(bf16[256,512]{1,0:T(8,128)(2,1)S(1)} %copy-done), channel_id=1, source_target_pairs={{0,384},{16,400},{32,416},{48,432},{64,448},{80,464},{96,480},{112... | collective-permute-start | bytes 786440 | tf_op jit(solution)/shard_map/ppermute | solution.py:251
  21.6 3.7 %all-to-all-done.got_ref = bf16[32,48,128]{2,1,0:T(8,128)(2,1)S(1)} async-done(((bf16[32,48,128]{2,1,0:T(8,128)(2,1)}), bf16[32,48,128]{2,1,0:T(8,128)(2,1)S(1)}, u32[]{:S(2)}, u32[]{:S(2)}) %all-to-all-start) | async-done | bytes 393248 | tf_op jit(solution)/shard_map/all_to_all | solution.py:217
  25.3 0.0 copy-done.1
  25.3 1.2 %shard_map.96 = bf16[16,32,128]{2,1,0:T(8,128)(2,1)} custom-call(bf16[32,48,128]{2,1,0:T(8,128)(2,1)S(1)} %all-to-all-done.got_ref, f32[6,8,128]{2,1,0:T(8,128)S(1)} %copy-done.1), custom_call_target="tpu_custom_call" | custom-call | tf_op jit(solution)/shard_map/pallas_call | solution.py:262
  26.4 13.0 %all-to-all-start.1 = ((bf16[16,32,128]{2,1,0:T(8,128)(2,1)}), bf16[16,32,128]{2,1,0:T(8,128)(2,1)S(1)}, u32[]{:S(2)}, u32[]{:S(2)}) async-start(bf16[16,32,128]{2,1,0:T(8,128)(2,1)} %shard_map.96), calls=%async_computation.1 | async-start | bytes 262144 | tf_op jit(solution)/shard_map/all_to_all | solution.py:217
  39.4 0.0 collective-permute-done.one_ref
  39.5 0.0 collective-permute-done.1.three_ref
  39.5 2.2 %collective-permute-start.2 = (bf16[128,512]{1,0:T(8,128)(2,1)S(1)}, bf16[128,512]{1,0:T(8,128)(2,1)S(1)}, u32[]{:S(2)}, u32[]{:S(2)}) collective-permute-start(bf16[128,512]{1,0:T(8,128)(2,1)S(1)} %get-tuple-element.8), channel_id=1, source_target_pairs={{0,128},{16,144},{32,160},{48,176},{64,192},{80,208},{96,224},{112... | collective-permute-start | bytes 393224 | tf_op jit(solution)/shard_map/ppermute | solution.py:251
  41.7 4.3 %collective-permute-start.3 = (bf16[128,512]{1,0:T(8,128)(2,1)S(1)}, bf16[128,512]{1,0:T(8,128)(2,1)S(1)}, u32[]{:S(2)}, u32[]{:S(2)}) collective-permute-start(bf16[128,512]{1,0:T(8,128)(2,1)S(1)} %get-tuple-element.9), channel_id=1, source_target_pairs={{0,384},{16,400},{32,416},{48,432},{64,448},{80,464},{96,480},{112... | collective-permute-start | bytes 393224 | tf_op jit(solution)/shard_map/ppermute | solution.py:251
  46.0 1.0 %collective-permute-done.2.low_ref = bf16[128,512]{1,0:T(8,128)(2,1)S(1)} collective-permute-done((bf16[128,512]{1,0:T(8,128)(2,1)S(1)}, bf16[128,512]{1,0:T(8,128)(2,1)S(1)}, u32[]{:S(2)}, u32[]{:S(2)}) %collective-permute-start.2) | collective-permute-done | bytes 131104 | tf_op jit(solution)/shard_map/ppermute | solution.py:251
  47.0 1.3 %collective-permute-done.3.high_ref = bf16[128,512]{1,0:T(8,128)(2,1)S(1)} collective-permute-done((bf16[128,512]{1,0:T(8,128)(2,1)S(1)}, bf16[128,512]{1,0:T(8,128)(2,1)S(1)}, u32[]{:S(2)}, u32[]{:S(2)}) %collective-permute-start.3) | collective-permute-done | bytes 131104 | tf_op jit(solution)/shard_map/ppermute | solution.py:251
  48.4 2.4 %all-to-all-done.1.x_ref = bf16[16,32,128]{2,1,0:T(8,128)(2,1)S(1)} async-done(((bf16[16,32,128]{2,1,0:T(8,128)(2,1)}), bf16[16,32,128]{2,1,0:T(8,128)(2,1)S(1)}, u32[]{:S(2)}, u32[]{:S(2)}) %all-to-all-start.1) | async-done | bytes 131104 | tf_op jit(solution)/shard_map/all_to_all | solution.py:217
  50.8 0.3 shard_map.98
  51.1 11.2 %all_to_all.15.got_ref = bf16[8,8,512]{2,1,0:T(8,128)(2,1)S(1)} all-to-all(bf16[8,8,512]{2,1,0:T(8,128)(2,1)S(1)} %shard_map.98), channel_id=1, replica_groups={{0,16,32,48,64,80,96,112},{128,144,160,176,192,208,224,240},{256,272,28..., dimensions={0} | all-to-all | bytes 131072 | tf_op jit(solution)/shard_map/all_to_all | solution.py:217
  62.3 0.6 shard_map.99
  (1 shorter events, 0.0 us)
Async XLA Ops:
  4.4 10.6 %copy-start = (bf16[256,512]{1,0:T(8,128)(2,1)S(1)}, bf16[256,512]{1,0:T(8,128)(2,1)}, u32[]{:S(2)}) copy-start(bf16[256,512]{1,0:T(8,128)(2,1)} %own_ref.1) | copy-start | bytes 786436
  4.4 20.9 %copy-start.1 = (f32[6,8,128]{2,1,0:T(8,128)S(1)}, f32[6,8,128]{2,1,0:T(8,128)}, u32[]{:S(2)}) copy-start(f32[6,8,128]{2,1,0:T(8,128)} %get-tuple-element.7.tree_ref) | copy-start | bytes 73732
  4.4 20.9 %all-to-all-start = ((bf16[32,48,128]{2,1,0:T(8,128)(2,1)}), bf16[32,48,128]{2,1,0:T(8,128)(2,1)S(1)}, u32[]{:S(2)}, u32[]{:S(2)}) async-start(bf16[32,48,128]{2,1,0:T(8,128)(2,1)} %get-tuple-element.6), calls=%async_computation | async-start | bytes 786432 | tf_op jit(solution)/shard_map/all_to_all | solution.py:217
  15.0 24.5 %collective-permute-start = (bf16[256,512]{1,0:T(8,128)(2,1)S(1)}, bf16[256,512]{1,0:T(8,128)(2,1)S(1)}, u32[]{:S(2)}, u32[]{:S(2)}) collective-permute-start(bf16[256,512]{1,0:T(8,128)(2,1)S(1)} %copy-done), channel_id=1, source_target_pairs={{0,128},{16,144},{32,160},{48,176},{64,192},{80,208},{96,224},{112... | collective-permute-start | bytes 786440 | tf_op jit(solution)/shard_map/ppermute | solution.py:251
  18.3 21.1 %collective-permute-start.1 = (bf16[256,512]{1,0:T(8,128)(2,1)S(1)}, bf16[256,512]{1,0:T(8,128)(2,1)S(1)}, u32[]{:S(2)}, u32[]{:S(2)}) collective-permute-start(bf16[256,512]{1,0:T(8,128)(2,1)S(1)} %copy-done), channel_id=1, source_target_pairs={{0,384},{16,400},{32,416},{48,432},{64,448},{80,464},{96,480},{112... | collective-permute-start | bytes 786440 | tf_op jit(solution)/shard_map/ppermute | solution.py:251
  26.4 24.3 %all-to-all-start.1 = ((bf16[16,32,128]{2,1,0:T(8,128)(2,1)}), bf16[16,32,128]{2,1,0:T(8,128)(2,1)S(1)}, u32[]{:S(2)}, u32[]{:S(2)}) async-start(bf16[16,32,128]{2,1,0:T(8,128)(2,1)} %shard_map.96), calls=%async_computation.1 | async-start | bytes 262144 | tf_op jit(solution)/shard_map/all_to_all | solution.py:217
  39.5 7.5 %collective-permute-start.2 = (bf16[128,512]{1,0:T(8,128)(2,1)S(1)}, bf16[128,512]{1,0:T(8,128)(2,1)S(1)}, u32[]{:S(2)}, u32[]{:S(2)}) collective-permute-start(bf16[128,512]{1,0:T(8,128)(2,1)S(1)} %get-tuple-element.8), channel_id=1, source_target_pairs={{0,128},{16,144},{32,160},{48,176},{64,192},{80,208},{96,224},{112... | collective-permute-start | bytes 393224 | tf_op jit(solution)/shard_map/ppermute | solution.py:251
  41.7 6.6 %collective-permute-start.3 = (bf16[128,512]{1,0:T(8,128)(2,1)S(1)}, bf16[128,512]{1,0:T(8,128)(2,1)S(1)}, u32[]{:S(2)}, u32[]{:S(2)}) collective-permute-start(bf16[128,512]{1,0:T(8,128)(2,1)S(1)} %get-tuple-element.9), channel_id=1, source_target_pairs={{0,384},{16,400},{32,416},{48,432},{64,448},{80,464},{96,480},{112... | collective-permute-start | bytes 393224 | tf_op jit(solution)/shard_map/ppermute | solution.py:251

commit v16 on v14

--- a/solution.py
+++ b/solution.py
@@ -11,7 +11,7 @@
 NEG = -(2.0**100)
 F32 = jnp.float32
 BF16 = jnp.bfloat16
-Z_GROUPS = [[s * 16 + (1 + s % 2 * 14) * k % 16 for k in range(16)] for s in range(32)]
+Z_GROUPS = [[s * 16 + (7 + s % 2 * 2) * k % 16 for k in range(16)] for s in range(32)]
 XC_GROUPS = [[y * 8 + k for k in range(8)] for y in range(4)]
 NT = (((1,), (1,)), ((), ()))
 VMEM = pl.BlockSpec(memory_space=pltpu.VMEM)
@@ -178,7 +178,7 @@
     total = jnp.zeros((64, 512), F32)
 
     def place(r, j):
-        return (1 + seq % 2 * 14) * (r * 4 + j) % 16
+        return (7 + seq % 2 * 2) * (r * 4 + j) % 16
 
     for k in range(4):
         j = (y + 4 - k) % 4

time: 63.2 us -> 63 us (level)
  blocking collectives: 11.2 us -> 9.63 us
  waiting for transfers between devices: 8.49 us -> 9.24 us
    all_to_all x1, blocking collectives: 11.2 us -> 9.63 us  [swap(): lax.all_to_all(array, axis, 0, 0, tiled=True, axis_index_groups=groups)]
    all_to_all x2, waiting for transfers between devices: 6.13 us -> 6.88 us  [swap(): lax.all_to_all(array, axis, 0, 0, tiled=True, axis_index_groups=groups)]
where the time goes in v16:
time: 63 us; the launch traced here: 61.9 us
  starting transfers between devices  36.6 us (58%)
  blocking collectives  9.63 us (15%)
  waiting for transfers between devices  9.24 us (15%)
  Pallas kernels  5.68 us (9%)
  between operations  0.74 us (1%)
    all_to_all x2, starting transfers between devices, swap(): lax.all_to_all(array, axis, 0, 0, tiled=True, axis_index_groups=groups)  23.5 us
    ppermute x4, starting transfers between devices, shift(): lax.ppermute(array, 'seq', [(s, (s + 8 * k) % 32) for s in range(32)])  13.1 us
    all_to_all x1, blocking collectives, swap(): lax.all_to_all(array, axis, 0, 0, tiled=True, axis_index_groups=groups)  9.63 us
    all_to_all x2, waiting for transfers between devices, swap(): lax.all_to_all(array, axis, 0, 0, tiled=True, axis_index_groups=groups)  6.88 us
    pallas_call x1, Pallas kernels, attend(): pl.pallas_call(attend_kernel, out_shape=(jax.ShapeDtypeStruct((32, 48, 12...  3.74 us
    ppermute x4, waiting for transfers between devices, shift(): lax.ppermute(array, 'seq', [(s, (s + 8 * k) % 32) for s in range(32)])  2.36 us
  transfers between devices with their start and end apart: 6, of which 4 were waited for; matrix products, arithmetic and copies ran while one was open for 0% of the time, Pallas kernels for 2%

profile of v16, /device:TPU:1, one launch (start us, length us, event | category | flops | bytes accessed | tf_op | source)
XLA Modules:
  0.0 61.9 jit_solution(5547616410761695899)
XLA Ops:
  0.6 3.7 %shard_map.95 = (bf16[32,48,128]{2,1,0:T(8,128)(2,1)}, f32[6,8,128]{2,1,0:T(8,128)}) custom-call(bf16[2,2,8,32,128]{4,3,2,1,0:T(8,128)(2,1)} %q_hbm.1, bf16[2,1024,128]{2,1,0:T(8,128)(2,1)} %k_hbm.1, bf16[2,1024,128]{2,1,0:T(8,128)(2,1)} %v_hbm.1, s32[2,32]{1,0:T(2,128)} %ids_hbm.1, bf16[2,2,32,128]{3,2,1,0:T(8,128)(2,1)} %tk_hbm.1, ...), custom_call_target="tpu_custom_call" | custom-call | tf_op jit(solution)/shard_map/pallas_call | solution.py:220
  4.4 0.0 copy-start
  4.4 0.0 copy-start.1
  4.4 10.6 %all-to-all-start = ((bf16[32,48,128]{2,1,0:T(8,128)(2,1)}), bf16[32,48,128]{2,1,0:T(8,128)(2,1)S(1)}, u32[]{:S(2)}, u32[]{:S(2)}) async-start(bf16[32,48,128]{2,1,0:T(8,128)(2,1)} %get-tuple-element.6), calls=%async_computation | async-start | bytes 786432 | tf_op jit(solution)/shard_map/all_to_all | solution.py:214
  15.0 0.0 copy-done
  15.0 3.3 %collective-permute-start = (bf16[256,512]{1,0:T(8,128)(2,1)S(1)}, bf16[256,512]{1,0:T(8,128)(2,1)S(1)}, u32[]{:S(2)}, u32[]{:S(2)}) collective-permute-start(bf16[256,512]{1,0:T(8,128)(2,1)S(1)} %copy-done), channel_id=1, source_target_pairs={{0,128},{16,144},{32,160},{48,176},{64,192},{80,208},{96,224},{112... | collective-permute-start | bytes 786440 | tf_op jit(solution)/shard_map/ppermute | solution.py:248
  18.3 3.2 %collective-permute-start.1 = (bf16[256,512]{1,0:T(8,128)(2,1)S(1)}, bf16[256,512]{1,0:T(8,128)(2,1)S(1)}, u32[]{:S(2)}, u32[]{:S(2)}) collective-permute-start(bf16[256,512]{1,0:T(8,128)(2,1)S(1)} %copy-done), channel_id=1, source_target_pairs={{0,384},{16,400},{32,416},{48,432},{64,448},{80,464},{96,480},{112... | collective-permute-start | bytes 786440 | tf_op jit(solution)/shard_map/ppermute | solution.py:248
  21.6 3.7 %all-to-all-done.got_ref = bf16[32,48,128]{2,1,0:T(8,128)(2,1)S(1)} async-done(((bf16[32,48,128]{2,1,0:T(8,128)(2,1)}), bf16[32,48,128]{2,1,0:T(8,128)(2,1)S(1)}, u32[]{:S(2)}, u32[]{:S(2)}) %all-to-all-start) | async-done | bytes 393248 | tf_op jit(solution)/shard_map/all_to_all | solution.py:214
  25.3 0.0 copy-done.1
  25.3 1.0 %shard_map.96 = bf16[16,32,128]{2,1,0:T(8,128)(2,1)} custom-call(bf16[32,48,128]{2,1,0:T(8,128)(2,1)S(1)} %all-to-all-done.got_ref, f32[6,8,128]{2,1,0:T(8,128)S(1)} %copy-done.1), custom_call_target="tpu_custom_call" | custom-call | tf_op jit(solution)/shard_map/pallas_call | solution.py:259
  26.3 13.0 %all-to-all-start.1 = ((bf16[16,32,128]{2,1,0:T(8,128)(2,1)}), bf16[16,32,128]{2,1,0:T(8,128)(2,1)S(1)}, u32[]{:S(2)}, u32[]{:S(2)}) async-start(bf16[16,32,128]{2,1,0:T(8,128)(2,1)} %shard_map.96), calls=%async_computation.1 | async-start | bytes 262144 | tf_op jit(solution)/shard_map/all_to_all | solution.py:214
  39.3 0.0 collective-permute-done.one_ref
  39.3 0.0 collective-permute-done.1.three_ref
  39.3 2.2 %collective-permute-start.2 = (bf16[128,512]{1,0:T(8,128)(2,1)S(1)}, bf16[128,512]{1,0:T(8,128)(2,1)S(1)}, u32[]{:S(2)}, u32[]{:S(2)}) collective-permute-start(bf16[128,512]{1,0:T(8,128)(2,1)S(1)} %get-tuple-element.8), channel_id=1, source_target_pairs={{0,128},{16,144},{32,160},{48,176},{64,192},{80,208},{96,224},{112... | collective-permute-start | bytes 393224 | tf_op jit(solution)/shard_map/ppermute | solution.py:248
  41.6 4.3 %collective-permute-start.3 = (bf16[128,512]{1,0:T(8,128)(2,1)S(1)}, bf16[128,512]{1,0:T(8,128)(2,1)S(1)}, u32[]{:S(2)}, u32[]{:S(2)}) collective-permute-start(bf16[128,512]{1,0:T(8,128)(2,1)S(1)} %get-tuple-element.9), channel_id=1, source_target_pairs={{0,384},{16,400},{32,416},{48,432},{64,448},{80,464},{96,480},{112... | collective-permute-start | bytes 393224 | tf_op jit(solution)/shard_map/ppermute | solution.py:248
  45.8 1.0 %collective-permute-done.2.low_ref = bf16[128,512]{1,0:T(8,128)(2,1)S(1)} collective-permute-done((bf16[128,512]{1,0:T(8,128)(2,1)S(1)}, bf16[128,512]{1,0:T(8,128)(2,1)S(1)}, u32[]{:S(2)}, u32[]{:S(2)}) %collective-permute-start.2) | collective-permute-done | bytes 131104 | tf_op jit(solution)/shard_map/ppermute | solution.py:248
  46.8 1.3 %collective-permute-done.3.high_ref = bf16[128,512]{1,0:T(8,128)(2,1)S(1)} collective-permute-done((bf16[128,512]{1,0:T(8,128)(2,1)S(1)}, bf16[128,512]{1,0:T(8,128)(2,1)S(1)}, u32[]{:S(2)}, u32[]{:S(2)}) %collective-permute-start.3) | collective-permute-done | bytes 131104 | tf_op jit(solution)/shard_map/ppermute | solution.py:248
  48.2 3.2 %all-to-all-done.1.x_ref = bf16[16,32,128]{2,1,0:T(8,128)(2,1)S(1)} async-done(((bf16[16,32,128]{2,1,0:T(8,128)(2,1)}), bf16[16,32,128]{2,1,0:T(8,128)(2,1)S(1)}, u32[]{:S(2)}, u32[]{:S(2)}) %all-to-all-start.1) | async-done | bytes 131104 | tf_op jit(solution)/shard_map/all_to_all | solution.py:214
  51.4 0.3 shard_map.98
  51.7 9.6 %all_to_all.15.got_ref = bf16[8,8,512]{2,1,0:T(8,128)(2,1)S(1)} all-to-all(bf16[8,8,512]{2,1,0:T(8,128)(2,1)S(1)} %shard_map.98), channel_id=1, replica_groups={{0,16,32,48,64,80,96,112},{128,144,160,176,192,208,224,240},{256,272,28..., dimensions={0} | all-to-all | bytes 131072 | tf_op jit(solution)/shard_map/all_to_all | solution.py:214
  61.3 0.6 shard_map.99
  (1 shorter events, 0.0 us)
Async XLA Ops:
  4.4 10.6 %copy-start = (bf16[256,512]{1,0:T(8,128)(2,1)S(1)}, bf16[256,512]{1,0:T(8,128)(2,1)}, u32[]{:S(2)}) copy-start(bf16[256,512]{1,0:T(8,128)(2,1)} %own_ref.1) | copy-start | bytes 786436
  4.4 20.9 %copy-start.1 = (f32[6,8,128]{2,1,0:T(8,128)S(1)}, f32[6,8,128]{2,1,0:T(8,128)}, u32[]{:S(2)}) copy-start(f32[6,8,128]{2,1,0:T(8,128)} %get-tuple-element.7.tree_ref) | copy-start | bytes 73732
  4.4 20.9 %all-to-all-start = ((bf16[32,48,128]{2,1,0:T(8,128)(2,1)}), bf16[32,48,128]{2,1,0:T(8,128)(2,1)S(1)}, u32[]{:S(2)}, u32[]{:S(2)}) async-start(bf16[32,48,128]{2,1,0:T(8,128)(2,1)} %get-tuple-element.6), calls=%async_computation | async-start | bytes 786432 | tf_op jit(solution)/shard_map/all_to_all | solution.py:214
  15.0 24.3 %collective-permute-start = (bf16[256,512]{1,0:T(8,128)(2,1)S(1)}, bf16[256,512]{1,0:T(8,128)(2,1)S(1)}, u32[]{:S(2)}, u32[]{:S(2)}) collective-permute-start(bf16[256,512]{1,0:T(8,128)(2,1)S(1)} %copy-done), channel_id=1, source_target_pairs={{0,128},{16,144},{32,160},{48,176},{64,192},{80,208},{96,224},{112... | collective-permute-start | bytes 786440 | tf_op jit(solution)/shard_map/ppermute | solution.py:248
  18.3 21.0 %collective-permute-start.1 = (bf16[256,512]{1,0:T(8,128)(2,1)S(1)}, bf16[256,512]{1,0:T(8,128)(2,1)S(1)}, u32[]{:S(2)}, u32[]{:S(2)}) collective-permute-start(bf16[256,512]{1,0:T(8,128)(2,1)S(1)} %copy-done), channel_id=1, source_target_pairs={{0,384},{16,400},{32,416},{48,432},{64,448},{80,464},{96,480},{112... | collective-permute-start | bytes 786440 | tf_op jit(solution)/shard_map/ppermute | solution.py:248
  26.3 25.1 %all-to-all-start.1 = ((bf16[16,32,128]{2,1,0:T(8,128)(2,1)}), bf16[16,32,128]{2,1,0:T(8,128)(2,1)S(1)}, u32[]{:S(2)}, u32[]{:S(2)}) async-start(bf16[16,32,128]{2,1,0:T(8,128)(2,1)} %shard_map.96), calls=%async_computation.1 | async-start | bytes 262144 | tf_op jit(solution)/shard_map/all_to_all | solution.py:214
  39.3 7.5 %collective-permute-start.2 = (bf16[128,512]{1,0:T(8,128)(2,1)S(1)}, bf16[128,512]{1,0:T(8,128)(2,1)S(1)}, u32[]{:S(2)}, u32[]{:S(2)}) collective-permute-start(bf16[128,512]{1,0:T(8,128)(2,1)S(1)} %get-tuple-element.8), channel_id=1, source_target_pairs={{0,128},{16,144},{32,160},{48,176},{64,192},{80,208},{96,224},{112... | collective-permute-start | bytes 393224 | tf_op jit(solution)/shard_map/ppermute | solution.py:248
  41.6 6.6 %collective-permute-start.3 = (bf16[128,512]{1,0:T(8,128)(2,1)S(1)}, bf16[128,512]{1,0:T(8,128)(2,1)S(1)}, u32[]{:S(2)}, u32[]{:S(2)}) collective-permute-start(bf16[128,512]{1,0:T(8,128)(2,1)S(1)} %get-tuple-element.9), channel_id=1, source_target_pairs={{0,384},{16,400},{32,416},{48,432},{64,448},{80,464},{96,480},{112... | collective-permute-start | bytes 393224 | tf_op jit(solution)/shard_map/ppermute | solution.py:248
